TPU v7x, 32 devices: a whole 2x2x4 slice. The times are simulated.
32 devices in a mesh: grp: 8 (over z, x), wide: 4 (over y, core).
Axes of the slice: x: 2, y: 2, z: 4, core: 2. Of those that a mesh axis runs over, the one named last changes fastest.
Arguments:
- hidden: bfloat16 [4096, 768], P(('grp', 'wide')), may hold values from -6 to 6
- char_codes: int32 [4096, 20], P(('grp', 'wide')), may hold values from 0 to 999
- word_length: int32 [4096], P(('grp', 'wide')), may hold values from 1 to 20, as said below
- sequence_length: int32 [32], P(('grp', 'wide')), may hold values from 64 to 128, as said below
- cotangent: bfloat16 [4096, 768], P(('grp', 'wide')), may hold values from -6 to 6
- attention_in: bfloat16 [768, 2304], P(None, ('grp', 'wide')), may hold values from -0.21875 to 0.21875
- attention_out: bfloat16 [768, 768], P(None, ('grp', 'wide')), may hold values from -1.5 to 1.5
- feed_in: bfloat16 [768, 3072], P(None, ('grp', 'wide')), may hold values from -0.21875 to 0.21875
- feed_bias: bfloat16 [3072], P(('grp', 'wide')), may hold values from -1 to 1
- feed_out: bfloat16 [3072, 768], P(None, ('grp', 'wide')), may hold values from -0.109375 to 0.109375
- char_table: bfloat16 [1000, 256], P(None, ('grp', 'wide')), may hold values from -6 to 6
- cell_input: bfloat16 [256, 2304], P(None, ('grp', 'wide')), may hold values from -0.375 to 0.375
- cell_recurrent: bfloat16 [384, 2304], P(None, ('grp', 'wide')), may hold values from -0.3125 to 0.3125
- cell_bias: bfloat16 [2, 2304], P(None, ('grp', 'wide')), may hold values from -1 to 1
- stream_weight: bfloat16 [2, 768, 768], P(None, None, ('grp', 'wide')), may hold values from -0.21875 to 0.21875
- merging_kernel: bfloat16 [3, 1536, 768], P(None, None, ('grp', 'wide')), may hold values from -0.09375 to 0.09375
- norm_gains: bfloat16 [3, 768], P(None, ('grp', 'wide')), may hold values from 0.5 to 1.5
- biases: bfloat16 [10, 768], P(None, ('grp', 'wide')), may hold values from -1 to 1
Outputs:
- output: bfloat16 [4096, 768], P(('grp', 'wide'))
- hidden_grad: bfloat16 [4096, 768], P(('grp', 'wide'))
- grad_attention_in: float32 [768, 2304], P(None, 'grp')
- grad_attention_out: float32 [768, 768], P(None, 'grp')
- grad_feed_in: float32 [768, 3072], P(None, 'grp')
- grad_feed_bias: float32 [3072], P('grp')
- grad_feed_out: float32 [3072, 768], P(None, 'grp')
- grad_char_table: float32 [1000, 256], P(None, 'grp')
- grad_cell_input: float32 [256, 2304], P(None, 'grp')
- grad_cell_recurrent: float32 [384, 2304], P(None, 'grp')
- grad_cell_bias: float32 [2, 2304], P(None, 'grp')
- grad_stream_weight: float32 [2, 768, 768], P(None, None, 'grp')
- grad_merging_kernel: float32 [3, 1536, 768], P(None, None, 'grp')
- grad_norm_gains: float32 [3, 768], P(None, 'grp')
- grad_biases: float32 [10, 768], P(None, 'grp')
Inputs may be any that keep to these rules, and one draw needn't show every extreme that they name: `word_length`: every token has at least one character; one token of the draw fills all 20 slots and one has a single character. `sequence_length`: one sequence of the draw is full and one holds 64 valid tokens.
All inputs are finite; a program needn't handle non-finite values.
Results may differ from a plain program's by a relative error of at most 0.02.
Values may be sent and summed in bfloat16 or wider, within the bound.
A program may use at most 320 MiB of HBM per device.

v0:
```python
from functools import partial

import jax
import jax.numpy as jnp
from jax import lax
from jax.sharding import PartitionSpec as P

HEADS = 12


norm_eps = 1e-05
masked_score = -1e30


def dot_plain(left_side, right_side):
    return jnp.dot(left_side, right_side, preferred_element_type=jnp.float32)


def dot_first(left_side, right_side):
    return lax.dot_general(
        left_side, right_side, (((0,), (0,)), ((), ())), preferred_element_type=jnp.float32
    )


def dot_second(left_side, right_side):
    return lax.dot_general(
        left_side, right_side, (((1,), (1,)), ((), ())), preferred_element_type=jnp.float32
    )


def layer_norm(inputs, gain_row, shift_row):
    centred = inputs - jnp.mean(inputs, axis=-1, keepdims=True)
    spread = jnp.mean(centred * centred, axis=-1, keepdims=True)
    return centred * lax.rsqrt(spread + norm_eps) * gain_row + shift_row


def gelu_exact(inputs):
    return jax.nn.gelu(inputs, approximate=False)


def gate_cell(previous, drive_in, recurrent, marker):
    hidden_units = previous.shape[-1]
    reset_gate = jax.nn.sigmoid(drive_in[:, :hidden_units] + recurrent[:, :hidden_units])
    update = jax.nn.sigmoid(
        drive_in[:, hidden_units : 2 * hidden_units] + recurrent[:, hidden_units : 2 * hidden_units]
    )
    candidate = jnp.tanh(
        drive_in[:, 2 * hidden_units :] + reset_gate * recurrent[:, 2 * hidden_units :]
    )
    fresh_state = (1.0 - update) * candidate + update * previous
    return marker * fresh_state + (1.0 - marker) * previous


def forward(gathered, hidden, char_codes, word_length, sequence_length):
    (
        attention_in,
        attention_out,
        feed_in,
        feed_bias,
        feed_out,
        char_table,
        cell_input,
        cell_recurrent,
        cell_bias,
        stream_weight,
        merging_kernel,
        norm_gains,
        biases,
    ) = gathered
    length, model_width = hidden.shape
    head_size = model_width // HEADS
    score_scale = head_size ** (-0.5)
    biases_wide = biases.astype(jnp.float32)
    gains_wide = norm_gains.astype(jnp.float32)
    joint_bias = jnp.concatenate([biases_wide[0], jnp.zeros_like(biases_wide[0]), biases_wide[1]])
    projected = (dot_plain(hidden, attention_in) + joint_bias).astype(jnp.bfloat16)
    projected = projected.reshape(length, 3, HEADS, head_size)
    queries = projected[:, 0]
    key_rows = projected[:, 1]
    value_rows = projected[:, 2]
    key_mask = jnp.where(jnp.arange(length) < sequence_length[0], 0.0, masked_score).astype(
        jnp.float32
    )
    scores = (
        jnp.einsum("qhd,khd->hqk", queries, key_rows, preferred_element_type=jnp.float32)
        * score_scale
        + key_mask
    )
    top_score = jnp.max(scores, axis=-1, keepdims=True)
    exponent = jnp.exp(scores - top_score)
    total_weight = jnp.sum(exponent, axis=-1, keepdims=True)
    log_total = top_score + jnp.log(total_weight)
    soft_low = (exponent / total_weight).astype(jnp.bfloat16)
    context = jnp.einsum("hqk,khd->qhd", soft_low, value_rows, preferred_element_type=jnp.float32)
    context = context.astype(jnp.bfloat16).reshape(length, model_width)
    one_sum = hidden.astype(jnp.float32) + dot_plain(context, attention_out) + biases_wide[2]
    first = layer_norm(one_sum, gains_wide[0], biases_wide[3])
    first_low = first.astype(jnp.bfloat16)
    inner_sum = dot_plain(first_low, feed_in) + feed_bias.astype(jnp.float32)
    activation = gelu_exact(inner_sum).astype(jnp.bfloat16)
    two_sum = first + dot_plain(activation, feed_out) + biases_wide[4]
    second = layer_norm(two_sum, gains_wide[1], biases_wide[5])
    second_low = second.astype(jnp.bfloat16)
    char_count = char_codes.shape[1]
    hidden_units = cell_recurrent.shape[0]
    gate_width = 3 * hidden_units
    cell_wide = cell_bias.astype(jnp.float32)
    char_flat = jnp.transpose(char_codes).reshape(char_count * length)
    embedded = char_table[char_flat]
    drives = (dot_plain(embedded, cell_input) + cell_wide[0]).reshape(
        char_count, length, 2 * gate_width
    )
    char_marks = (jnp.arange(char_count)[:, None] < word_length[None, :]).astype(jnp.float32)[
        :, :, None
    ]
    weight_onward = cell_recurrent[:, :gate_width]
    weight_behind = cell_recurrent[:, gate_width:]

    def advance(carried, position):
        onward, behind, total_onward, total_behind = carried
        mirror = char_count - 1 - position
        drive_onward = lax.dynamic_index_in_dim(drives, position, 0, keepdims=False)[:, :gate_width]
        drive_behind = lax.dynamic_index_in_dim(drives, mirror, 0, keepdims=False)[:, gate_width:]
        mark_onward = lax.dynamic_index_in_dim(char_marks, position, 0, keepdims=False)
        mark_behind = lax.dynamic_index_in_dim(char_marks, mirror, 0, keepdims=False)
        recur_onward = (
            dot_plain(onward.astype(jnp.bfloat16), weight_onward) + cell_wide[1, :gate_width]
        )
        recur_behind = (
            dot_plain(behind.astype(jnp.bfloat16), weight_behind) + cell_wide[1, gate_width:]
        )
        next_onward = gate_cell(onward, drive_onward, recur_onward, mark_onward)
        next_behind = gate_cell(behind, drive_behind, recur_behind, mark_behind)
        carried = (
            next_onward,
            next_behind,
            total_onward + mark_onward * next_onward,
            total_behind + mark_behind * next_behind,
        )
        return (carried, (onward, behind, recur_onward, recur_behind))

    zero_state = jnp.zeros((length, hidden_units), jnp.float32)
    final_carry, history = lax.scan(
        advance, (zero_state, zero_state, zero_state, zero_state), jnp.arange(char_count)
    )
    counts = word_length.astype(jnp.float32)[:, None]
    pooled = jnp.concatenate([final_carry[2], final_carry[3]], axis=-1) / counts
    pooled_low = pooled.astype(jnp.bfloat16)
    token_side = dot_plain(second_low, stream_weight[0]) + biases_wide[6]
    char_side = dot_plain(pooled_low, stream_weight[1]) + biases_wide[7]
    joined = jnp.concatenate([token_side, char_side], axis=-1).astype(jnp.bfloat16)
    padded = jnp.pad(joined, ((1, 1), (0, 0)))
    windows = jnp.concatenate([padded[:-2], padded[1:-1], padded[2:]], axis=-1)
    merged_out = (
        dot_plain(windows, merging_kernel.reshape(6 * model_width, model_width)) + biases_wide[8]
    )
    third_sum = second + merged_out
    output = layer_norm(third_sum, gains_wide[2], biases_wide[9]).astype(jnp.bfloat16)
    saved_values = {
        "hidden": hidden,
        "queries": queries,
        "key_rows": key_rows,
        "value_rows": value_rows,
        "key_mask": key_mask,
        "log_total": log_total,
        "context": context,
        "one_sum": one_sum,
        "first_low": first_low,
        "inner_sum": inner_sum,
        "activation": activation,
        "two_sum": two_sum,
        "second_low": second_low,
        "drives": drives,
        "char_marks": char_marks,
        "history": history,
        "embedded": embedded,
        "char_flat": char_flat,
        "pooled_low": pooled_low,
        "windows": windows,
        "third_sum": third_sum,
        "word_length": word_length,
    }
    return (output, saved_values)


def backward(gathered, saved_values, cotangent):
    (
        attention_in,
        attention_out,
        feed_in,
        feed_bias,
        feed_out,
        char_table,
        cell_input,
        cell_recurrent,
        cell_bias,
        stream_weight,
        merging_kernel,
        norm_gains,
        biases,
    ) = gathered
    gains_wide = norm_gains.astype(jnp.float32)
    biases_wide = biases.astype(jnp.float32)
    hidden = saved_values["hidden"]
    length, model_width = hidden.shape
    head_size = model_width // HEADS
    score_scale = head_size ** (-0.5)
    _, pull_three = jax.vjp(layer_norm, saved_values["third_sum"], gains_wide[2], biases_wide[9])
    merged_grad, gain_three, shift_three = pull_three(cotangent.astype(jnp.float32))
    merged_low = merged_grad.astype(jnp.bfloat16)
    grad_merging = dot_first(saved_values["windows"], merged_low).reshape(merging_kernel.shape)
    window_grad = dot_second(merged_low, merging_kernel.reshape(6 * model_width, model_width))
    window_grad = window_grad.reshape(length, 3, 2 * model_width)
    joined_grad = (
        window_grad[:, 1]
        + jnp.pad(window_grad[1:, 0], ((0, 1), (0, 0)))
        + jnp.pad(window_grad[:-1, 2], ((1, 0), (0, 0)))
    )
    token_grad = joined_grad[:, :model_width]
    char_grad = joined_grad[:, model_width:]
    token_low = token_grad.astype(jnp.bfloat16)
    char_low = char_grad.astype(jnp.bfloat16)
    grad_stream = jnp.stack(
        [
            dot_first(saved_values["second_low"], token_low),
            dot_first(saved_values["pooled_low"], char_low),
        ]
    )
    pooled_grad = dot_second(char_low, stream_weight[1])
    drives = saved_values["drives"]
    char_marks = saved_values["char_marks"]
    states_onward, states_behind, recurs_onward, recurs_behind = saved_values["history"]
    char_count = drives.shape[0]
    hidden_units = cell_recurrent.shape[0]
    gate_width = 3 * hidden_units
    weight_onward = cell_recurrent[:, :gate_width]
    weight_behind = cell_recurrent[:, gate_width:]
    counts = saved_values["word_length"].astype(jnp.float32)[:, None]
    pool_onward = pooled_grad[:, :hidden_units] / counts
    pool_behind = pooled_grad[:, hidden_units:] / counts

    def retreat(carried, position):
        grad_onward, grad_behind, bias_onward, bias_behind = carried
        mirror = char_count - 1 - position
        mark_onward = lax.dynamic_index_in_dim(char_marks, position, 0, keepdims=False)
        mark_behind = lax.dynamic_index_in_dim(char_marks, mirror, 0, keepdims=False)
        drive_onward = lax.dynamic_index_in_dim(drives, position, 0, keepdims=False)[:, :gate_width]
        drive_behind = lax.dynamic_index_in_dim(drives, mirror, 0, keepdims=False)[:, gate_width:]
        prior_onward = lax.dynamic_index_in_dim(states_onward, position, 0, keepdims=False)
        prior_behind = lax.dynamic_index_in_dim(states_behind, position, 0, keepdims=False)
        recur_onward = lax.dynamic_index_in_dim(recurs_onward, position, 0, keepdims=False)
        recur_behind = lax.dynamic_index_in_dim(recurs_behind, position, 0, keepdims=False)
        _, pull_onward = jax.vjp(
            partial(gate_cell, marker=mark_onward), prior_onward, drive_onward, recur_onward
        )
        _, pull_behind = jax.vjp(
            partial(gate_cell, marker=mark_behind), prior_behind, drive_behind, recur_behind
        )
        state_onward, input_onward, recur_grad_onward = pull_onward(
            grad_onward + mark_onward * pool_onward
        )
        state_behind, input_behind, recur_grad_behind = pull_behind(
            grad_behind + mark_behind * pool_behind
        )
        low_onward = recur_grad_onward.astype(jnp.bfloat16)
        low_behind = recur_grad_behind.astype(jnp.bfloat16)
        carried = (
            state_onward + dot_second(low_onward, weight_onward),
            state_behind + dot_second(low_behind, weight_behind),
            bias_onward + jnp.sum(recur_grad_onward, axis=0),
            bias_behind + jnp.sum(recur_grad_behind, axis=0),
        )
        return (carried, (input_onward, input_behind, low_onward, low_behind))

    zero_state = jnp.zeros((length, hidden_units), jnp.float32)
    zero_bias = jnp.zeros((gate_width,), jnp.float32)
    final_back, traced = lax.scan(
        retreat,
        (zero_state, zero_state, zero_bias, zero_bias),
        jnp.arange(char_count),
        reverse=True,
    )
    drive_grad = jnp.concatenate([traced[0], traced[1][::-1]], axis=-1)
    grad_cell_bias = jnp.stack(
        [jnp.sum(drive_grad, axis=(0, 1)), jnp.concatenate([final_back[2], final_back[3]])]
    )
    drive_low = drive_grad.astype(jnp.bfloat16).reshape(char_count * length, 2 * gate_width)
    grad_cell_input = dot_first(saved_values["embedded"], drive_low)
    embed_grad = dot_second(drive_low, cell_input)
    grad_table = (
        jnp.zeros(char_table.shape, jnp.float32).at[saved_values["char_flat"]].add(embed_grad)
    )
    recur_weight_onward = dot_first(
        states_onward.reshape(char_count * length, hidden_units).astype(jnp.bfloat16),
        traced[2].reshape(char_count * length, gate_width),
    )
    recur_weight_behind = dot_first(
        states_behind.reshape(char_count * length, hidden_units).astype(jnp.bfloat16),
        traced[3].reshape(char_count * length, gate_width),
    )
    grad_cell_recurrent = jnp.concatenate([recur_weight_onward, recur_weight_behind], axis=1)
    second_grad = merged_grad + dot_second(token_low, stream_weight[0])
    _, pull_two = jax.vjp(layer_norm, saved_values["two_sum"], gains_wide[1], biases_wide[5])
    two_grad, gain_two, shift_two = pull_two(second_grad)
    two_low = two_grad.astype(jnp.bfloat16)
    grad_feed_out = dot_first(saved_values["activation"], two_low)
    _, pull_gelu = jax.vjp(gelu_exact, saved_values["inner_sum"])
    (inner_grad,) = pull_gelu(dot_second(two_low, feed_out))
    inner_low = inner_grad.astype(jnp.bfloat16)
    grad_feed_in = dot_first(saved_values["first_low"], inner_low)
    first_grad = two_grad + dot_second(inner_low, feed_in)
    _, pull_one = jax.vjp(layer_norm, saved_values["one_sum"], gains_wide[0], biases_wide[3])
    one_grad, gain_one, shift_one = pull_one(first_grad)
    one_low = one_grad.astype(jnp.bfloat16)
    grad_attention_out = dot_first(saved_values["context"], one_low)
    context_grad = (
        dot_second(one_low, attention_out).astype(jnp.bfloat16).reshape(length, HEADS, head_size)
    )
    queries = saved_values["queries"]
    key_rows = saved_values["key_rows"]
    value_rows = saved_values["value_rows"]
    scores = (
        jnp.einsum("qhd,khd->hqk", queries, key_rows, preferred_element_type=jnp.float32)
        * score_scale
        + saved_values["key_mask"]
    )
    soft_weights = jnp.exp(scores - saved_values["log_total"])
    soft_low = soft_weights.astype(jnp.bfloat16)
    soft_grad = jnp.einsum(
        "qhd,khd->hqk", context_grad, value_rows, preferred_element_type=jnp.float32
    )
    value_grad = jnp.einsum(
        "hqk,qhd->khd", soft_low, context_grad, preferred_element_type=jnp.float32
    )
    score_grad = soft_weights * (
        soft_grad - jnp.sum(soft_weights * soft_grad, axis=-1, keepdims=True)
    )
    score_low = score_grad.astype(jnp.bfloat16)
    query_grad = (
        jnp.einsum("hqk,khd->qhd", score_low, key_rows, preferred_element_type=jnp.float32)
        * score_scale
    )
    key_grad = (
        jnp.einsum("hqk,qhd->khd", score_low, queries, preferred_element_type=jnp.float32)
        * score_scale
    )
    projected_grad = jnp.stack([query_grad, key_grad, value_grad], axis=1).reshape(
        length, 3 * model_width
    )
    projected_low = projected_grad.astype(jnp.bfloat16)
    grad_attention_in = dot_first(hidden, projected_low)
    hidden_grad = (one_grad + dot_second(projected_low, attention_in)).astype(jnp.bfloat16)
    grad_gains = jnp.stack([gain_one, gain_two, gain_three])
    grad_biases = jnp.stack(
        [
            jnp.sum(query_grad, axis=0).reshape(model_width),
            jnp.sum(value_grad, axis=0).reshape(model_width),
            jnp.sum(one_grad, axis=0),
            shift_one,
            jnp.sum(two_grad, axis=0),
            shift_two,
            jnp.sum(token_grad, axis=0),
            jnp.sum(char_grad, axis=0),
            jnp.sum(merged_grad, axis=0),
            shift_three,
        ]
    )
    grad_feed_bias = jnp.sum(inner_grad, axis=0)
    param_grads = (
        grad_attention_in,
        grad_attention_out,
        grad_feed_in,
        grad_feed_bias,
        grad_feed_out,
        grad_table,
        grad_cell_input,
        grad_cell_recurrent,
        grad_cell_bias,
        grad_stream,
        grad_merging,
        grad_gains,
        grad_biases,
    )
    return (hidden_grad, param_grads)


def shards(
    hidden,
    char_codes,
    word_length,
    sequence_length,
    cotangent,
    attention_in,
    attention_out,
    feed_in,
    feed_bias,
    feed_out,
    char_table,
    cell_input,
    cell_recurrent,
    cell_bias,
    stream_weight,
    merging_kernel,
    norm_gains,
    biases,
):
    gathered = (
        lax.all_gather(attention_in, ("grp", "wide"), axis=1, tiled=True),
        lax.all_gather(attention_out, ("grp", "wide"), axis=1, tiled=True),
        lax.all_gather(feed_in, ("grp", "wide"), axis=1, tiled=True),
        lax.all_gather(feed_bias, ("grp", "wide"), axis=0, tiled=True),
        lax.all_gather(feed_out, ("grp", "wide"), axis=1, tiled=True),
        lax.all_gather(char_table, ("grp", "wide"), axis=1, tiled=True),
        lax.all_gather(cell_input, ("grp", "wide"), axis=1, tiled=True),
        lax.all_gather(cell_recurrent, ("grp", "wide"), axis=1, tiled=True),
        lax.all_gather(cell_bias, ("grp", "wide"), axis=1, tiled=True),
        lax.all_gather(stream_weight, ("grp", "wide"), axis=2, tiled=True),
        lax.all_gather(merging_kernel, ("grp", "wide"), axis=2, tiled=True),
        lax.all_gather(norm_gains, ("grp", "wide"), axis=1, tiled=True),
        lax.all_gather(biases, ("grp", "wide"), axis=1, tiled=True),
    )
    output, saved_values = forward(gathered, hidden, char_codes, word_length, sequence_length)
    saved_values, shards_late = lax.optimization_barrier(
        (
            saved_values,
            (
                attention_in,
                attention_out,
                feed_in,
                feed_bias,
                feed_out,
                char_table,
                cell_input,
                cell_recurrent,
                cell_bias,
                stream_weight,
                merging_kernel,
                norm_gains,
                biases,
            ),
        )
    )
    regathered = (
        lax.all_gather(shards_late[0], ("grp", "wide"), axis=1, tiled=True),
        lax.all_gather(shards_late[1], ("grp", "wide"), axis=1, tiled=True),
        lax.all_gather(shards_late[2], ("grp", "wide"), axis=1, tiled=True),
        lax.all_gather(shards_late[3], ("grp", "wide"), axis=0, tiled=True),
        lax.all_gather(shards_late[4], ("grp", "wide"), axis=1, tiled=True),
        lax.all_gather(shards_late[5], ("grp", "wide"), axis=1, tiled=True),
        lax.all_gather(shards_late[6], ("grp", "wide"), axis=1, tiled=True),
        lax.all_gather(shards_late[7], ("grp", "wide"), axis=1, tiled=True),
        lax.all_gather(shards_late[8], ("grp", "wide"), axis=1, tiled=True),
        lax.all_gather(shards_late[9], ("grp", "wide"), axis=2, tiled=True),
        lax.all_gather(shards_late[10], ("grp", "wide"), axis=2, tiled=True),
        lax.all_gather(shards_late[11], ("grp", "wide"), axis=1, tiled=True),
        lax.all_gather(shards_late[12], ("grp", "wide"), axis=1, tiled=True),
    )
    hidden_grad, param_grads = backward(regathered, saved_values, cotangent)
    group_sums = (
        lax.psum_scatter(
            param_grads[0].astype(jnp.bfloat16), "grp", scatter_dimension=1, tiled=True
        ).astype(jnp.float32),
        lax.psum_scatter(
            param_grads[1].astype(jnp.bfloat16), "grp", scatter_dimension=1, tiled=True
        ).astype(jnp.float32),
        lax.psum_scatter(
            param_grads[2].astype(jnp.bfloat16), "grp", scatter_dimension=1, tiled=True
        ).astype(jnp.float32),
        lax.psum_scatter(
            param_grads[3].astype(jnp.bfloat16), "grp", scatter_dimension=0, tiled=True
        ).astype(jnp.float32),
        lax.psum_scatter(
            param_grads[4].astype(jnp.bfloat16), "grp", scatter_dimension=1, tiled=True
        ).astype(jnp.float32),
        lax.psum_scatter(
            param_grads[5].astype(jnp.bfloat16), "grp", scatter_dimension=1, tiled=True
        ).astype(jnp.float32),
        lax.psum_scatter(
            param_grads[6].astype(jnp.bfloat16), "grp", scatter_dimension=1, tiled=True
        ).astype(jnp.float32),
        lax.psum_scatter(
            param_grads[7].astype(jnp.bfloat16), "grp", scatter_dimension=1, tiled=True
        ).astype(jnp.float32),
        lax.psum_scatter(
            param_grads[8].astype(jnp.bfloat16), "grp", scatter_dimension=1, tiled=True
        ).astype(jnp.float32),
        lax.psum_scatter(
            param_grads[9].astype(jnp.bfloat16), "grp", scatter_dimension=2, tiled=True
        ).astype(jnp.float32),
        lax.psum_scatter(
            param_grads[10].astype(jnp.bfloat16), "grp", scatter_dimension=2, tiled=True
        ).astype(jnp.float32),
        lax.psum_scatter(
            param_grads[11].astype(jnp.bfloat16), "grp", scatter_dimension=1, tiled=True
        ).astype(jnp.float32),
        lax.psum_scatter(
            param_grads[12].astype(jnp.bfloat16), "grp", scatter_dimension=1, tiled=True
        ).astype(jnp.float32),
    )
    summed = (
        lax.psum(group_sums[0].astype(jnp.bfloat16), "wide").astype(jnp.float32),
        lax.psum(group_sums[1].astype(jnp.bfloat16), "wide").astype(jnp.float32),
        lax.psum(group_sums[2].astype(jnp.bfloat16), "wide").astype(jnp.float32),
        lax.psum(group_sums[3].astype(jnp.bfloat16), "wide").astype(jnp.float32),
        lax.psum(group_sums[4].astype(jnp.bfloat16), "wide").astype(jnp.float32),
        lax.psum(group_sums[5].astype(jnp.bfloat16), "wide").astype(jnp.float32),
        lax.psum(group_sums[6].astype(jnp.bfloat16), "wide").astype(jnp.float32),
        lax.psum(group_sums[7].astype(jnp.bfloat16), "wide").astype(jnp.float32),
        lax.psum(group_sums[8].astype(jnp.bfloat16), "wide").astype(jnp.float32),
        lax.psum(group_sums[9].astype(jnp.bfloat16), "wide").astype(jnp.float32),
        lax.psum(group_sums[10].astype(jnp.bfloat16), "wide").astype(jnp.float32),
        lax.psum(group_sums[11].astype(jnp.bfloat16), "wide").astype(jnp.float32),
        lax.psum(group_sums[12].astype(jnp.bfloat16), "wide").astype(jnp.float32),
    )
    return (
        output,
        hidden_grad,
        summed[0],
        summed[1],
        summed[2],
        summed[3],
        summed[4],
        summed[5],
        summed[6],
        summed[7],
        summed[8],
        summed[9],
        summed[10],
        summed[11],
        summed[12],
    )


def solution(mesh):
    in_specs = (
        P(("grp", "wide"), None),
        P(("grp", "wide"), None),
        P(("grp", "wide")),
        P(("grp", "wide")),
        P(("grp", "wide"), None),
        P(None, ("grp", "wide")),
        P(None, ("grp", "wide")),
        P(None, ("grp", "wide")),
        P(("grp", "wide")),
        P(None, ("grp", "wide")),
        P(None, ("grp", "wide")),
        P(None, ("grp", "wide")),
        P(None, ("grp", "wide")),
        P(None, ("grp", "wide")),
        P(None, None, ("grp", "wide")),
        P(None, None, ("grp", "wide")),
        P(None, ("grp", "wide")),
        P(None, ("grp", "wide")),
    )
    out_specs = (
        P(("grp", "wide"), None),
        P(("grp", "wide"), None),
        P(None, "grp"),
        P(None, "grp"),
        P(None, "grp"),
        P("grp"),
        P(None, "grp"),
        P(None, "grp"),
        P(None, "grp"),
        P(None, "grp"),
        P(None, "grp"),
        P(None, None, "grp"),
        P(None, None, "grp"),
        P(None, "grp"),
        P(None, "grp"),
    )
    return jax.shard_map(shards, mesh=mesh, in_specs=in_specs, out_specs=out_specs, check_vma=False)
```

profile of v0, /device:TPU:0, one launch (start us, length us, event | category | flops | bytes accessed | tf_op | source)
XLA Modules:
  0.0 2474.2 jit_solution(11413091591701060921)
XLA Ops:
  14.1 43.9 %all-gather = bf16[32,24,10]{1,2,0:T(8,128)(2,1)S(1)} all-gather(bf16[1,24,10]{1,2,0:T(8,128)(2,1)} %bitcast.305), channel_id=1, replica_groups=mesh['grp'=8,'wide'=4] {'grp','wide'}, dimensions={0}, use_global_device_ids=true | all-gather | bytes 15840 | tf_op jit(solution)/shard_map/all_gather | solution.py:420
  59.1 38.3 %all_gather.74 = bf16[1000,256]{0,1:T(8,128)(2,1)S(1)} all-gather(bf16[1000,8]{0,1:T(8,128)(2,1)S(1)} %copy-done.52), channel_id=1, replica_groups=mesh['grp'=8,'wide'=4] {'grp','wide'}, dimensions={1}, use_global_device_ids=true | all-gather | bytes 528000 | tf_op jit(solution)/shard_map/all_gather | solution.py:413
  97.7 37.7 %all-gather.2 = bf16[32,72,2]{1,2,0:T(2,128)(2,1)S(1)} all-gather(bf16[1,72,2]{1,2,0:T(2,128)(2,1)S(1)} %bitcast.308), channel_id=1, replica_groups=mesh['grp'=8,'wide'=4] {'grp','wide'}, dimensions={0}, use_global_device_ids=true | all-gather | bytes 9504 | tf_op jit(solution)/shard_map/all_gather | solution.py:416
  135.8 37.4 %all-reduce.11 = bf16[3072]{0:T(1024)(128)(2,1)S(1)} all-reduce(bf16[3072]{0:T(1024)(128)(2,1)S(1)} %dynamic-update-slice), channel_id=1, replica_groups=mesh['grp'=8,'wide'=4] {'grp','wide'}, use_global_device_ids=true, to_apply=%add.11 | all-reduce | flops 3072 | bytes 12288
  173.9 40.0 %all-gather.1 = bf16[32,24,3]{1,2,0:T(4,128)(2,1)S(1)} all-gather(bf16[1,24,3]{1,2,0:T(4,128)(2,1)S(1)} %bitcast.306), channel_id=1, replica_groups=mesh['grp'=8,'wide'=4] {'grp','wide'}, dimensions={0}, use_global_device_ids=true | all-gather | bytes 4752 | tf_op jit(solution)/shard_map/all_gather | solution.py:419
  214.7 7.6 gather_fusion
  222.3 11.6 convolution_add_fusion.4
  244.5 5.5 broadcast.442.clone.1
  250.0 185.2 %while.56 = (s32[]{:T(128)}, f32[128,384]{1,0:T(8,128)S(1)}, f32[128,384]{1,0:T(8,128)S(1)}, f32[128,384]{1,0:T(8,128)S(1)}, f32[128,384]{1,0:T(8,128)S(1)}, /*i...) while((s32[]{:T(128)}, f32[128,384]{1,0:T(8,128)S(1)}, ...), condition=%wide.region_7.8_spmd.clone, body=%wide.region_6.7_spmd.clone.sunk | while | flops 229048576 | bytes 13992259 | solution.py:143
  445.6 7.8 fusion.84
  460.8 46.5 %all-gather.35.cloned.1.call-done = bf16[3,1536,768]{1,2,0:T(8,128)(2,1)} async-done(((bf16[3,1536,24]{1,2,0:T(8,128)(2,1)}), bf16[3,1536,768]{1,2,0:T(8,128)(2,1)}) %all-gather.35.cloned.1.call-update) | async-done | bytes 7077904 | tf_op jit(solution)/shard_map/all_gather | solution.py:418
  507.3 10.3 copy.126
  525.8 39.1 %all-gather.3 = bf16[32,24,3]{1,2,0:T(4,128)(2,1)S(1)} all-gather(bf16[1,24,3]{1,2,0:T(4,128)(2,1)S(1)} %bitcast.307), channel_id=1, replica_groups=mesh['grp'=8,'wide'=4] {'grp','wide'}, dimensions={0}, use_global_device_ids=true | all-gather | bytes 4752 | tf_op jit(solution)/shard_map/all_gather | solution.py:455
  568.8 8.0 all-gather.49.cloned.1.call-done
  581.8 69.3 %all-gather.37.cloned.1.call-done = bf16[3,1536,768]{1,2,0:T(8,128)(2,1)} async-done(((bf16[3,1536,24]{1,2,0:T(8,128)(2,1)}), bf16[3,1536,768]{1,2,0:T(8,128)(2,1)}) %all-gather.37.cloned.1.call-update) | async-done | bytes 7077904 | tf_op jit(solution)/shard_map/all_gather | solution.py:454
  655.6 54.3 %all-gather.39.cloned.1.call-done = bf16[2,768,768]{1,2,0:T(8,128)(2,1)} async-done(((bf16[2,768,24]{1,2,0:T(8,128)(2,1)}), bf16[2,768,768]{1,2,0:T(8,128)(2,1)}) %all-gather.39.cloned.1.call-update) | async-done | bytes 2359312 | tf_op jit(solution)/shard_map/all_gather | solution.py:453
  712.4 62.7 %all-gather.41.cloned.1.call-done = bf16[3072,768]{0,1:T(8,128)(2,1)} async-done(((bf16[3072,24]{0,1:T(8,128)(2,1)}), bf16[3072,768]{0,1:T(8,128)(2,1)}) %all-gather.41.cloned.1.call-update) | async-done | bytes 4718608 | tf_op jit(solution)/shard_map/all_gather | solution.py:448
  775.1 8.4 fusion.171
  783.5 57.0 %all-gather.43.cloned.1.call-done = bf16[768,3072]{0,1:T(8,128)(2,1)} async-done(((bf16[768,96]{0,1:T(8,128)(2,1)}), bf16[768,3072]{0,1:T(8,128)(2,1)}) %all-gather.43.cloned.1.call-update) | async-done | bytes 4718608 | tf_op jit(solution)/shard_map/all_gather | solution.py:446
  844.5 51.6 %all-gather.45.cloned.1.call-done = bf16[768,768]{0,1:T(8,128)(2,1)} async-done(((bf16[768,24]{0,1:T(8,128)(2,1)}), bf16[768,768]{0,1:T(8,128)(2,1)}) %all-gather.45.cloned.1.call-update) | async-done | bytes 1179664 | tf_op jit(solution)/shard_map/all_gather | solution.py:445
  901.0 5.5 broadcast.442
  906.5 5.6 broadcast.442.clone.2
  918.9 354.4 %while.57 = (s32[]{:T(128)}, f32[128,384]{1,0:T(8,128)}, f32[128,384]{1,0:T(8,128)}, f32[1152]{0:T(1024)S(1)}, f32[1152]{0:T(1024)S(1)}, /*index=5*/f32[20,128,1...) while((s32[]{:T(128)}, f32[128,384]{1,0:T(8,128)}, ...), condition=%wide.region_37.38_spmd.clone, body=%wide.region_34.37_spmd.clone.sunk | while | flops 234457600 | bytes 33476860 | solution.py:277
  1273.3 9.9 rev.3
  1283.3 9.1 maximum_reduce_fusion
  1299.8 7.7 rev.5
  1307.5 7.8 convert.110
  1316.7 7.6 fusion.75
  1324.3 14.9 scatter_custom_fusion
  1343.3 6.9 copy.137
  1350.5 6.8 fusion.79
  1369.8 6.6 copy.148
  1382.7 10.3 copy.138
  1395.6 8.7 fusion.76
  1416.0 20.5 all-reduce.12
  1440.1 47.4 %reduce-scatter.44.cloned.1.call-done = bf16[96,10]{1,0:T(8,128)(2,1)} async-done(((bf16[768,10]{1,0:T(8,128)(2,1)}), bf16[96,10]{1,0:T(8,128)(2,1)}) %reduce-scatter.44.cloned.1.call-update) | async-done | bytes 1936
  1488.9 63.8 %reduce-scatter.36.cloned.1.call-done = bf16[32,1000]{1,0:T(8,128)(2,1)} async-done(((bf16[256,1000]{1,0:T(8,128)(2,1)}), bf16[32,1000]{1,0:T(8,128)(2,1)}) %reduce-scatter.36.cloned.1.call-update) | async-done | bytes 64016
  1554.6 109.4 %all-reduce.20.cloned.1.call-done = bf16[2,768,768]{1,0,2:T(2,128)(2,1)} async-done(((bf16[2,768,768]{1,0,2:T(2,128)(2,1)}), bf16[2,768,768]{1,0,2:T(2,128)(2,1)}) %all-reduce.20.cloned.1.call-update) | async-done | bytes 2359312
  1665.8 67.9 %reduce-scatter.38.cloned.1.call-done = bf16[288,384]{1,0:T(8,128)(2,1)} async-done(((bf16[2304,384]{1,0:T(8,128)(2,1)}), bf16[288,384]{1,0:T(8,128)(2,1)}) %reduce-scatter.38.cloned.1.call-update) | async-done | bytes 221200
  1735.5 96.2 %reduce-scatter.34.cloned.1.call-done = bf16[384,768]{1,0:T(8,128)(2,1)} async-done(((bf16[3072,768]{1,0:T(8,128)(2,1)}), bf16[384,768]{1,0:T(8,128)(2,1)}) %reduce-scatter.34.cloned.1.call-update) | async-done | bytes 589840
  1833.8 130.7 %reduce-scatter.32.cloned.1.call-done = bf16[3,1536,96]{1,2,0:T(8,128)(2,1)} async-done(((bf16[3,1536,768]{1,2,0:T(8,128)(2,1)}), bf16[3,1536,96]{1,2,0:T(8,128)(2,1)}) %reduce-scatter.32.cloned.1.call-update) | async-done | bytes 884752 | tf_op jit(solution)/shard_map/reduce_scatter | solution.py:490
  1964.5 67.5 %reduce-scatter.26.cloned.1.call-done = bf16[768,96]{0,1:T(8,128)(2,1)} async-done(((bf16[768,768]{0,1:T(8,128)(2,1)}), bf16[768,96]{0,1:T(8,128)(2,1)}) %reduce-scatter.26.cloned.1.call-update) | async-done | bytes 147472 | tf_op jit(solution)/shard_map/reduce_scatter | solution.py:463
  2032.0 67.3 %reduce-scatter.30.cloned.1.call-done = bf16[256,288]{0,1:T(8,128)(2,1)} async-done(((bf16[256,2304]{0,1:T(8,128)(2,1)}), bf16[256,288]{0,1:T(8,128)(2,1)}) %reduce-scatter.30.cloned.1.call-update) | async-done | bytes 147472 | tf_op jit(solution)/shard_map/reduce_scatter | solution.py:478
  2099.3 82.1 %reduce-scatter.24.cloned.1.call-done = bf16[768,288]{0,1:T(8,128)(2,1)} async-done(((bf16[768,2304]{0,1:T(8,128)(2,1)}), bf16[768,288]{0,1:T(8,128)(2,1)}) %reduce-scatter.24.cloned.1.call-update) | async-done | bytes 442384 | tf_op jit(solution)/shard_map/reduce_scatter | solution.py:460
  2181.4 98.9 %reduce-scatter.28.cloned.1.call-done = bf16[3072,96]{0,1:T(8,128)(2,1)} async-done(((bf16[3072,768]{0,1:T(8,128)(2,1)}), bf16[3072,96]{0,1:T(8,128)(2,1)}) %reduce-scatter.28.cloned.1.call-update) | async-done | bytes 589840 | tf_op jit(solution)/shard_map/reduce_scatter | solution.py:472
  2282.3 61.2 %all-gather.47.cloned.1.call-done = bf16[768,2304]{0,1:T(8,128)(2,1)} async-done(((bf16[768,72]{0,1:T(8,128)(2,1)}), bf16[768,2304]{0,1:T(8,128)(2,1)}) %all-gather.47.cloned.1.call-update) | async-done | bytes 3538960 | tf_op jit(solution)/shard_map/all_gather | solution.py:444
  2346.9 31.1 %all-reduce.22.cloned.1.call-done = (bf16[1000,32]{1,0:T(8,128)(2,1)}, bf16[384]{0:T(512)(128)(2,1)}, bf16[2,288]{1,0:T(2,128)(2,1)}, bf16[3,96]{1,0:T(4,128)(2,1)}, bf16[10,96]{1,0:T(8,128)(2,1)}) async-done(((bf16[1000,32]{1,0:T(8,128)(2,1)}, bf16[384]{0:T(512)(128)(2,1)}, bf16[2,288]{1,0:T(2,128)(2,1)}, bf16[3,96]{1,0:T(4,128)(2,1)}, bf16[10,96]{1,0:T(8,128)(2,1)}), (bf16[1000,32]{1,0:T(8,128)(2,1)}, ...) | async-done | bytes 68432 | tf_op jit(solution)/shard_map/psum | solution.py:506
  2384.6 72.4 %all-reduce.24.cloned.1.call-done = (bf16[384,288]{1,0:T(8,128)(2,1)}, bf16[2,768,96]{1,0,2:T(2,128)(2,1)}, bf16[768,288]{0,1:T(8,128)(2,1)}, bf16[768,96]{0,1:T...) async-done(((bf16[384,288]{1,0:T(8,128)(2,1)}, bf16[2,768,96]{1,0,2:T(2,128)(2,1)}, ...) | async-done | bytes 3317776 | tf_op jit(solution)/shard_map/psum | solution.py:508
  (1256 shorter events, 557.9 us)
Async XLA Ops:
  7.2 51.9 %copy-start.52 = (bf16[1000,8]{0,1:T(8,128)(2,1)S(1)}, bf16[1000,8]{0,1:T(8,128)(2,1)}, u32[]{:S(2)}) copy-start(bf16[1000,8]{0,1:T(8,128)(2,1)} %param.32) | copy-start | bytes 48004
  7.2 215.1 %all-gather.31.cloned.1.call-start = ((), (), s32[]{:S(2)}) async-start(), calls=%async_computation.16 | async-start | bytes 1216512 | tf_op jit(solution)/shard_map/all_gather | solution.py:414
  7.9 226.0 %all-gather.33.cloned.1.call-start = ((), (), s32[]{:S(2)}) async-start(), calls=%async_computation.17 | async-start | bytes 1824768 | tf_op jit(solution)/shard_map/all_gather | solution.py:415
  8.7 426.7 %all-gather.29.cloned.1.call-start = ((), (), s32[]{:S(2)}) async-start(), calls=%async_computation.15 | async-start | bytes 2433024 | tf_op jit(solution)/shard_map/all_gather | solution.py:417
  9.4 88.2 %copy-start.47 = (s32[128,20]{0,1:T(8,128)S(1)}, s32[128,20]{0,1:T(8,128)}, u32[]{:S(2)}) copy-start(s32[128,20]{0,1:T(8,128)} %param.23) | copy-start | bytes 30724
  9.4 88.2 %copy-start.74 = (bf16[2,72]{1,0:T(2,128)(2,1)S(1)}, bf16[2,72]{1,0:T(2,128)(2,1)}, u32[]{:S(2)}) copy-start(bf16[2,72]{1,0:T(2,128)(2,1)} %param.35) | copy-start | bytes 868
  9.4 427.9 %all-gather.21.cloned.1.call-start = ((), (), s32[]{:S(2)}) async-start(), calls=%async_computation.11 | async-start | bytes 3649536 | tf_op jit(solution)/shard_map/all_gather | solution.py:408
  10.0 431.7 %all-gather.23.cloned.1.call-start = ((), (), s32[]{:S(2)}) async-start(), calls=%async_computation.12 | async-start | bytes 1216512 | tf_op jit(solution)/shard_map/all_gather | solution.py:409
  10.6 124.9 %copy-start.77 = (bf16[96]{0:T(256)(128)(2,1)S(1)}, bf16[96]{0:T(256)(128)(2,1)}, u32[]{:S(2)}) copy-start(bf16[96]{0:T(256)(128)(2,1)} %param.30) | copy-start | bytes 580
  10.6 163.2 %copy-start.72 = (bf16[3,24]{1,0:T(4,128)(2,1)S(1)}, bf16[3,24]{1,0:T(4,128)(2,1)}, u32[]{:S(2)}) copy-start(bf16[3,24]{1,0:T(4,128)(2,1)} %param.38) | copy-start | bytes 436
  10.6 435.0 %all-gather.25.cloned.1.call-start = ((), (), s32[]{:S(2)}) async-start(), calls=%async_computation.13 | async-start | bytes 4866048 | tf_op jit(solution)/shard_map/all_gather | solution.py:410
  11.2 442.2 %all-gather.27.cloned.1.call-start = ((), (), s32[]{:S(2)}) async-start(), calls=%async_computation.14 | async-start | bytes 4866048 | tf_op jit(solution)/shard_map/all_gather | solution.py:412
  11.9 495.3 %all-gather.35.cloned.1.call-start = ((), (), s32[]{:S(2)}) async-start(), calls=%async_computation.18 | async-start | bytes 7299072 | tf_op jit(solution)/shard_map/all_gather | solution.py:418
  12.7 564.1 %all-gather.49.cloned.1.call-start = ((), (), s32[]{:S(2)}) async-start(), calls=%async_computation.28 | async-start | bytes 1824768 | tf_op jit(solution)/shard_map/all_gather | solution.py:451
  173.8 267.1 %copy-start.73 = (f32[128]{0:T(128)}, f32[128]{0:T(128)S(1)}, u32[]{:S(2)}) copy-start(f32[128]{0:T(128)S(1)} %compare_select_fusion.2) | copy-start | bytes 1540
  222.3 11.7 copy-start.12
  517.6 47.6 %copy-start.75 = (s32[128]{0:T(128)S(1)}, s32[128]{0:T(128)}, u32[]{:S(2)}) copy-start(s32[128]{0:T(128)} %param.24) | copy-start | bytes 1540
  522.4 44.3 %copy-start = (f32[128,768]{1,0:T(8,128)}, f32[128,768]{1,0:T(8,128)S(1)}, u32[]{:S(2)}) copy-start(f32[128,768]{1,0:T(8,128)S(1)} %get-tuple-element.640) | copy-start | bytes 1179652
  522.4 128.7 %all-gather.37.cloned.1.call-start = ((), (), s32[]{:S(2)}) async-start(), calls=%async_computation.19 | async-start | bytes 7299072 | tf_op jit(solution)/shard_map/all_gather | solution.py:454
  523.0 186.8 %all-gather.39.cloned.1.call-start = ((), (), s32[]{:S(2)}) async-start(), calls=%async_computation.20 | async-start | bytes 2433024 | tf_op jit(solution)/shard_map/all_gather | solution.py:453
  523.7 251.4 %all-gather.41.cloned.1.call-start = ((), (), s32[]{:S(2)}) async-start(), calls=%async_computation.21 | async-start | bytes 4866048 | tf_op jit(solution)/shard_map/all_gather | solution.py:448
  524.3 316.1 %all-gather.43.cloned.1.call-start = ((), (), s32[]{:S(2)}) async-start(), calls=%async_computation.22 | async-start | bytes 4866048 | tf_op jit(solution)/shard_map/all_gather | solution.py:446
  525.1 371.1 %all-gather.45.cloned.1.call-start = ((), (), s32[]{:S(2)}) async-start(), calls=%async_computation.23 | async-start | bytes 1216512 | tf_op jit(solution)/shard_map/all_gather | solution.py:445
  565.6 751.1 %all-gather.51.cloned.1.call-start = ((), (), s32[]{:S(2)}) async-start(), calls=%async_computation.29 | async-start | bytes 1216512 | tf_op jit(solution)/shard_map/all_gather | solution.py:450
  566.7 143.1 %copy-start.58 = (f32[128]{0:T(128)}, f32[128]{0:T(128)S(1)}, u32[]{:S(2)}) copy-start(f32[128]{0:T(128)S(1)} %negate_multiply_fusion.4) | copy-start | bytes 1540
  568.7 868.5 %reduce-scatter.42.cloned.1.call-start = ((), (), s32[]{:S(2)}) async-start(), calls=%async_computation.36 | async-start | bytes 221184
  655.5 243.0 %copy-start.2 = (f32[128,1536]{1,0:T(8,128)}, f32[128,1536]{1,0:T(8,128)S(1)}, u32[]{:S(2)}) copy-start(f32[128,1536]{1,0:T(8,128)S(1)} %fusion.121) | copy-start | bytes 2359300
  712.4 128.0 %copy-start.7 = (f32[128,768]{1,0:T(8,128)}, f32[128,768]{1,0:T(8,128)S(1)}, u32[]{:S(2)}) copy-start(f32[128,768]{1,0:T(8,128)S(1)} %get-tuple-element.1104) | copy-start | bytes 1179652
  712.4 128.0 %copy-start.69 = (f32[128]{0:T(128)}, f32[128]{0:T(128)S(1)}, u32[]{:S(2)}) copy-start(f32[128]{0:T(128)S(1)} %negate_multiply_fusion.3) | copy-start | bytes 1540
  783.5 60.8 %copy-start.17 = (bf16[128,3072]{1,0:T(8,128)(2,1)}, bf16[128,3072]{1,0:T(8,128)(2,1)S(1)}, u32[]{:S(2)}) copy-start(bf16[128,3072]{1,0:T(8,128)(2,1)S(1)} %get-tuple-element.1163) | copy-start | bytes 2359300
  844.5 55.7 %copy-start.4 = (f32[128,768]{1,0:T(8,128)}, f32[128,768]{1,0:T(8,128)S(1)}, u32[]{:S(2)}) copy-start(f32[128,768]{1,0:T(8,128)S(1)} %get-tuple-element.1102) | copy-start | bytes 1179652
  844.5 55.7 %copy-start.65 = (f32[128]{0:T(128)}, f32[128]{0:T(128)S(1)}, u32[]{:S(2)}) copy-start(f32[128]{0:T(128)S(1)} %negate_multiply_fusion.2) | copy-start | bytes 1540
  1283.2 11.3 copy-start.23
  1283.3 11.3 copy-start.30
  1298.3 140.3 %reduce-scatter.40.cloned.1.call-start = ((), (), s32[]{:S(2)}) async-start(), calls=%async_computation.35 | async-start | bytes 663552
  1299.6 187.9 %reduce-scatter.44.cloned.1.call-start = ((), (), s32[]{:S(2)}) async-start(), calls=%async_computation.37 | async-start | bytes 221184
  1316.6 236.2 %reduce-scatter.36.cloned.1.call-start = ((), (), s32[]{:S(2)}) async-start(), calls=%async_computation.33 | async-start | bytes 589824
  1340.3 323.6 %all-reduce.20.cloned.1.call-start = ((), (), s32[]{:S(2)}) async-start(), calls=%async_computation.38 | async-start | bytes 4718592
  1350.2 383.5 %reduce-scatter.38.cloned.1.call-start = ((), (), s32[]{:S(2)}) async-start(), calls=%async_computation.34 | async-start | bytes 1990656
  1365.1 466.5 %reduce-scatter.34.cloned.1.call-start = ((), (), s32[]{:S(2)}) async-start(), calls=%async_computation.32 | async-start | bytes 5308416
  1376.5 588.1 %reduce-scatter.32.cloned.1.call-start = ((), (), s32[]{:S(2)}) async-start(), calls=%async_computation.31 | async-start | bytes 7962624 | tf_op jit(solution)/shard_map/reduce_scatter | solution.py:490
  1393.1 638.9 %reduce-scatter.26.cloned.1.call-start = ((), (), s32[]{:S(2)}) async-start(), calls=%async_computation.26 | async-start | bytes 1327104 | tf_op jit(solution)/shard_map/reduce_scatter | solution.py:463
  1395.6 703.7 %reduce-scatter.30.cloned.1.call-start = ((), (), s32[]{:S(2)}) async-start(), calls=%async_computation.30 | async-start | bytes 1327104 | tf_op jit(solution)/shard_map/reduce_scatter | solution.py:478
  1404.4 777.0 %reduce-scatter.24.cloned.1.call-start = ((), (), s32[]{:S(2)}) async-start(), calls=%async_computation.25 | async-start | bytes 3981312 | tf_op jit(solution)/shard_map/reduce_scatter | solution.py:460
  1408.4 871.9 %reduce-scatter.28.cloned.1.call-start = ((), (), s32[]{:S(2)}) async-start(), calls=%async_computation.27 | async-start | bytes 5308416 | tf_op jit(solution)/shard_map/reduce_scatter | solution.py:472
  1413.3 930.2 %all-gather.47.cloned.1.call-start = ((), (), s32[]{:S(2)}) async-start(), calls=%async_computation.24 | async-start | bytes 3649536 | tf_op jit(solution)/shard_map/all_gather | solution.py:444
  1414.1 963.9 %all-reduce.22.cloned.1.call-start = ((), (), s32[]{:S(2)}) async-start(), calls=%async_computation.39 | async-start | bytes 527360 | tf_op jit(solution)/shard_map/psum | solution.py:506
  1554.5 902.5 %all-reduce.24.cloned.1.call-start = ((), (), s32[]{:S(2)}) async-start(), calls=%async_computation.40 | async-start | bytes 6782976 | tf_op jit(solution)/shard_map/psum | solution.py:508
  (235 other events, 560.2 us)
Sparse Core Ops, SparseCore 0:
  10.9 57.4 all-gather.30
  71.2 54.3 all-gather.32
  128.4 56.1 all-gather.28
  187.5 58.9 all-gather.20
  249.2 52.9 all-gather.22
  305.0 62.5 all-gather.24
  370.5 62.3 all-gather.26
  435.7 71.4 all-gather.34
  522.5 54.2 all-gather.48
  579.5 71.5 all-gather.36
  653.9 55.8 all-gather.38
  712.6 62.4 all-gather.40
  778.0 62.3 all-gather.42
  843.2 52.8 all-gather.44
  898.9 53.0 all-gather.50
  1298.4 60.0 reduce-scatter.41
  1362.2 61.1 reduce-scatter.39
  1427.4 60.0 reduce-scatter.43
  1491.8 60.9 reduce-scatter.35
  1556.2 107.6 all-reduce.19
  1668.4 65.2 reduce-scatter.37
  1737.3 94.2 reduce-scatter.33
  1835.4 129.1 reduce-scatter.31
  1968.7 63.2 reduce-scatter.25
  2036.3 62.9 reduce-scatter.29
  2103.2 78.1 reduce-scatter.23
  2185.3 94.9 reduce-scatter.27
  2283.6 59.8 all-gather.46
  2347.5 30.4 all-reduce.21
  2382.1 74.8 all-reduce.23
where the time goes:
time: 2490 us; the launch traced here: 2470 us
  waiting for transfers between devices  1350 us (54%)
  local copies, waits for them, and re-layouts  281 us (11%)
  blocking collectives  257 us (10%)
  other arithmetic  223 us (9%)
  matrix products  203 us (8%)
  loops' own time  137 us (6%)
    unnamed x37, waiting for transfers between devices  393 us
    reduce_scatter x1, waiting for transfers between devices, shards(): lax.psum_scatter(param_grads[10].astype(jnp.bfloat16), 'grp', scatter_dim...  131 us
    reduce_scatter x1, waiting for transfers between devices, shards(): lax.psum_scatter(param_grads[4].astype(jnp.bfloat16), 'grp', scatter_dime...  98.9 us
    dot_general x48, matrix products, dot_plain(): return jnp.dot(left_side, right_side, preferred_element_type=jnp.float32)  83.4 us
    reduce_scatter x1, waiting for transfers between devices, shards(): lax.psum_scatter(param_grads[0].astype(jnp.bfloat16), 'grp', scatter_dime...  82.1 us
    dot_general x48, matrix products, dot_second(): lax.dot_general(left_side, right_side, (((1,), (1,)), ((), ())), preferre...  76.8 us
    psum x1, waiting for transfers between devices, shards(): lax.psum(group_sums[7].astype(jnp.bfloat16), 'wide').astype(jnp.float32)  72.4 us
    another operation x1, loops' own time, backward(): lax.scan(retreat, (zero_state, zero_state, zero_bias, zero_bias), jnp.ara...  71.5 us
  transfers between devices with their start and end apart: 30, of which 20 were waited for; matrix products, arithmetic and copies ran while one was open for 27% of the time, Pallas kernels for 0%

commit v1 on v0

v1 whole, which is shorter than its diff:
```python
from functools import partial

import jax
import jax.numpy as jnp
from jax import lax
from jax.experimental import pallas as pl
from jax.experimental.pallas import tpu as pltpu
from jax.sharding import PartitionSpec as P

HEADS = 12
HID = 384
EMB = 256
CHARS = 20
TOKENS = 128
norm_eps = 1e-05
masked_score = -1e30
MESH = pl.DeviceIdType.MESH
EVERY = slice(None)
LOW = jnp.bfloat16
WIDE = jnp.float32

BLOCKS = {
    "CELL": (144, 768),
    "TABLE": (16, 1024),
    "ATT": (144, 768),
    "OUT": (48, 1024),
    "IN": (192, 768),
    "FEED": (48, 3072),
    "STREAM": (48, 1536),
    "MERGE": (48, 4608),
}
KINDS = tuple(BLOCKS)
PIECES = (
    ("CELL", 0, 384, 384),
    ("TABLE", 0, 512, 512),
    ("ATT", 0, 384, 384),
    ("OUT", 0, 512, 512),
    ("IN", 0, 128, 128),
    ("IN", 256, 512, 256),
    ("FEED", 0, 768, 768),
    ("FEED", 1536, 2304, 768),
    ("STREAM", 0, 768, 768),
    ("MERGE", 0, 768, 768),
    ("MERGE", 1536, 2304, 768),
    ("MERGE", 3072, 3840, 768),
)

X_WIDTH = 768
RECORD = X_WIDTH + 4 * HID
GATE_R, GATE_Z, GATE_N, GATE_Q = (X_WIDTH + i * HID for i in range(4))


def dot_plain(left_side, right_side):
    return jnp.dot(left_side, right_side, preferred_element_type=WIDE)


def dot_first(left_side, right_side):
    return lax.dot_general(left_side, right_side, (((0,), (0,)), ((), ())), preferred_element_type=WIDE)


def dot_second(left_side, right_side):
    return lax.dot_general(left_side, right_side, (((1,), (1,)), ((), ())), preferred_element_type=WIDE)


def sigmoid(inputs):
    return 0.5 * jnp.tanh(0.5 * inputs) + 0.5


class Spot:
    def __init__(self, per_place):
        self.grp, self.wide = lax.axis_index("grp"), lax.axis_index("wide")
        self.z, self.x = self.grp // 2, self.grp % 2
        self.y, self.core = self.wide // per_place, self.wide % 2
        self.to_x = (self.grp + 1 - 2 * self.x, self.wide)
        self.to_y = (self.grp, self.wide + per_place - 2 * per_place * self.y)
        self.sibling = (self.grp, self.wide + 1 - 2 * self.core)

    def hop(self, k):
        return (2 * ((self.z + k) % 4) + self.x, self.wide)

    def greet(self):
        barrier = pltpu.get_barrier_semaphore()
        for other in [self.to_x, self.to_y, self.sibling] + [self.hop(k) for k in (1, 2, 3)]:
            pl.semaphore_signal(barrier, 1, device_id=other, device_id_type=MESH)
        pl.semaphore_wait(barrier, 6)

    def near(self, core):
        if core == 0:
            return self.x, self.y, self.to_x, self.to_y
        return self.y, self.x, self.to_y, self.to_x


def remote(source, target, sent, received, device):
    return pltpu.make_async_remote_copy(
        src_ref=source, dst_ref=target, send_sem=sent, recv_sem=received, device_id=device, device_id_type=MESH
    )


class Gather:
    def __init__(self, spot, own, whole, sems):
        self.spot, self.own, self.whole = spot, own, whole
        self.sent, self.got = sems

    def region(self, core, p, z, f, l):
        kind, first, second, width = PIECES[p]
        lanes = pl.ds((first, second)[core], width)
        return self.whole[kind].at[z, f, l, :, lanes] if core == 0 else self.whole[kind].at[z, l, f, :, lanes]

    def move(self, part, p, j, device, source=None):
        return remote(part if source is None else source, part, self.sent.at[p, j], self.got.at[p, j], device)

    def along(self, core, p, k):
        f, l, _, _ = self.spot.near(core)
        kind, first, second, width = PIECES[p]
        source = self.own[kind].at[:, pl.ds((first, second)[core], width)]
        return self.move(self.region(core, p, self.spot.z, f, l), p, k - 1, self.spot.hop(k), source)

    def along_in(self, core, p, k):
        f, l, _, _ = self.spot.near(core)
        return self.move(self.region(core, p, (self.spot.z + 4 - k) % 4, f, l), p, k - 1, self.spot.hop(k))

    def line(self, core, p, mine):
        f, l, to_f, _ = self.spot.near(core)
        return self.move(self.region(core, p, EVERY, f if mine else 1 - f, l), p, 3, to_f)

    def plane(self, core, p, mine):
        f, l, _, to_l = self.spot.near(core)
        return self.move(self.region(core, p, EVERY, EVERY, l if mine else 1 - l), p, 4, to_l)

    def aside(self, core, p, j):
        f, l, _, _ = self.spot.near(core)
        if j < 3:
            part = self.region(core, p, (self.spot.z + 3 - j) % 4, f, l)
        elif j == 3:
            part = self.region(core, p, EVERY, 1 - f, l)
        else:
            part = self.region(core, p, EVERY, EVERY, 1 - l)
        return self.move(part, p, 5 + j, self.spot.sibling)

    def start(self, core, p):
        for k in (1, 3, 2):
            self.along(core, p, k).start()

    def second(self, core, p):
        for k in (1, 3, 2):
            self.along_in(core, p, k).wait_recv()
        self.line(core, p, True).start()
        for k in (1, 3, 2):
            self.aside(core, p, k - 1).start()

    def third(self, core, p):
        self.line(core, p, False).wait_recv()
        self.plane(core, p, True).start()
        self.aside(core, p, 3).start()

    def fourth(self, core, p):
        self.plane(core, p, False).wait_recv()
        self.aside(core, p, 4).start()

    def fifth(self, core, p):
        for j in range(5):
            self.aside(1 - core, p, j).wait_recv()

    def drain(self, core, p):
        for k in (1, 2, 3):
            self.along(core, p, k).wait_send()
        self.line(core, p, True).wait_send()
        self.plane(core, p, True).wait_send()
        for j in range(5):
            self.aside(core, p, j).wait_send()

    def program(self):
        steps = []
        count = len(PIECES)
        ahead = 3
        for p in range(ahead):
            steps.append(("start", p))
        for s in range(count + 3):
            if s + ahead < count:
                steps.append(("start", s + ahead))
            for lag, stage in enumerate(("second", "third", "fourth", "fifth")):
                if 0 <= s - lag < count:
                    steps.append((stage, s - lag))
        return steps

    def run(self, steps):
        for core in (0, 1):

            @pl.when(self.spot.core == core)
            def _():
                for stage, p in steps:
                    getattr(self, stage)(core, p)


def gru_forward_step(t, cell, record, state, total, shifts, lengths):
    for way in (0, 1):
        base = way * RECORD
        place = t if way == 0 else CHARS - 1 - t
        live = lengths[...] > place
        lanes = pl.ds(way * HID, HID)
        h = state[:, lanes]
        record[t, :, pl.ds(base + EMB, HID)] = h.astype(LOW)
        x = record[t, :, pl.ds(base, X_WIDTH)]
        weights = cell[pl.ds(2 * way, 2)].reshape(3 * HID, X_WIDTH)
        both = dot_second(x, weights[: 2 * HID])
        drive_n = dot_second(x[:, :EMB], weights[2 * HID :, :EMB]) + shifts[way, 0:1]
        recur_n = dot_second(x[:, EMB : EMB + HID], weights[2 * HID :, EMB : EMB + HID]) + shifts[way, 1:2]
        r = sigmoid(both[:, :HID])
        u = sigmoid(both[:, HID:])
        n = jnp.tanh(drive_n + r * recur_n)
        fresh = jnp.where(live, n + u * (h - n), h)
        state[:, lanes] = fresh
        total[:, lanes] += jnp.where(live, fresh, 0.0)
        record[t, :, pl.ds(base + GATE_R, HID)] = r.astype(LOW)
        record[t, :, pl.ds(base + GATE_Z, HID)] = u.astype(LOW)
        record[t, :, pl.ds(base + GATE_N, HID)] = n.astype(LOW)
        record[t, :, pl.ds(base + GATE_Q, HID)] = recur_n.astype(LOW)


def one_hot(codes, t, vocabulary):
    return (lax.broadcasted_iota(jnp.int32, (TOKENS, vocabulary), 1) == codes[t]).astype(LOW)


def forward_kernel(per_place, *refs):
    count = len(KINDS)
    own = dict(zip(KINDS, refs[:count]))
    codes, lengths = refs[count : count + 2]
    outs = refs[count + 2 :]
    whole = dict(zip(KINDS, outs[:count]))
    record_out, pooled = outs[count : count + 2]
    record, state, shifts, sent, got, own_sem, record_sem = outs[count + 2 :]
    spot = Spot(per_place)
    own_copies = [
        pltpu.make_async_copy(own[kind], whole[kind].at[spot.z, spot.x, spot.y], own_sem.at[i])
        for i, kind in enumerate(KINDS)
    ]
    for copy in own_copies:
        copy.start()
    spot.greet()
    for copy in own_copies:
        copy.wait()
    gather = Gather(spot, own, whole, (sent, got))
    steps = gather.program()
    lead = steps.index(("fifth", 1)) + 1
    gather.run(steps[:lead])

    table = whole["TABLE"][...].reshape(EMB, 1024)
    cell = whole["CELL"]
    ones = (lax.broadcasted_iota(jnp.int32, (TOKENS, 128), 1) < 2).astype(LOW)

    def embed(c, carry):
        rows = dot_second(one_hot(codes, c, 1024), table).astype(LOW)
        record[c, :, pl.ds(0, EMB)] = rows
        record[CHARS - 1 - c, :, pl.ds(RECORD, EMB)] = rows
        record[c, :, pl.ds(EMB + HID, 128)] = ones
        record[c, :, pl.ds(RECORD + EMB + HID, 128)] = ones
        return carry

    lax.fori_loop(0, CHARS, embed, 0)
    pick = (
        lax.broadcasted_iota(jnp.int32, (8, 128), 0) == lax.broadcasted_iota(jnp.int32, (8, 128), 1)
    ).astype(LOW)
    for way in (0, 1):
        late = cell[pl.ds(2 * way, 2)].reshape(3 * HID, X_WIDTH)[2 * HID :, EMB + HID :]
        shifts[way] = dot_second(pick, late)
    state[...] = jnp.zeros_like(state)
    pooled[...] = jnp.zeros_like(pooled)
    rest = steps[lead:]
    share = -(-len(rest) // CHARS)

    def advance(t, carry):
        gru_forward_step(t, cell, record, state, pooled, shifts, lengths)
        pltpu.make_async_copy(record.at[t], record_out.at[t], record_sem.at[t]).start()
        for k in range(CHARS):

            @pl.when(t == k)
            def _():
                gather.run(rest[k * share : (k + 1) * share])

        return carry

    lax.fori_loop(0, CHARS, advance, 0)
    pooled[...] = pooled[...] / lengths[...].astype(WIDE)

    def landed(t, carry):
        pltpu.make_async_copy(record.at[t], record_out.at[t], record_sem.at[t]).wait()
        return carry

    lax.fori_loop(0, CHARS, landed, 0)
    gather.run([("drain", p) for p in range(len(PIECES))])


def gather_and_read(own, codes, lengths, per_place):
    count = len(KINDS)
    in_vmem = pl.BlockSpec(memory_space=pltpu.VMEM)
    anywhere = pl.BlockSpec(memory_space=pl.ANY)
    results = pl.pallas_call(
        partial(forward_kernel, per_place),
        out_shape=[jax.ShapeDtypeStruct((4, 2, 2) + BLOCKS[kind], LOW) for kind in KINDS]
        + [
            jax.ShapeDtypeStruct((CHARS, TOKENS, 2 * RECORD), LOW),
            jax.ShapeDtypeStruct((TOKENS, 2 * HID), WIDE),
        ],
        in_specs=[in_vmem] * (count + 2),
        out_specs=[in_vmem if kind in ("CELL", "TABLE") else anywhere for kind in KINDS] + [anywhere, in_vmem],
        scratch_shapes=[
            pltpu.VMEM((CHARS, TOKENS, 2 * RECORD), LOW),
            pltpu.VMEM((TOKENS, 2 * HID), WIDE),
            pltpu.VMEM((2, 8, HID), WIDE),
            pltpu.SemaphoreType.DMA((len(PIECES), 10)),
            pltpu.SemaphoreType.DMA((len(PIECES), 10)),
            pltpu.SemaphoreType.DMA((count,)),
            pltpu.SemaphoreType.DMA((CHARS,)),
        ],
        compiler_params=pltpu.CompilerParams(collective_id=0, has_side_effects=True, vmem_limit_bytes=56 << 20),
    )(*[own[kind] for kind in KINDS], codes, lengths)
    return dict(zip(KINDS, results[:count])), results[count], results[count + 1]


def pack(shards, per_place):
    (attention_in, attention_out, feed_in, feed_bias, feed_out, char_table, cell_input, cell_recurrent, cell_bias,
     stream_weight, merging_kernel, norm_gains, biases) = shards

    def lanes(parts, width):
        together = jnp.concatenate(parts, axis=1)
        return jnp.pad(together, ((0, 0), (0, width - together.shape[1])))

    def flat(stacked):
        return [jnp.transpose(part) for part in stacked]

    rows = attention_out.shape[1]
    thin = lanes(
        [
            lanes([attention_out.T, biases.T, norm_gains.T, feed_bias.reshape(rows, 4)], 1024),
            feed_out.T,
            *flat(stream_weight),
            *flat(merging_kernel),
        ],
        10240,
    )
    middle = lanes([cell_input.T, cell_recurrent.T, cell_bias.T], 768)
    middle = jnp.concatenate([middle, attention_in.T], axis=1)
    parts = [thin, middle, feed_in.T, lanes([char_table.T], 1024)]
    if per_place == 2:
        size = lax.axis_size("wide")
        swap = [(i, i + 1 - 2 * (i % 2)) for i in range(size)]
        first = lax.axis_index("wide") % 2 == 0
        whole = []
        for part in parts:
            other = lax.ppermute(part, "wide", swap)
            whole.append(jnp.concatenate([jnp.where(first, part, other), jnp.where(first, other, part)], axis=0))
    else:
        size = lax.axis_size("wide")
        groups = [list(range(i, i + per_place)) for i in range(0, size, per_place)]
        whole = [lax.all_gather(part, "wide", axis=0, tiled=True, axis_index_groups=groups) for part in parts]
    thin, middle, feed, table = whole
    return {
        "CELL": middle[:, :768],
        "TABLE": table,
        "ATT": middle[:, 768:],
        "OUT": thin[:, :1024],
        "IN": feed,
        "FEED": thin[:, 1024:4096],
        "STREAM": thin[:, 4096:5632],
        "MERGE": thin[:, 5632:],
    }


def gru_backward_step(t, cell, record, state_grad, pool_grad, lengths):
    for way in (0, 1):
        base = way * RECORD
        place = t if way == 0 else CHARS - 1 - t
        live = lengths[...] > place
        lanes = pl.ds(way * HID, HID)

        def saved(at):
            return record[t, :, pl.ds(base + at, HID)].astype(WIDE)

        r, u, n, recur_n, h = saved(GATE_R), saved(GATE_Z), saved(GATE_N), saved(GATE_Q), saved(EMB)
        grad = state_grad[:, lanes]
        fresh = jnp.where(live, grad + pool_grad[:, lanes], 0.0)
        kept = jnp.where(live, 0.0, grad)
        grad_n = fresh * (1.0 - u) * (1.0 - n * n)
        grad_z = fresh * (h - n) * u * (1.0 - u)
        grad_r = grad_n * recur_n * r * (1.0 - r)
        low_r, low_z, low_n, low_q = (v.astype(LOW) for v in (grad_r, grad_z, grad_n, grad_n * r))
        record[t, :, pl.ds(base + GATE_R, HID)] = low_r
        record[t, :, pl.ds(base + GATE_Z, HID)] = low_z
        record[t, :, pl.ds(base + GATE_N, HID)] = low_n
        record[t, :, pl.ds(base + GATE_Q, HID)] = low_q
        weights = cell[pl.ds(2 * way, 2)].reshape(3 * HID, X_WIDTH)[:, EMB : EMB + HID]
        gates = jnp.concatenate([low_r, low_z, low_q], axis=1)
        state_grad[:, lanes] = kept + fresh * u + dot_plain(gates, weights)


def cell_gradient(way, record, result):
    base = way * RECORD
    rows = CHARS * TOKENS

    def every(at, width):
        return record[:, :, pl.ds(base + at, width)].reshape(rows, width)

    x = every(0, X_WIDTH)
    for gate, at in ((0, GATE_R), (1, GATE_Z)):
        result[pl.ds((3 * way + gate) * HID, HID)] = dot_first(every(at, HID), x).astype(LOW)
    drive, recur = dot_first(every(GATE_N, HID), x), dot_first(every(GATE_Q, HID), x)
    lane = lax.broadcasted_iota(jnp.int32, (HID, X_WIDTH), 1)
    result[pl.ds((3 * way + 2) * HID, HID)] = jnp.where(
        (lane < EMB) | (lane == EMB + HID), drive, recur
    ).astype(LOW)


def table_gradient(c, cell, record, codes, result):
    drive = jnp.zeros((TOKENS, EMB), WIDE)
    for way, t in ((0, c), (1, CHARS - 1 - c)):
        gates = record[t, :, pl.ds(way * RECORD + GATE_R, 3 * HID)]
        drive += dot_plain(gates, cell[pl.ds(2 * way, 2)].reshape(3 * HID, X_WIDTH)[:, :EMB])
    result[...] += dot_first(drive.astype(LOW), one_hot(codes, c, 1024))


def layer_norm(inputs, gain_row, shift_row):
    centred = inputs - jnp.mean(inputs, axis=-1, keepdims=True)
    spread = jnp.mean(centred * centred, axis=-1, keepdims=True)
    return centred * lax.rsqrt(spread + norm_eps) * gain_row + shift_row


def gelu_exact(inputs):
    return jax.nn.gelu(inputs, approximate=False)


def dense(whole, hidden, sequence_length, cotangent, pooled):
    w = {kind: part.reshape(-1, part.shape[-1]) for kind, part in whole.items()}
    small = w["OUT"][:, 768:785]
    small_rows = jnp.transpose(small[:, :13]).astype(WIDE)
    biases, gains = small_rows[:10], small_rows[10:]
    feed_bias = small[:, 13:].reshape(-1).astype(WIDE)
    length, width = hidden.shape
    head = width // HEADS
    scale = head ** (-0.5)
    joint_bias = jnp.concatenate([biases[0], jnp.zeros_like(biases[0]), biases[1]])
    projected = (dot_second(hidden, w["ATT"]) + joint_bias).astype(LOW)
    projected = projected.reshape(length, 3, HEADS, head)
    queries, keys, values = projected[:, 0], projected[:, 1], projected[:, 2]
    mask = jnp.where(jnp.arange(length) < sequence_length[0], 0.0, masked_score).astype(WIDE)
    scores = jnp.einsum("qhd,khd->hqk", queries, keys, preferred_element_type=WIDE) * scale + mask
    weight = jnp.exp(scores - jnp.max(scores, axis=-1, keepdims=True))
    soft = weight / jnp.sum(weight, axis=-1, keepdims=True)
    soft_low = soft.astype(LOW)
    context = jnp.einsum("hqk,khd->qhd", soft_low, values, preferred_element_type=WIDE)
    context = context.astype(LOW).reshape(length, width)
    one_sum = hidden.astype(WIDE) + dot_second(context, w["OUT"][:, :768]) + biases[2]
    first = layer_norm(one_sum, gains[0], biases[3])
    first_low = first.astype(LOW)
    inner = dot_second(first_low, w["IN"]) + feed_bias
    active = gelu_exact(inner).astype(LOW)
    two_sum = first + dot_second(active, w["FEED"]) + biases[4]
    second = layer_norm(two_sum, gains[1], biases[5])
    second_low = second.astype(LOW)
    pooled_low = pooled.astype(LOW)
    token_side = dot_second(second_low, w["STREAM"][:, :768]) + biases[6]
    char_side = dot_second(pooled_low, w["STREAM"][:, 768:]) + biases[7]
    joined = jnp.concatenate([token_side, char_side], axis=-1).astype(LOW)
    padded = jnp.pad(joined, ((1, 1), (0, 0)))
    windows = jnp.concatenate([padded[:-2], padded[1:-1], padded[2:]], axis=-1)
    third_sum = second + dot_second(windows, w["MERGE"]) + biases[8]
    output = layer_norm(third_sum, gains[2], biases[9]).astype(LOW)

    _, pull_three = jax.vjp(layer_norm, third_sum, gains[2], biases[9])
    merged_grad, gain_three, shift_three = pull_three(cotangent.astype(WIDE))
    merged_low = merged_grad.astype(LOW)
    grads = {"MERGE": dot_first(merged_low, windows)}
    window_grad = dot_plain(merged_low, w["MERGE"]).reshape(length, 3, 2 * width)
    joined_grad = (
        window_grad[:, 1]
        + jnp.pad(window_grad[1:, 0], ((0, 1), (0, 0)))
        + jnp.pad(window_grad[:-1, 2], ((1, 0), (0, 0)))
    )
    token_grad, char_grad = joined_grad[:, :width], joined_grad[:, width:]
    token_low, char_low = token_grad.astype(LOW), char_grad.astype(LOW)
    grads["STREAM"] = jnp.concatenate([dot_first(token_low, second_low), dot_first(char_low, pooled_low)], axis=1)
    pooled_grad = dot_plain(char_low, w["STREAM"][:, 768:])
    second_grad = merged_grad + dot_plain(token_low, w["STREAM"][:, :768])
    _, pull_two = jax.vjp(layer_norm, two_sum, gains[1], biases[5])
    two_grad, gain_two, shift_two = pull_two(second_grad)
    two_low = two_grad.astype(LOW)
    grads["FEED"] = dot_first(two_low, active)
    _, pull_gelu = jax.vjp(gelu_exact, inner)
    (inner_grad,) = pull_gelu(dot_plain(two_low, w["FEED"]))
    inner_low = inner_grad.astype(LOW)
    grads["IN"] = dot_first(inner_low, first_low)
    first_grad = two_grad + dot_plain(inner_low, w["IN"])
    _, pull_one = jax.vjp(layer_norm, one_sum, gains[0], biases[3])
    one_grad, gain_one, shift_one = pull_one(first_grad)
    one_low = one_grad.astype(LOW)
    grad_out = dot_first(one_low, context)
    context_grad = dot_plain(one_low, w["OUT"][:, :768]).astype(LOW).reshape(length, HEADS, head)
    soft_grad = jnp.einsum("qhd,khd->hqk", context_grad, values, preferred_element_type=WIDE)
    value_grad = jnp.einsum("hqk,qhd->khd", soft_low, context_grad, preferred_element_type=WIDE)
    score_grad = soft * (soft_grad - jnp.sum(soft * soft_grad, axis=-1, keepdims=True))
    score_low = score_grad.astype(LOW)
    query_grad = jnp.einsum("hqk,khd->qhd", score_low, keys, preferred_element_type=WIDE) * scale
    key_grad = jnp.einsum("hqk,qhd->khd", score_low, queries, preferred_element_type=WIDE) * scale
    projected_low = jnp.stack([query_grad, key_grad, value_grad], axis=1).reshape(length, 3 * width).astype(LOW)
    grads["ATT"] = dot_first(projected_low, hidden)
    hidden_grad = (one_grad + dot_plain(projected_low, w["ATT"])).astype(LOW)
    small_grads = jnp.stack(
        [
            jnp.sum(query_grad, axis=0).reshape(width),
            jnp.sum(value_grad, axis=0).reshape(width),
            jnp.sum(one_grad, axis=0),
            shift_one,
            jnp.sum(two_grad, axis=0),
            shift_two,
            jnp.sum(token_grad, axis=0),
            jnp.sum(char_grad, axis=0),
            jnp.sum(merged_grad, axis=0),
            shift_three,
            gain_one,
            gain_two,
            gain_three,
        ]
    )
    feed_bias_grad = jnp.sum(inner_grad, axis=0).reshape(width, 4)
    grads["OUT"] = jnp.pad(
        jnp.concatenate([grad_out, jnp.transpose(small_grads), feed_bias_grad], axis=1), ((0, 0), (0, 256 - 17))
    )
    grads = {
        kind: part.astype(LOW).reshape((4, 2, 2) + BLOCKS[kind]) for kind, part in grads.items()
    }
    return output, hidden_grad, pooled_grad, grads


def backward_kernel(record_in, cell, table, codes, lengths, pool_grad, cell_grad, table_grad, record, state_grad, total, record_sem):
    copy = pltpu.make_async_copy(record_in, record, record_sem)
    copy.start()
    copy.wait()
    state_grad[...] = jnp.zeros_like(state_grad)

    def retreat(i, carry):
        gru_backward_step(CHARS - 1 - i, cell, record, state_grad, pool_grad, lengths)
        return carry

    lax.fori_loop(0, CHARS, retreat, 0)
    for way in (0, 1):
        cell_gradient(way, record, cell_grad)
    total[...] = jnp.zeros_like(total)

    def look_up(c, carry):
        table_gradient(c, cell, record, codes, total)
        return carry

    lax.fori_loop(0, CHARS, look_up, 0)
    table_grad[...] = total[...].astype(LOW)


def gru_backward(record, cell, table, codes, lengths, pool_grad):
    in_vmem = pl.BlockSpec(memory_space=pltpu.VMEM)
    return pl.pallas_call(
        backward_kernel,
        out_shape=[jax.ShapeDtypeStruct((6 * HID, X_WIDTH), LOW), jax.ShapeDtypeStruct((EMB, 1024), LOW)],
        in_specs=[pl.BlockSpec(memory_space=pl.ANY)] + [in_vmem] * 5,
        out_specs=[in_vmem] * 2,
        scratch_shapes=[
            pltpu.VMEM((CHARS, TOKENS, 2 * RECORD), LOW),
            pltpu.VMEM((TOKENS, 2 * HID), WIDE),
            pltpu.VMEM((EMB, 1024), WIDE),
            pltpu.SemaphoreType.DMA,
        ],
        compiler_params=pltpu.CompilerParams(vmem_limit_bytes=56 << 20),
    )(record, cell, table, codes, lengths, pool_grad)


def unpack(final):
    part = {kind: value.reshape(-1, value.shape[-1]).astype(WIDE) for kind, value in final.items()}
    cell, table, out, stream, merge = (part[kind] for kind in ("CELL", "TABLE", "OUT", "STREAM", "MERGE"))
    small = out[:, 768:785]
    return (
        part["ATT"].T,
        out[:, :768].T,
        part["IN"].T,
        small[:, 13:].reshape(-1),
        part["FEED"].T,
        table[:, :1000].T,
        cell[:, :EMB].T,
        cell[:, EMB : EMB + HID].T,
        cell[:, EMB + HID : EMB + HID + 2].T,
        jnp.stack([stream[:, :768].T, stream[:, 768:].T]),
        jnp.stack([merge[:, k * 1536 : (k + 1) * 1536].T for k in range(3)]),
        small[:, 10:13].T,
        small[:, :10].T,
    )


def shards(hidden, char_codes, word_length, sequence_length, cotangent, *parameters):
    wide = lax.axis_size("wide")
    per_place = wide // 2
    own = pack(parameters, per_place)
    codes = jnp.transpose(char_codes)[:, :, None]
    lengths = word_length[:, None]
    whole, record, pooled = gather_and_read(own, codes, lengths, per_place)
    output, hidden_grad, pooled_grad, grads = dense(whole, hidden, sequence_length, cotangent, pooled)
    pool_grad = pooled_grad / lengths.astype(WIDE)
    cell_grad, table_grad = gru_backward(record, whole["CELL"], whole["TABLE"], codes, lengths, pool_grad)
    grads["CELL"] = cell_grad.reshape((4, 2, 2) + BLOCKS["CELL"])
    grads["TABLE"] = table_grad.reshape((4, 2, 2) + BLOCKS["TABLE"])
    final = {}
    for kind, part in grads.items():
        part = part.reshape((8, 2) + part.shape[3:])
        part = lax.psum_scatter(part, "grp", scatter_dimension=0, tiled=True)
        final[kind] = lax.psum(part, "wide")
    return (output, hidden_grad, *unpack(final))


def solution(mesh):
    rows = P(("grp", "wide"), None)
    flat = P(("grp", "wide"))
    last = P(None, ("grp", "wide"))
    deep = P(None, None, ("grp", "wide"))
    in_specs = (rows, rows, flat, flat, rows, last, last, last, flat, last, last, last, last, last, deep, deep, last, last)
    out_specs = (rows, rows) + (P(None, "grp"),) * 3 + (P("grp"),) + (P(None, "grp"),) * 5 + (P(None, None, "grp"),) * 2 + (P(None, "grp"),) * 2
    return jax.shard_map(shards, mesh=mesh, in_specs=in_specs, out_specs=out_specs, check_vma=False)
```

time: 2490 us -> 1110 us (0.45)
  waiting for transfers between devices: 1350 us -> 720 us
  blocking collectives: 257 us -> 0 us
  local copies, waits for them, and re-layouts: 281 us -> 61.8 us
  Pallas kernels: 0 us -> 212 us
  other arithmetic: 223 us -> 26.1 us
  matrix products: 203 us -> 65.2 us
  loops' own time: 137 us -> 0 us
    all_gather x16 -> x0, waiting for transfers between devices: 411 us -> none  [the longest x1 69.3 us: shards(): lax.all_gather(shards_late[10], ('grp', 'wide'), axis=2, tiled=True)]
    unnamed x37 -> x9, waiting for transfers between devices: 393 us -> 0.65 us
    pallas_call x0 -> x2, Pallas kernels: none -> 212 us  [the longest x1 157 us: gather_and_read(): pl.pallas_call(partial(forward_kernel, per_place), out_shape=[jax.ShapeDt...]
    all_gather x5 -> x0, blocking collectives: 199 us -> none  [the longest x1 43.9 us: shards(): lax.all_gather(biases, ('grp', 'wide'), axis=1, tiled=True)]
    reduce_scatter x5 -> x8, waiting for transfers between devices: 446 us -> 645 us  [shards(): part = lax.psum_scatter(part, 'grp', scatter_dimension=0, tiled=True)]
    another operation x2 -> x0, loops' own time: 137 us -> none  [the longest x1 71.5 us: backward(): lax.scan(retreat, (zero_state, zero_state, zero_bias, zero_bias), jnp.ara...]
    squeeze x82 -> x1, local copies, waits for them, and re-layouts: 117 us -> 0.11 us  [dense(): window_grad[1:, 0]]
    mul x80 -> x0, other arithmetic: 74.4 us -> none  [the longest x40 46.7 us: gate_cell(): jax.nn.sigmoid(drive_in[:, hidden_units:2 * hidden_units] + recurrent[:,...]
  transfers between devices with their start and end apart: 30 -> 13, of which waited for: 20 -> 9; matrix products, arithmetic and copies ran while one was open for 27% -> 6% of each run, Pallas kernels for 0% -> 0%
where the time goes in v1:
time: 1110 us; the launch traced here: 1100 us
  waiting for transfers between devices  720 us (65%)
  Pallas kernels  212 us (19%)
  matrix products  65.2 us (6%)
  local copies, waits for them, and re-layouts  61.8 us (6%)
  other arithmetic  26.1 us (2%)
  between operations  15.7 us (1%)
    reduce_scatter x8, waiting for transfers between devices, shards(): part = lax.psum_scatter(part, 'grp', scatter_dimension=0, tiled=True)  645 us
    pallas_call x1, Pallas kernels, gather_and_read(): pl.pallas_call(partial(forward_kernel, per_place), out_shape=[jax.ShapeDt...  157 us
    psum x1, waiting for transfers between devices, shards(): final[kind] = lax.psum(part, 'wide')  73.8 us
    pallas_call x1, Pallas kernels, gru_backward(): pl.pallas_call(backward_kernel, out_shape=[jax.ShapeDtypeStruct((6 * HID,...  55.7 us
  transfers between devices with their start and end apart: 13, of which 9 were waited for; matrix products, arithmetic and copies ran while one was open for 6% of the time, Pallas kernels for 0%

profile of v1, /device:TPU:0, one launch (start us, length us, event | category | flops | bytes accessed | tf_op | source)
XLA Modules:
  0.0 1102.4 jit_solution(7111133767362927685)
XLA Ops:
  20.7 1.6 copy.53.refs_8_.codes
  29.4 156.6 %shard_map.289 = (bf16[4,2,2,144,768]{4,3,2,1,0:T(8,128)(2,1)}, bf16[4,2,2,16,1024]{4,3,2,1,0:T(8,128)(2,1)}, bf16[4,2,2,144,768]{4,3,2,1,0:T(8,128)(2,1)}, bf16...) custom-call(bf16[144,768]{1,0:T(8,128)(2,1)} %get-tuple-element.118., ...), custom_call_target="tpu_custom_call" | custom-call | tf_op jit(solution)/shard_map/pallas_call | solution.py:297
  188.5 3.1 fusion.1
  191.6 1.3 fusion.77
  193.6 2.0 fusion.78
  196.4 8.6 multiply_convert_fusion
  205.0 1.8 fusion.79
  208.4 2.4 fusion.80
  211.9 10.5 copy.57
  223.3 5.6 fusion.42
  229.3 1.4 copy-done.5
  232.9 2.3 fusion.81
  235.2 1.5 multiply_reduce_fusion.2
  238.7 1.7 copy.58
  240.4 1.7 multiply_reduce_fusion
  243.1 2.4 bitcast_reduce_fusion.1
  245.5 1.8 reshape.243
  247.3 1.6 copy.62
  248.9 1.3 stack_reshape.8
  250.3 2.4 convolution_divide_fusion.pool_grad
  252.6 55.7 %shard_map.290 = (bf16[2304,768]{1,0:T(8,128)(2,1)}, bf16[256,1024]{1,0:T(8,128)(2,1)}) custom-call(bf16[20,128,4608]{2,1,0:T(8,128)(2,1)} %get-tuple-element.34.record_in, bf16[4,2,2,144,768]{4,3,2,1,0:T(8,128)(2,1)} %get-tuple-element.35.cell, bf16[4,2,2,16,1024]{4,3,2,1,0:T(8,128)(2,1)} %get-tuple-element.36.table, s32[20,128,1]{2,1,0:T(8,128)} %copy.53.refs_8_.codes, ...), custom_call_target="tpu_custom_call" | custom-call | tf_op jit(solution)/shard_map/pallas_call | solution.py:558
  308.6 3.0 bitcast_reduce_fusion
  311.7 1.3 stack_reshape.9
  314.4 1.3 reshape.237
  317.0 1.3 reshape.238
  322.0 2.7 stack.78
  324.7 1.5 convolution_convert_fusion.4
  327.3 2.5 copy.75
  329.8 2.7 pad.35.clone
  332.6 1.5 convolution_convert_fusion.5
  334.7 1.7 pad_maximum_fusion
  337.4 1.3 fusion.12
  339.7 2.8 convolution_convert_fusion.3
  343.3 3.7 convolution_convert_fusion.2
  348.2 3.6 convolution_convert_fusion.1
  353.1 5.0 convolution_convert_fusion
  358.1 11.4 %reduce-scatter.17.cloned.1.call-done = bf16[1,2,16,1024]{3,2,1,0:T(8,128)(2,1)} async-done(((bf16[8,2,16,1024]{3,2,1,0:T(8,128)(2,1)}), bf16[1,2,16,1024]{3,2,1,0:T(8,128)(2,1)}) %reduce-scatter.17.cloned.1.call-update) | async-done | bytes 65552 | tf_op jit(solution)/shard_map/reduce_scatter | solution.py:609
  369.6 68.3 %reduce-scatter.11.cloned.1.call-done = bf16[1,2,48,1024]{3,2,1,0:T(8,128)(2,1)} async-done(((bf16[8,2,48,1024]{3,2,1,0:T(8,128)(2,1)}), bf16[1,2,48,1024]{3,2,1,0:T(8,128)(2,1)}) %reduce-scatter.11.cloned.1.call-update) | async-done | bytes 196624 | tf_op jit(solution)/shard_map/reduce_scatter | solution.py:609
  437.8 71.4 %reduce-scatter.21.cloned.1.call-done = bf16[1,2,48,1536]{3,2,1,0:T(8,128)(2,1)} async-done(((bf16[8,2,48,1536]{3,2,1,0:T(8,128)(2,1)}), bf16[1,2,48,1536]{3,2,1,0:T(8,128)(2,1)}) %reduce-scatter.21.cloned.1.call-update) | async-done | bytes 294928 | tf_op jit(solution)/shard_map/reduce_scatter | solution.py:609
  509.3 81.7 %reduce-scatter.9.cloned.1.call-done = bf16[1,2,144,768]{3,2,1,0:T(8,128)(2,1)} async-done(((bf16[8,2,144,768]{3,2,1,0:T(8,128)(2,1)}), bf16[1,2,144,768]{3,2,1,0:T(8,128)(2,1)}) %reduce-scatter.9.cloned.1.call-update) | async-done | bytes 442384 | tf_op jit(solution)/shard_map/reduce_scatter | solution.py:609
  591.0 82.2 %reduce-scatter.19.cloned.1.call-done = bf16[1,2,144,768]{3,2,1,0:T(8,128)(2,1)} async-done(((bf16[8,2,144,768]{3,2,1,0:T(8,128)(2,1)}), bf16[1,2,144,768]{3,2,1,0:T(8,128)(2,1)}) %reduce-scatter.19.cloned.1.call-update) | async-done | bytes 442384 | tf_op jit(solution)/shard_map/reduce_scatter | solution.py:609
  673.2 98.5 %reduce-scatter.13.cloned.1.call-done = bf16[1,2,192,768]{3,2,1,0:T(8,128)(2,1)} async-done(((bf16[8,2,192,768]{3,2,1,0:T(8,128)(2,1)}), bf16[1,2,192,768]{3,2,1,0:T(8,128)(2,1)}) %reduce-scatter.13.cloned.1.call-update) | async-done | bytes 589840 | tf_op jit(solution)/shard_map/reduce_scatter | solution.py:609
  771.8 98.7 %reduce-scatter.15.cloned.1.call-done = bf16[1,2,48,3072]{3,2,1,0:T(8,128)(2,1)} async-done(((bf16[8,2,48,3072]{3,2,1,0:T(8,128)(2,1)}), bf16[1,2,48,3072]{3,2,1,0:T(8,128)(2,1)}) %reduce-scatter.15.cloned.1.call-update) | async-done | bytes 589840 | tf_op jit(solution)/shard_map/reduce_scatter | solution.py:609
  870.5 132.9 %reduce-scatter.23.cloned.1.call-done = bf16[1,2,48,4608]{3,2,1,0:T(8,128)(2,1)} async-done(((bf16[8,2,48,4608]{3,2,1,0:T(8,128)(2,1)}), bf16[1,2,48,4608]{3,2,1,0:T(8,128)(2,1)}) %reduce-scatter.23.cloned.1.call-update) | async-done | bytes 884752 | tf_op jit(solution)/shard_map/reduce_scatter | solution.py:609
  1004.0 3.4 fusion.17
  1007.4 73.8 %all-reduce.10.cloned.1.call-done = (bf16[768,384]{0,1:T(8,128)(2,1)}, bf16[768,288]{0,1:T(8,128)(2,1)}, bf16[96,1024]{1,0:T(8,128)(2,1)}, bf16[3072,96]{0,1:T(8...) async-done(((bf16[768,384]{0,1:T(8,128)(2,1)}, bf16[768,288]{0,1:T(8,128)(2,1)}, ...) | async-done | bytes 3506192 | tf_op jit(solution)/shard_map/psum | solution.py:610
  1087.4 1.3 copy.66
  1094.4 1.3 pad_maximum_fusion.1
  (274 shorter events, 58.3 us)
Async XLA Ops:
  7.2 12.8 %copy-start.28 = (bf16[768,96]{0,1:T(8,128)(2,1)S(1)}, bf16[768,96]{0,1:T(8,128)(2,1)}, u32[]{:S(2)}) copy-start(bf16[768,96]{0,1:T(8,128)(2,1)} %param.25) | copy-start | bytes 442372
  7.2 13.5 %copy-start.40 = (s32[128,20]{0,1:T(8,128)S(1)}, s32[128,20]{0,1:T(8,128)}, u32[]{:S(2)}) copy-start(s32[128,20]{0,1:T(8,128)} %param.19) | copy-start | bytes 30724
  7.2 15.1 %copy-start.57 = (s32[128]{0:T(128)S(1)}, s32[128]{0:T(128)}, u32[]{:S(2)}) copy-start(s32[128]{0:T(128)} %param.20) | copy-start | bytes 1540
  7.2 362.3 %reduce-scatter.17.cloned.1.call-start = ((), (), s32[]{:S(2)}) async-start(), calls=%async_computation.12 | async-start | bytes 589824 | tf_op jit(solution)/shard_map/reduce_scatter | solution.py:609
  8.0 15.5 %copy-start.6 = (bf16[128,768]{1,0:T(8,128)(2,1)S(1)}, bf16[128,768]{1,0:T(8,128)(2,1)}, u32[]{:S(2)}) copy-start(bf16[128,768]{1,0:T(8,128)(2,1)} %param.22) | copy-start | bytes 589828
  8.9 15.3 %copy-start.32 = (bf16[1000,8]{0,1:T(8,128)(2,1)S(1)}, bf16[1000,8]{0,1:T(8,128)(2,1)}, u32[]{:S(2)}) copy-start(bf16[1000,8]{0,1:T(8,128)(2,1)} %param.28) | copy-start | bytes 48004
  9.9 15.8 %collective-permute-start = (bf16[72,1536]{1,0:T(8,128)(2,1)S(1)}, bf16[72,1536]{1,0:T(8,128)(2,1)S(1)}, u32[]{:S(2)}, u32[]{:S(2)}) collective-permute-start(bf16[72,1536]{1,0:T(8,128)(2,1)S(1)} %pad_maximum_fusion.9), channel_id=1, source_target_pairs={{0,1},{1,0},{2,3},{3,2},{4,5},{5,4},{6,7},{7,6},{8,9},{9,8},{10,11... | collective-permute-start | bytes 663560 | tf_op jit(solution)/shard_map/ppermute | solution.py:350
  11.1 13.1 %collective-permute-start.1 = (bf16[8,1024]{1,0:T(8,128)(2,1)S(1)}, bf16[8,1024]{1,0:T(8,128)(2,1)S(1)}, u32[]{:S(2)}, u32[]{:S(2)}) collective-permute-start(bf16[8,1024]{1,0:T(8,128)(2,1)S(1)} %pad.30), channel_id=1, source_target_pairs={{0,1},{1,0},{2,3},{3,2},{4,5},{5,4},{6,7},{7,6},{8,9},{9,8},{10,11... | collective-permute-start | bytes 49160 | tf_op jit(solution)/shard_map/ppermute | solution.py:350
  18.6 7.1 copy-start.21
  19.5 7.0 collective-permute-start.2
  19.9 4.9 collective-permute-start.3
  20.7 172.3 %copy-start.60 = (f32[128]{0:T(128)}, f32[128]{0:T(128)S(1)}, u32[]{:S(2)}) copy-start(f32[128]{0:T(128)S(1)} %compare_select_fusion) | copy-start | bytes 1540
  186.0 2.5 copy-start.25
  193.6 11.4 %slice-start.4 = ((s8[4718592]{0:T(1024)(128)(4,1)}), s8[4194304]{0:T(1024)(128)(4,1)S(1)}, s32[]{:S(2)}) async-start(s8[4718592]{0:T(1024)(128)(4,1)} %bitcast.227), calls=%async_computation.21 | async-start | bytes 8388608
  193.6 14.8 %slice-start = ((s8[7077888]{0:T(1024)(128)(4,1)}), s8[4194304]{0:T(1024)(128)(4,1)S(1)}, s32[]{:S(2)}) async-start(s8[7077888]{0:T(1024)(128)(4,1)} %bitcast.217), calls=%async_computation.17 | async-start | bytes 8388608
  195.7 9.3 copy-start.34
  195.9 9.1 copy-start.43
  196.4 8.6 slice-start.5
  196.4 12.0 %slice-start.1 = ((s8[7077888]{0:T(1024)(128)(4,1)}), s8[2883584]{0:T(1024)(128)(4,1)S(1)}, s32[]{:S(2)}) async-start(s8[7077888]{0:T(1024)(128)(4,1)} %bitcast.217), calls=%async_computation.18 | async-start | bytes 5767168
  206.8 22.4 %copy-start.46 = (f32[128]{0:T(128)}, f32[128]{0:T(128)S(1)}, u32[]{:S(2)}) copy-start(f32[128]{0:T(128)S(1)} %broadcast_multiply_fusion.1) | copy-start | bytes 1540
  207.0 22.2 %copy-start.53 = (f32[128]{0:T(128)}, f32[128]{0:T(128)S(1)}, u32[]{:S(2)}) copy-start(f32[128]{0:T(128)S(1)} %fusion.61) | copy-start | bytes 1540
  208.1 2.7 copy-start.17
  208.4 2.5 copy-start.9
  208.4 2.5 copy-start.11
  223.3 6.0 copy-start.37
  223.3 9.5 slice-start.6
  228.9 4.0 slice-start.7
  229.0 3.8 copy-start.61
  229.0 3.8 copy-start.62
  230.7 4.5 slice-start.2
  235.2 2.4 copy-start.30
  308.4 129.4 %reduce-scatter.11.cloned.1.call-start = ((), (), s32[]{:S(2)}) async-start(), calls=%async_computation.9 | async-start | bytes 1769472 | tf_op jit(solution)/shard_map/reduce_scatter | solution.py:609
  313.0 6.5 copy-start.38
  313.0 7.2 copy-start.52
  313.0 7.8 copy-start.51
  313.0 8.4 copy-start.50
  332.5 176.7 %reduce-scatter.21.cloned.1.call-start = ((), (), s32[]{:S(2)}) async-start(), calls=%async_computation.14 | async-start | bytes 2654208 | tf_op jit(solution)/shard_map/reduce_scatter | solution.py:609
  336.4 254.6 %reduce-scatter.9.cloned.1.call-start = ((), (), s32[]{:S(2)}) async-start(), calls=%async_computation.8 | async-start | bytes 3981312 | tf_op jit(solution)/shard_map/reduce_scatter | solution.py:609
  342.6 330.6 %reduce-scatter.19.cloned.1.call-start = ((), (), s32[]{:S(2)}) async-start(), calls=%async_computation.13 | async-start | bytes 3981312 | tf_op jit(solution)/shard_map/reduce_scatter | solution.py:609
  343.2 428.6 %reduce-scatter.13.cloned.1.call-start = ((), (), s32[]{:S(2)}) async-start(), calls=%async_computation.10 | async-start | bytes 5308416 | tf_op jit(solution)/shard_map/reduce_scatter | solution.py:609
  347.1 523.4 %reduce-scatter.15.cloned.1.call-start = ((), (), s32[]{:S(2)}) async-start(), calls=%async_computation.11 | async-start | bytes 5308416 | tf_op jit(solution)/shard_map/reduce_scatter | solution.py:609
  351.8 651.5 %reduce-scatter.23.cloned.1.call-start = ((), (), s32[]{:S(2)}) async-start(), calls=%async_computation.15 | async-start | bytes 7962624 | tf_op jit(solution)/shard_map/reduce_scatter | solution.py:609
  358.1 723.1 %all-reduce.10.cloned.1.call-start = ((), (), s32[]{:S(2)}) async-start(), calls=%async_computation.16 | async-start | bytes 7012352 | tf_op jit(solution)/shard_map/psum | solution.py:610
  1084.0 2.4 copy-start.22
  1084.8 2.6 copy-start.20
  1086.4 2.9 copy-start.19
  1087.4 3.1 copy-start.31
  1087.4 4.4 copy-start.23
  (36 other events, 52.6 us)
Sparse Core Ops, SparseCore 0:
  308.5 60.9 reduce-scatter.16
  373.9 63.8 reduce-scatter.10
  441.3 67.8 reduce-scatter.20
  512.7 78.2 reduce-scatter.8
  594.5 78.7 reduce-scatter.18
  676.7 94.9 reduce-scatter.12
  775.4 95.0 reduce-scatter.14
  874.2 129.1 reduce-scatter.22
  1006.5 74.6 all-reduce.9

commit v2 on v1

--- a/solution.py
+++ b/solution.py
@@ -401,13 +401,11 @@
         return record[:, :, pl.ds(base + at, width)].reshape(rows, width)
 
     x = every(0, X_WIDTH)
-    for gate, at in ((0, GATE_R), (1, GATE_Z)):
-        result[pl.ds((3 * way + gate) * HID, HID)] = dot_first(every(at, HID), x).astype(LOW)
+    parts = [dot_first(every(at, HID), x).astype(LOW) for at in (GATE_R, GATE_Z)]
     drive, recur = dot_first(every(GATE_N, HID), x), dot_first(every(GATE_Q, HID), x)
     lane = lax.broadcasted_iota(jnp.int32, (HID, X_WIDTH), 1)
-    result[pl.ds((3 * way + 2) * HID, HID)] = jnp.where(
-        (lane < EMB) | (lane == EMB + HID), drive, recur
-    ).astype(LOW)
+    parts.append(jnp.where((lane < EMB) | (lane == EMB + HID), drive, recur).astype(LOW))
+    result[...] = jnp.concatenate(parts, axis=0).reshape(result.shape)
 
 
 def table_gradient(c, cell, record, codes, result):
@@ -415,7 +413,360 @@
     for way, t in ((0, c), (1, CHARS - 1 - c)):
         gates = record[t, :, pl.ds(way * RECORD + GATE_R, 3 * HID)]
         drive += dot_plain(gates, cell[pl.ds(2 * way, 2)].reshape(3 * HID, X_WIDTH)[:, :EMB])
-    result[...] += dot_first(drive.astype(LOW), one_hot(codes, c, 1024))
+    which = (lax.broadcasted_iota(jnp.int32, (1024, TOKENS), 0) == codes[pl.ds(c, 1)]).astype(LOW)
+    result[...] += dot_plain(which, drive.astype(LOW))
+
+
+ROWS, LANES = 48, 768
+PARTS = (
+    [("MERGE", 0, 48, 0, 768, 768, 0, 0, True)],
+    [("MERGE", 0, 48, 1536, 2304, 768, 0, 0, True)],
+    [("MERGE", 0, 48, 3072, 3840, 768, 0, 0, True)],
+    [("STREAM", 0, 48, 0, 768, 768, 0, 0, True)],
+    [("FEED", 0, 48, 0, 768, 768, 0, 0, True)],
+    [("FEED", 0, 48, 1536, 2304, 768, 0, 0, True)],
+    [("IN", 0, 48, 0, 384, 384, 0, 0, True), ("IN", 48, 48, 0, 384, 384, 0, 384, True)],
+    [("IN", 96, 48, 0, 384, 384, 0, 0, True), ("IN", 144, 48, 0, 384, 384, 0, 384, True)],
+    [("ATT", 0, 48, 0, 384, 384, 0, 0, True), ("ATT", 48, 48, 0, 384, 384, 0, 384, True)],
+    [("ATT", 96, 48, 0, 384, 384, 0, 0, True), ("OUT", 0, 48, 0, 512, 384, 0, 384, True)],
+    [("CELL", 0, 48, 0, 384, 384, 0, 0, True), ("CELL", 48, 48, 0, 384, 384, 0, 384, True)],
+    [
+        ("CELL", 96, 48, 0, 384, 384, 0, 0, True),
+        ("OUT", 0, 48, 384, 896, 128, 0, 384, True),
+        ("TABLE", 0, 16, 0, 512, 256, 0, 512, True),
+        ("TABLE", 0, 16, 256, 768, 256, 16, 512, True),
+        ("TABLE", 0, 16, 256, 768, 256, 32, 512, False),
+    ],
+)
+SLOTS = 7
+SUBS = 5
+DENSE_PARTS = 10
+AT_FIRST, AT_HOP, AT_NEXT, AT_LAST, AT_RESULT = SUBS, SUBS, SUBS + 4, SUBS + 5, SUBS + 6
+MOVES = 2 * SUBS + 6
+
+
+class Reduce:
+    def __init__(self, spot, grads, landing, buffers, result, sems):
+        self.spot, self.grads, self.landing, self.result = spot, grads, landing, result
+        self.sums, self.other, self.one_in, self.next_in, self.final = buffers
+        self.sent, self.got, self.load_sem, self.keep_sem, self.free = sems
+
+    def move(self, source, target, p, j, device):
+        return remote(source, target, self.sent.at[p, j], self.got.at[p, j], device)
+
+    def outside(self, ref, sub, core):
+        _, row, rows, first, second, width, _, _, _ = sub
+        return ref.at[..., pl.ds(row, rows), pl.ds((first, second)[core], width)]
+
+    def inside(self, ref, sub):
+        _, _, rows, _, _, width, row, lane, _ = sub
+        return ref.at[..., pl.ds(row, rows), pl.ds(lane, width)]
+
+    def given(self, core, p):
+        return [
+            self.move(
+                self.outside(self.grads[sub[0]], sub, 1 - core), self.inside(self.landing.at[p], sub), p, i, self.spot.sibling
+            )
+            for i, sub in enumerate(PARTS[p])
+        ]
+
+    def loads(self, core, p):
+        own = [
+            pltpu.make_async_copy(
+                self.outside(self.grads[sub[0]], sub, core), self.inside(self.sums.at[p % SLOTS], sub), self.load_sem.at[p % 2, i]
+            )
+            for i, sub in enumerate(PARTS[p])
+        ]
+        return own + [pltpu.make_async_copy(self.landing.at[p], self.other.at[p % 2], self.load_sem.at[p % 2, SUBS])]
+
+    def first(self, core, p):
+        s, slot = self.spot, p % SLOTS
+        if core == 0:
+            return self.move(self.sums.at[slot, :, 1 - s.x], self.one_in.at[slot], p, AT_FIRST, s.to_x)
+        return self.move(self.sums.at[slot, :, :, 1 - s.y], self.one_in.at[slot], p, AT_FIRST, s.to_y)
+
+    def hop(self, core, p, k):
+        s, slot = self.spot, p % SLOTS
+        z = (s.z + k) % 4
+        if core == 0:
+            return self.move(self.sums.at[slot, z, s.x], self.next_in.at[slot, pl.ds(2 * k - 2, 2)], p, AT_HOP + k, s.hop(k))
+        return self.move(self.sums.at[slot, z, s.x, s.y], self.next_in.at[slot, 3 + k], p, AT_HOP + k, s.hop(k))
+
+    def next(self, core, p):
+        s, slot = self.spot, p % SLOTS
+        if core == 0:
+            return self.move(self.sums.at[slot, s.z, s.x], self.next_in.at[slot, pl.ds(6, 2)], p, AT_NEXT, s.to_y)
+        return self.move(self.sums.at[slot, :, 1 - s.x, s.y], self.next_in.at[slot, pl.ds(0, 4)], p, AT_NEXT, s.to_x)
+
+    def last(self, p, mine):
+        s, slot = self.spot, p % SLOTS
+        part = self.final.at[slot, s.y if mine else 1 - s.y]
+        return self.move(part, part, p, AT_LAST, s.to_y)
+
+    def results(self, core, p):
+        return [
+            self.move(self.inside(self.final.at[p % SLOTS], sub), self.outside(self.result[sub[0]], sub, core), p, AT_RESULT + i, self.spot.sibling)
+            for i, sub in enumerate(PARTS[p])
+            if sub[-1]
+        ]
+
+    def kept(self, core, p):
+        return [
+            pltpu.make_async_copy(
+                self.inside(self.final.at[p % SLOTS], sub), self.outside(self.result[sub[0]], sub, core), self.keep_sem.at[p, i]
+            )
+            for i, sub in enumerate(PARTS[p])
+            if sub[-1]
+        ]
+
+    def give(self, core, p):
+        for copy in self.given(core, p):
+            copy.start()
+
+    def fetch(self, core, p):
+        for copy in self.given(core, p):
+            copy.wait_recv()
+        for copy in self.loads(core, p):
+            copy.start()
+
+    def stage_one(self, core, p):
+        for copy in self.loads(core, p):
+            copy.wait()
+        slot = p % SLOTS
+
+        def add(i, carry):
+            at = (i // 4, i // 2 % 2, i % 2)
+            self.sums[slot, at[0], at[1], at[2]] += self.other[p % 2, at[0], at[1], at[2]]
+            return carry
+
+        lax.fori_loop(0, 16, add, 0)
+        if p >= SLOTS:
+            for i in range(5):
+                pl.semaphore_wait(self.free.at[i], 1)
+        self.first(core, p).start()
+
+    def stage_two(self, core, p):
+        s, slot = self.spot, p % SLOTS
+        self.first(core, p).wait_recv()
+
+        def add(i, carry):
+            if core == 0:
+                self.sums[slot, i // 2, s.x, i % 2] += self.one_in[slot, i // 2, i % 2]
+            else:
+                self.sums[slot, i // 2, i % 2, s.y] += self.one_in[slot, i // 2, i % 2]
+            return carry
+
+        lax.fori_loop(0, 8, add, 0)
+        if core == 0:
+            for k in (1, 3, 2):
+                self.hop(core, p, k).start()
+        else:
+            self.next(core, p).start()
+
+    def stage_three(self, core, p):
+        s, slot = self.spot, p % SLOTS
+        if core == 0:
+            for k in (1, 3, 2):
+                self.hop(core, p, k).wait_recv()
+
+            def add(i, carry):
+                total = self.sums[slot, s.z, s.x, i].astype(WIDE)
+                for k in range(3):
+                    total += self.next_in[slot, 2 * k + i].astype(WIDE)
+                self.sums[slot, s.z, s.x, i] = total.astype(LOW)
+                return carry
+
+            lax.fori_loop(0, 2, add, 0)
+            self.next(core, p).start()
+        else:
+            self.next(core, p).wait_recv()
+
+            def add(i, carry):
+                self.sums[slot, i, s.x, s.y] += self.next_in[slot, i]
+                return carry
+
+            lax.fori_loop(0, 4, add, 0)
+            for k in (1, 3, 2):
+                self.hop(core, p, k).start()
+
+    def stage_four(self, core, p):
+        s, slot = self.spot, p % SLOTS
+        if core == 0:
+            self.next(core, p).wait_recv()
+
+            def add(i, carry):
+                self.final[slot, i] = self.sums[slot, s.z, s.x, i] + self.next_in[slot, 6 + i]
+                return carry
+
+            lax.fori_loop(0, 2, add, 0)
+        else:
+            for k in (1, 3, 2):
+                self.hop(core, p, k).wait_recv()
+            total = self.sums[slot, s.z, s.x, s.y].astype(WIDE)
+            for k in range(3):
+                total += self.next_in[slot, 4 + k].astype(WIDE)
+            self.final[slot, s.y] = total.astype(LOW)
+            self.last(p, True).start()
+
+    def stage_five(self, core, p):
+        if core == 1:
+            self.last(p, False).wait_recv()
+        for copy in self.results(core, p) + self.kept(core, p):
+            copy.start()
+
+    def release(self, core, p):
+        self.first(core, p).wait_send()
+        for k in (1, 2, 3):
+            self.hop(core, p, k).wait_send()
+        self.next(core, p).wait_send()
+        if core == 1:
+            self.last(p, True).wait_send()
+        for copy in self.results(core, p):
+            copy.wait_send()
+        for copy in self.kept(core, p):
+            copy.wait()
+        if p + SLOTS < len(PARTS):
+            s = self.spot
+            for i, device in enumerate((s.to_x, s.to_y)):
+                pl.semaphore_signal(self.free.at[i], 1, device_id=device, device_id_type=MESH)
+            for k in (1, 2, 3):
+                pl.semaphore_signal(self.free.at[1 + 4 - k], 1, device_id=s.hop(k), device_id_type=MESH)
+
+    def finish(self, core, p):
+        for copy in self.given(core, p):
+            copy.wait_send()
+        for copy in self.results(1 - core, p):
+            copy.wait_recv()
+
+    def program(self):
+        count = len(PARTS)
+        turns = [[("fetch", 0)]]
+        for s in range(count + 6):
+            turn = []
+            for stage, p in (
+                ("stage_one", s),
+                ("fetch", s + 1),
+                ("stage_two", s - 1),
+                ("stage_three", s - 2),
+                ("stage_four", s - 3),
+                ("stage_five", s - 4),
+                ("release", s - 5),
+            ):
+                if 0 <= p < count:
+                    turn.append((stage, p))
+            turns.append(turn)
+        return turns
+
+    def run(self, steps):
+        for core in (0, 1):
+
+            @pl.when(self.spot.core == core)
+            def _():
+                for stage, p in steps:
+                    getattr(self, stage)(core, p)
+
+
+def backward_kernel(per_place, *refs):
+    dense_kinds = [kind for kind in KINDS if kind not in ("CELL", "TABLE")]
+    grads = dict(zip(dense_kinds, refs[:6]))
+    record_in, cell, codes, lengths, pool_grad = refs[6:11]
+    result = dict(zip(KINDS, refs[11:19]))
+    landing, grads["CELL"], grads["TABLE"] = refs[19:22]
+    record, state_grad, total, cell_part, table_part = refs[22:27]
+    buffers, (record_sem, out_sem), sems = refs[27:32], refs[32:34], refs[34:39]
+    spot = Spot(per_place)
+
+    def record_copy(t):
+        return pltpu.make_async_copy(record_in.at[t], record.at[t], record_sem.at[t])
+
+    def fill(i, carry):
+        record_copy(CHARS - 1 - i).start()
+        return carry
+
+    lax.fori_loop(0, CHARS, fill, 0)
+    spot.greet()
+    reduce = Reduce(spot, grads, landing, buffers, result, sems)
+    reduce.run([("give", p) for p in range(DENSE_PARTS)])
+    turns = reduce.program()
+    state_grad[...] = jnp.zeros_like(state_grad)
+    total[...] = jnp.zeros_like(total)
+    early = TURNS_IN_LOOP
+    steps = [step for turn in turns[:early] for step in turn]
+    share = -(-len(steps) // CHARS)
+
+    def retreat(i, carry):
+        t = CHARS - 1 - i
+        record_copy(t).wait()
+        gru_backward_step(t, cell, record, state_grad, pool_grad, lengths)
+        for k in range(CHARS):
+
+            @pl.when(i == k)
+            def _():
+                reduce.run(steps[k * share : (k + 1) * share])
+
+        return carry
+
+    lax.fori_loop(0, CHARS, retreat, 0)
+    for way in (0, 1):
+        cell_gradient(way, record, cell_part)
+        copy = pltpu.make_async_copy(cell_part, grads["CELL"].at[pl.ds(2 * way, 2)], out_sem.at[0])
+        copy.start()
+        reduce.run(turns[early + way])
+        copy.wait()
+
+    def look_up(c, carry):
+        table_gradient(c, cell, record, codes, total)
+        return carry
+
+    lax.fori_loop(0, CHARS, look_up, 0)
+    table_part[...] = jnp.transpose(total[...]).astype(LOW).reshape((4, 2, 2) + BLOCKS["TABLE"])
+    copy = pltpu.make_async_copy(table_part, grads["TABLE"], out_sem.at[0])
+    copy.start()
+    copy.wait()
+    reduce.run([("give", p) for p in range(DENSE_PARTS, len(PARTS))])
+    for turn in turns[early + 2 :]:
+        reduce.run(turn)
+    reduce.run([("finish", p) for p in range(len(PARTS))])
+
+
+TURNS_IN_LOOP = 7
+
+
+def reduce_and_return(grads, record, cell, codes, lengths, pool_grad, per_place):
+    dense_kinds = [kind for kind in KINDS if kind not in ("CELL", "TABLE")]
+    in_vmem = pl.BlockSpec(memory_space=pltpu.VMEM)
+    anywhere = pl.BlockSpec(memory_space=pl.ANY)
+    count = len(PARTS)
+    shapes = [jax.ShapeDtypeStruct((2,) + BLOCKS[kind], LOW) for kind in KINDS]
+    shapes += [jax.ShapeDtypeStruct((count, 4, 2, 2, ROWS, LANES), LOW)]
+    shapes += [jax.ShapeDtypeStruct((4, 2, 2) + BLOCKS[kind], LOW) for kind in ("CELL", "TABLE")]
+    results = pl.pallas_call(
+        partial(backward_kernel, per_place),
+        out_shape=shapes,
+        in_specs=[anywhere] * 7 + [in_vmem] * 4,
+        out_specs=[anywhere] * len(shapes),
+        scratch_shapes=[
+            pltpu.VMEM((CHARS, TOKENS, 2 * RECORD), LOW),
+            pltpu.VMEM((TOKENS, 2 * HID), WIDE),
+            pltpu.VMEM((1024, EMB), WIDE),
+            pltpu.VMEM((2, 2, 2) + BLOCKS["CELL"], LOW),
+            pltpu.VMEM((4, 2, 2) + BLOCKS["TABLE"], LOW),
+            pltpu.VMEM((SLOTS, 4, 2, 2, ROWS, LANES), LOW),
+            pltpu.VMEM((2, 4, 2, 2, ROWS, LANES), LOW),
+            pltpu.VMEM((SLOTS, 4, 2, ROWS, LANES), LOW),
+            pltpu.VMEM((SLOTS, 8, ROWS, LANES), LOW),
+            pltpu.VMEM((SLOTS, 2, ROWS, LANES), LOW),
+            pltpu.SemaphoreType.DMA((CHARS,)),
+            pltpu.SemaphoreType.DMA((1,)),
+            pltpu.SemaphoreType.DMA((count, MOVES)),
+            pltpu.SemaphoreType.DMA((count, MOVES)),
+            pltpu.SemaphoreType.DMA((2, SUBS + 1)),
+            pltpu.SemaphoreType.DMA((count, SUBS)),
+            pltpu.SemaphoreType.REGULAR((5,)),
+        ],
+        compiler_params=pltpu.CompilerParams(collective_id=1, has_side_effects=True, vmem_limit_bytes=60 << 20),
+    )(*[grads[kind] for kind in dense_kinds], record, cell, codes, lengths, pool_grad)
+    return dict(zip(KINDS, results[:8]))
 
 
 def layer_norm(inputs, gain_row, shift_row):
@@ -530,46 +881,6 @@
     return output, hidden_grad, pooled_grad, grads
 
 
-def backward_kernel(record_in, cell, table, codes, lengths, pool_grad, cell_grad, table_grad, record, state_grad, total, record_sem):
-    copy = pltpu.make_async_copy(record_in, record, record_sem)
-    copy.start()
-    copy.wait()
-    state_grad[...] = jnp.zeros_like(state_grad)
-
-    def retreat(i, carry):
-        gru_backward_step(CHARS - 1 - i, cell, record, state_grad, pool_grad, lengths)
-        return carry
-
-    lax.fori_loop(0, CHARS, retreat, 0)
-    for way in (0, 1):
-        cell_gradient(way, record, cell_grad)
-    total[...] = jnp.zeros_like(total)
-
-    def look_up(c, carry):
-        table_gradient(c, cell, record, codes, total)
-        return carry
-
-    lax.fori_loop(0, CHARS, look_up, 0)
-    table_grad[...] = total[...].astype(LOW)
-
-
-def gru_backward(record, cell, table, codes, lengths, pool_grad):
-    in_vmem = pl.BlockSpec(memory_space=pltpu.VMEM)
-    return pl.pallas_call(
-        backward_kernel,
-        out_shape=[jax.ShapeDtypeStruct((6 * HID, X_WIDTH), LOW), jax.ShapeDtypeStruct((EMB, 1024), LOW)],
-        in_specs=[pl.BlockSpec(memory_space=pl.ANY)] + [in_vmem] * 5,
-        out_specs=[in_vmem] * 2,
-        scratch_shapes=[
-            pltpu.VMEM((CHARS, TOKENS, 2 * RECORD), LOW),
-            pltpu.VMEM((TOKENS, 2 * HID), WIDE),
-            pltpu.VMEM((EMB, 1024), WIDE),
-            pltpu.SemaphoreType.DMA,
-        ],
-        compiler_params=pltpu.CompilerParams(vmem_limit_bytes=56 << 20),
-    )(record, cell, table, codes, lengths, pool_grad)
-
-
 def unpack(final):
     part = {kind: value.reshape(-1, value.shape[-1]).astype(WIDE) for kind, value in final.items()}
     cell, table, out, stream, merge = (part[kind] for kind in ("CELL", "TABLE", "OUT", "STREAM", "MERGE"))
@@ -600,14 +911,8 @@
     whole, record, pooled = gather_and_read(own, codes, lengths, per_place)
     output, hidden_grad, pooled_grad, grads = dense(whole, hidden, sequence_length, cotangent, pooled)
     pool_grad = pooled_grad / lengths.astype(WIDE)
-    cell_grad, table_grad = gru_backward(record, whole["CELL"], whole["TABLE"], codes, lengths, pool_grad)
-    grads["CELL"] = cell_grad.reshape((4, 2, 2) + BLOCKS["CELL"])
-    grads["TABLE"] = table_grad.reshape((4, 2, 2) + BLOCKS["TABLE"])
-    final = {}
-    for kind, part in grads.items():
-        part = part.reshape((8, 2) + part.shape[3:])
-        part = lax.psum_scatter(part, "grp", scatter_dimension=0, tiled=True)
-        final[kind] = lax.psum(part, "wide")
+    rows = jnp.transpose(char_codes)
+    final = reduce_and_return(grads, record, whole["CELL"], rows, lengths, pool_grad, per_place)
     return (output, hidden_grad, *unpack(final))
 
 

time: 1110 us -> 456 us (0.41)
  waiting for transfers between devices: 720 us -> 0.01 us
  Pallas kernels: 212 us -> 321 us
  local copies, waits for them, and re-layouts: 61.8 us -> 39.5 us
  between operations: 15.7 us -> 2.85 us
    reduce_scatter x8 -> x0, waiting for transfers between devices: 645 us -> none  [shards(): part = lax.psum_scatter(part, 'grp', scatter_dimension=0, tiled=True)]
    pallas_call x1, Pallas kernels: 55.7 us -> 163 us  [reduce_and_return(): pl.pallas_call(partial(backward_kernel, per_place), out_shape=shapes, in_...]
    psum x1 -> x0, waiting for transfers between devices: 73.8 us -> none  [shards(): final[kind] = lax.psum(part, 'wide')]
  transfers between devices with their start and end apart: 13 -> 4, of which waited for: 9 -> 0; matrix products, arithmetic and copies ran while one was open for 6% -> 4% of each run, Pallas kernels for 0% -> 0%
where the time goes in v2:
time: 456 us; the launch traced here: 450 us
  Pallas kernels  321 us (70%)
  matrix products  59.9 us (13%)
  local copies, waits for them, and re-layouts  39.5 us (9%)
  other arithmetic  25.7 us (6%)
    pallas_call x1, Pallas kernels, reduce_and_return(): pl.pallas_call(partial(backward_kernel, per_place), out_shape=shapes, in_...  163 us
    pallas_call x1, Pallas kernels, gather_and_read(): pl.pallas_call(partial(forward_kernel, per_place), out_shape=[jax.ShapeDt...  158 us
    dot_general x7, matrix products, dot_first(): lax.dot_general(left_side, right_side, (((0,), (0,)), ((), ())), preferre...  20.1 us
    dot_general x7, matrix products, dot_second(): lax.dot_general(left_side, right_side, (((1,), (1,)), ((), ())), preferre...  17.9 us
    dot_general x7, matrix products, dot_plain(): return jnp.dot(left_side, right_side, preferred_element_type=WIDE)  13.9 us
    unnamed x159, local copies, waits for them, and re-layouts  13.8 us
    dot_general x1, local copies, waits for them, and re-layouts, dot_plain(): return jnp.dot(left_side, right_side, preferred_element_type=WIDE)  10.3 us
  transfers between devices with their start and end apart: 4, of which 0 were waited for; matrix products, arithmetic and copies ran while one was open for 4% of the time, Pallas kernels for 0%

profile of v2, /device:TPU:0, one launch (start us, length us, event | category | flops | bytes accessed | tf_op | source)
XLA Modules:
  0.0 450.2 jit_solution(17183128484272248313)
XLA Ops:
  3.6 1.0 pad_maximum_fusion.9
  8.2 0.9 bitcast_dynamic-update-slice_fusion
  10.7 0.9 bitcast_dynamic-update-slice_fusion.3
  11.6 0.9 bitcast_dynamic-update-slice_fusion.2
  12.5 0.9 bitcast_dynamic-update-slice_fusion.1
  16.1 1.5 copy.54.refs_8_
  22.8 157.8 %shard_map.289 = (bf16[4,2,2,144,768]{4,3,2,1,0:T(8,128)(2,1)}, bf16[4,2,2,16,1024]{4,3,2,1,0:T(8,128)(2,1)}, bf16[4,2,2,144,768]{4,3,2,1,0:T(8,128)(2,1)}, bf16...) custom-call(bf16[144,768]{1,0:T(8,128)(2,1)} %get-tuple-element.90.r, ...), custom_call_target="tpu_custom_call" | custom-call | tf_op jit(solution)/shard_map/pallas_call | solution.py:297
  180.6 1.0 slice.220
  181.6 1.0 slice_convert_fusion.2
  183.1 3.1 fusion.1
  186.3 1.3 fusion.77
  189.9 8.9 %multiply_convert_fusion = (bf16[128,3072]{1,0:T(8,128)(2,1)S(1)}, f32[128,3072]{1,0:T(8,128)}, f32[128,3072]{1,0:T(8,128)}) fusion(f32[3072]{0:T(1024)S(1)} %reshape.266, bf16[3072,768]{1,0:T(8,128)(2,1)} %bitcast.231, f32[128,768]{1,0:T(8,128)S(1)} %get-tuple-element.103, f32[768]{0:T(1024)S(1)} %get-tuple-element.67, f32[768]{0:T(1024)S(1)} %get-tuple-element.68, ...), kind=kOutput, calls=%fused_computation.13 | convolution fusion | flops 630423552 | bytes 9063424 | tf_op jit(solution)/shard_map/dot_general | solution.py:62
  198.8 1.8 fusion.79
  202.2 2.4 fusion.80
  205.6 0.9 fusion.74
  207.2 5.2 %convolution_convert_fusion = bf16[768,4608]{1,0:T(8,128)(2,1)} fusion(bf16[128,1536]{1,0:T(8,128)(2,1)S(1)} %get-tuple-element.94, bf16[128,768]{1,0:T(8,128)(2,1)S(1)} %fusion.16, bf16[128,768]{1,0:T(8,128)(2,1)S(1)} %fusion.15, bf16[128,1536]{1,0:T(8,128)(2,1)S(1)} %get-tuple-element.93, f32[128,768]{1,0:T(8,128)S(1)} %get-tuple-element.77, ...), kind=kOutput, calls=%fused_computation.1 | convolution fusion | flops 914423808 | bytes 8651264 | tf_op jit(solution)/shard_map/dot_general | solution.py:58
  212.4 10.3 %copy.58 = bf16[4608,768]{1,0:T(8,128)(2,1)} copy(bf16[4608,768]{0,1:T(8,128)(2,1)} %bitcast.224) | data formatting | bytes 14155776 | tf_op jit(solution)/shard_map/dot_general | solution.py:54
  222.7 5.6 %fusion.42 = f32[128,3,1536]{2,0,1:T(8,128)S(1)} fusion(bf16[3,1536,768]{2,1,0:T(8,128)(2,1)} %bitcast.221, f32[128,768]{1,0:T(8,128)S(1)} %get-tuple-element.77, f32[128]{0:T(128)S(1)} %negate_multiply_fusion.3), kind=kOutput, calls=%fused_computation.148 | convolution fusion | flops 906166272 | bytes 9830912 | tf_op jit(solution)/shard_map/dot_general | solution.py:54
  228.6 1.5 copy-done.6
  230.1 1.0 multiply_reduce_fusion.1
  231.4 2.3 fusion.81
  233.7 1.5 multiply_reduce_fusion.2
  235.2 0.9 fusion.72
  236.1 1.1 convolution_convert_fusion.7
  239.2 1.7 copy.59
  241.0 3.1 bitcast_reduce_fusion
  244.0 1.7 multiply_reduce_fusion
  246.0 0.9 copy-done.20
  247.2 0.9 bitcast_reduce_fusion.1
  248.1 1.5 convolution_convert_fusion.4
  249.7 1.6 convolution_convert_fusion.6
  251.3 1.5 convolution_convert_fusion.5
  252.9 1.4 fusion.17
  254.3 2.9 convolution_convert_fusion.3
  257.1 3.6 convolution_convert_fusion.2
  260.8 3.8 convolution_convert_fusion.1
  264.8 1.1 convolution_divide_fusion.refs_10_
  266.9 1.4 pad_maximum_fusion.2
  268.3 0.9 copy.78
  269.2 1.4 pad.35.clone
  271.4 1.6 pad_maximum_fusion.refs_4_
  273.0 163.5 %shard_map.290 = (bf16[2,144,768]{2,1,0:T(8,128)(2,1)}, bf16[2,16,1024]{2,1,0:T(8,128)(2,1)}, bf16[2,144,768]{2,1,0:T(8,128)(2,1)}, bf16[2,48,1024]{2,1,0:T(8,12...) custom-call(bf16[4,2,2,144,768]{4,3,2,1,0:T(8,128)(2,1)} %bitcast.22, ...), custom_call_target="tpu_custom_call" | custom-call | tf_op jit(solution)/shard_map/pallas_call | solution.py:743
  436.5 1.0 bitcast_convert_fusion.4
  438.4 1.1 convert_bitcast_fusion.1
  444.7 1.4 copy.66
  446.1 1.2 convert_bitcast_fusion
  447.6 0.9 pad_maximum_fusion.4
  448.5 1.3 pad_maximum_fusion.1
  (252 shorter events, 32.6 us)
Async XLA Ops:
  0.6 13.5 %copy-start.60 = (s32[128]{0:T(128)S(1)}, s32[128]{0:T(128)}, u32[]{:S(2)}) copy-start(s32[128]{0:T(128)} %param.20) | copy-start | bytes 1540
  0.7 14.1 %copy-start.9 = (bf16[128,768]{1,0:T(8,128)(2,1)S(1)}, bf16[128,768]{1,0:T(8,128)(2,1)}, u32[]{:S(2)}) copy-start(bf16[128,768]{1,0:T(8,128)(2,1)} %param.22) | copy-start | bytes 589828
  0.7 15.4 %copy-start.31 = (s32[128,20]{0,1:T(8,128)S(1)}, s32[128,20]{0,1:T(8,128)}, u32[]{:S(2)}) copy-start(s32[128,20]{0,1:T(8,128)} %param.19) | copy-start | bytes 30724
  1.4 16.2 %collective-permute-start.1 = (bf16[8,1024]{1,0:T(8,128)(2,1)S(1)}, bf16[8,1024]{1,0:T(8,128)(2,1)S(1)}, u32[]{:S(2)}, u32[]{:S(2)}) collective-permute-start(bf16[8,1024]{1,0:T(8,128)(2,1)S(1)} %pad.30), channel_id=1, source_target_pairs={{0,1},{1,0},{2,3},{3,2},{4,5},{5,4},{6,7},{7,6},{8,9},{9,8},{10,11... | collective-permute-start | bytes 49160 | tf_op jit(solution)/shard_map/ppermute | solution.py:350
  1.9 16.4 %collective-permute-start.3 = (bf16[96,768]{1,0:T(8,128)(2,1)}, bf16[96,768]{1,0:T(8,128)(2,1)S(1)}, u32[]{:S(2)}, u32[]{:S(2)}) collective-permute-start(bf16[96,768]{1,0:T(8,128)(2,1)} %bitcast.264), channel_id=1, source_target_pairs={{0,1},{1,0},{2,3},{3,2},{4,5},{5,4},{6,7},{7,6},{8,9},{9,8},{10,11... | collective-permute-start | bytes 442376 | tf_op jit(solution)/shard_map/ppermute | solution.py:350
  3.6 14.1 %copy-start.30 = (bf16[1000,8]{0,1:T(8,128)(2,1)S(1)}, bf16[1000,8]{0,1:T(8,128)(2,1)}, u32[]{:S(2)}) copy-start(bf16[1000,8]{0,1:T(8,128)(2,1)} %param.28) | copy-start | bytes 48004
  3.6 14.7 %copy-start.26 = (bf16[768,96]{0,1:T(8,128)(2,1)S(1)}, bf16[768,96]{0,1:T(8,128)(2,1)}, u32[]{:S(2)}) copy-start(bf16[768,96]{0,1:T(8,128)(2,1)} %param.25) | copy-start | bytes 442372
  4.5 14.5 %collective-permute-start = (bf16[72,1536]{1,0:T(8,128)(2,1)S(1)}, bf16[72,1536]{1,0:T(8,128)(2,1)S(1)}, u32[]{:S(2)}, u32[]{:S(2)}) collective-permute-start(bf16[72,1536]{1,0:T(8,128)(2,1)S(1)} %pad_maximum_fusion.9), channel_id=1, source_target_pairs={{0,1},{1,0},{2,3},{3,2},{4,5},{5,4},{6,7},{7,6},{8,9},{9,8},{10,11... | collective-permute-start | bytes 663560 | tf_op jit(solution)/shard_map/ppermute | solution.py:350
  12.5 6.6 %copy-start.15 = (bf16[768,72]{0,1:T(8,128)(2,1)S(1)}, bf16[768,72]{0,1:T(8,128)(2,1)}, u32[]{:S(2)}) copy-start(bf16[768,72]{0,1:T(8,128)(2,1)} %param.23) | copy-start | bytes 331780
  13.4 6.5 %collective-permute-start.2 = (bf16[24,10240]{1,0:T(8,128)(2,1)S(1)}, bf16[24,10240]{1,0:T(8,128)(2,1)S(1)}, u32[]{:S(2)}, u32[]{:S(2)}) collective-permute-start(bf16[24,10240]{1,0:T(8,128)(2,1)S(1)} %bitcast_dynamic-update-slice_fusion.1), channel_id=1, source_target_pairs={{0,1},{1,0},{2,3},{3,2},{4,5},{5,4},{6,7},{7,6},{8,9},{9,8},{10,11... | collective-permute-start | bytes 1474568 | tf_op jit(solution)/shard_map/ppermute | solution.py:350
  14.1 173.5 %copy-start.62 = (f32[128]{0:T(128)}, f32[128]{0:T(128)S(1)}, u32[]{:S(2)}) copy-start(f32[128]{0:T(128)S(1)} %compare_select_fusion) | copy-start | bytes 1540
  180.6 2.5 copy-start.21
  188.2 10.6 %copy-start.24 = (bf16[12,64,128]{2,1,0:T(8,128)(2,1)}, bf16[12,64,128]{2,1,0:T(8,128)(2,1)S(1)}, u32[]{:S(2)}) copy-start(bf16[12,64,128]{2,1,0:T(8,128)(2,1)S(1)} %convolution_convert_fusion.8) | copy-start | bytes 589828
  189.0 9.8 %slice-start.4 = ((s8[4718592]{0:T(1024)(128)(4,1)}), s8[4194304]{0:T(1024)(128)(4,1)S(1)}, s32[]{:S(2)}) async-start(s8[4718592]{0:T(1024)(128)(4,1)} %bitcast.235), calls=%async_computation.4 | async-start | bytes 8388608
  189.0 13.1 %slice-start = ((s8[7077888]{0:T(1024)(128)(4,1)}), s8[4194304]{0:T(1024)(128)(4,1)S(1)}, s32[]{:S(2)}) async-start(s8[7077888]{0:T(1024)(128)(4,1)} %bitcast.225), calls=%async_computation | async-start | bytes 8388608
  189.6 44.0 %copy-start.33 = (f32[128]{0:T(128)}, f32[128]{0:T(128)S(1)}, u32[]{:S(2)}) copy-start(f32[128]{0:T(128)S(1)} %broadcast_multiply_fusion.2) | copy-start | bytes 1540
  189.8 43.8 %copy-start.38 = (f32[128]{0:T(128)}, f32[128]{0:T(128)S(1)}, u32[]{:S(2)}) copy-start(f32[128]{0:T(128)S(1)} %fusion.60) | copy-start | bytes 1540
  189.8 8.9 %slice-start.5 = ((s8[4718592]{0:T(1024)(128)(4,1)}), s8[524288]{0:T(1024)(128)(4,1)S(1)}, s32[]{:S(2)}) async-start(s8[4718592]{0:T(1024)(128)(4,1)} %bitcast.235), calls=%async_computation.5 | async-start | bytes 1048576
  189.9 12.3 %slice-start.1 = ((s8[7077888]{0:T(1024)(128)(4,1)}), s8[2883584]{0:T(1024)(128)(4,1)S(1)}, s32[]{:S(2)}) async-start(s8[7077888]{0:T(1024)(128)(4,1)} %bitcast.225), calls=%async_computation.1 | async-start | bytes 5767168
  200.6 30.5 %copy-start.40 = (f32[128]{0:T(128)}, f32[128]{0:T(128)S(1)}, u32[]{:S(2)}) copy-start(f32[128]{0:T(128)S(1)} %broadcast_multiply_fusion.1) | copy-start | bytes 1540
  200.8 30.3 %copy-start.55 = (f32[128]{0:T(128)}, f32[128]{0:T(128)S(1)}, u32[]{:S(2)}) copy-start(f32[128]{0:T(128)S(1)} %fusion.61) | copy-start | bytes 1540
  222.7 8.7 %slice-start.6 = ((s8[4718592]{0:T(1024)(128)(4,1)}), s8[4194304]{0:T(1024)(128)(4,1)S(1)}, s32[]{:S(2)}) async-start(s8[4718592]{0:T(1024)(128)(4,1)} %bitcast.238), calls=%async_computation.6 | async-start | bytes 8388608
  228.2 3.1 slice-start.7
  228.4 3.0 copy-start.63
  228.4 3.0 copy-start.64
  230.1 3.6 slice-start.2
  231.3 6.6 %copy-start.42 = (f32[128]{0:T(128)}, f32[128]{0:T(128)S(1)}, u32[]{:S(2)}) copy-start(f32[128]{0:T(128)S(1)} %negate_multiply_fusion.2) | copy-start | bytes 1540
  233.7 2.4 copy-start.28
  236.1 2.5 copy-start.57
  245.8 2.3 copy-start.25
  245.8 2.3 copy-start.58
  246.8 2.8 copy-start.41
  246.8 2.8 copy-start.56
  249.7 3.1 copy-start.23
  249.7 3.2 copy-start.2
  254.3 2.9 copy-start.34
  254.3 2.9 copy-start.39
  257.1 3.7 copy-start.4
  257.1 3.7 copy-start.43
  260.8 3.9 copy-start.44
  260.8 4.0 copy-start.45
  260.8 4.0 copy-start.7
  260.8 4.0 copy-start.61
  438.4 2.6 copy-start.29
  439.5 4.2 copy-start.18
  439.5 2.9 slice-start.8
  440.3 4.3 copy-start.14
  444.7 2.6 copy-start.11
  (30 other events, 48.4 us)

commit v3 on v2

--- a/solution.py
+++ b/solution.py
@@ -45,6 +45,8 @@
     ("MERGE", 3072, 3840, 768),
 )
 
+AHEAD = 3
+
 X_WIDTH = 768
 RECORD = X_WIDTH + 4 * HID
 GATE_R, GATE_Z, GATE_N, GATE_Q = (X_WIDTH + i * HID for i in range(4))
@@ -60,6 +62,10 @@
 
 def dot_second(left_side, right_side):
     return lax.dot_general(left_side, right_side, (((1,), (1,)), ((), ())), preferred_element_type=WIDE)
+
+
+def lanes_of(ref, start, width):
+    return ref[:, pl.ds(start, width)]
 
 
 def sigmoid(inputs):
@@ -97,8 +103,8 @@
 
 
 class Gather:
-    def __init__(self, spot, own, whole, sems):
-        self.spot, self.own, self.whole = spot, own, whole
+    def __init__(self, spot, whole, sems):
+        self.spot, self.whole = spot, whole
         self.sent, self.got = sems
 
     def region(self, core, p, z, f, l):
@@ -106,14 +112,12 @@
         lanes = pl.ds((first, second)[core], width)
         return self.whole[kind].at[z, f, l, :, lanes] if core == 0 else self.whole[kind].at[z, l, f, :, lanes]
 
-    def move(self, part, p, j, device, source=None):
-        return remote(part if source is None else source, part, self.sent.at[p, j], self.got.at[p, j], device)
+    def move(self, part, p, j, device):
+        return remote(part, part, self.sent.at[p, j], self.got.at[p, j], device)
 
     def along(self, core, p, k):
         f, l, _, _ = self.spot.near(core)
-        kind, first, second, width = PIECES[p]
-        source = self.own[kind].at[:, pl.ds((first, second)[core], width)]
-        return self.move(self.region(core, p, self.spot.z, f, l), p, k - 1, self.spot.hop(k), source)
+        return self.move(self.region(core, p, self.spot.z, f, l), p, k - 1, self.spot.hop(k))
 
     def along_in(self, core, p, k):
         f, l, _, _ = self.spot.near(core)
@@ -169,19 +173,17 @@
         for j in range(5):
             self.aside(core, p, j).wait_send()
 
-    def program(self):
-        steps = []
+    def turns(self):
         count = len(PIECES)
-        ahead = 3
-        for p in range(ahead):
-            steps.append(("start", p))
+        turns = []
         for s in range(count + 3):
-            if s + ahead < count:
-                steps.append(("start", s + ahead))
+            ahead = range(AHEAD + 1) if s == 0 else [s + AHEAD]
+            turn = [("start", p) for p in ahead if p < count]
             for lag, stage in enumerate(("second", "third", "fourth", "fifth")):
                 if 0 <= s - lag < count:
-                    steps.append((stage, s - lag))
-        return steps
+                    turn.append((stage, s - lag))
+            turns.append(turn)
+        return turns
 
     def run(self, steps):
         for core in (0, 1):
@@ -192,15 +194,20 @@
                     getattr(self, stage)(core, p)
 
 
-def gru_forward_step(t, cell, record, state, total, shifts, lengths):
+RING = 4
+
+
+def gru_forward_step(t, cell, spelled, record, state, total, shifts, lengths):
+    slot = t % RING
     for way in (0, 1):
         base = way * RECORD
         place = t if way == 0 else CHARS - 1 - t
         live = lengths[...] > place
         lanes = pl.ds(way * HID, HID)
         h = state[:, lanes]
-        record[t, :, pl.ds(base + EMB, HID)] = h.astype(LOW)
-        x = record[t, :, pl.ds(base, X_WIDTH)]
+        record[slot, :, pl.ds(base, EMB)] = spelled[place]
+        record[slot, :, pl.ds(base + EMB, HID)] = h.astype(LOW)
+        x = record[slot, :, pl.ds(base, X_WIDTH)]
         weights = cell[pl.ds(2 * way, 2)].reshape(3 * HID, X_WIDTH)
         both = dot_second(x, weights[: 2 * HID])
         drive_n = dot_second(x[:, :EMB], weights[2 * HID :, :EMB]) + shifts[way, 0:1]
@@ -211,24 +218,98 @@
         fresh = jnp.where(live, n + u * (h - n), h)
         state[:, lanes] = fresh
         total[:, lanes] += jnp.where(live, fresh, 0.0)
-        record[t, :, pl.ds(base + GATE_R, HID)] = r.astype(LOW)
-        record[t, :, pl.ds(base + GATE_Z, HID)] = u.astype(LOW)
-        record[t, :, pl.ds(base + GATE_N, HID)] = n.astype(LOW)
-        record[t, :, pl.ds(base + GATE_Q, HID)] = recur_n.astype(LOW)
-
-
-def one_hot(codes, t, vocabulary):
-    return (lax.broadcasted_iota(jnp.int32, (TOKENS, vocabulary), 1) == codes[t]).astype(LOW)
+        record[slot, :, pl.ds(base + GATE_R, HID)] = r.astype(LOW)
+        record[slot, :, pl.ds(base + GATE_Z, HID)] = u.astype(LOW)
+        record[slot, :, pl.ds(base + GATE_N, HID)] = n.astype(LOW)
+        record[slot, :, pl.ds(base + GATE_Q, HID)] = recur_n.astype(LOW)
+
+
+def spread_matrix():
+    shape = (512, 512)
+    row, lane = lax.broadcasted_iota(jnp.int32, shape, 0), lax.broadcasted_iota(jnp.int32, shape, 1)
+    return (4 * (row % 128) + row // 128 == lane).astype(LOW)
+
+
+def read_small(out, small, feed_row, shuffle):
+    columns = out[:, :, :, :, pl.ds(768, 128)].reshape(768, 128).astype(WIDE)
+    rows = jnp.transpose(columns)
+    small[...] = rows[:32]
+    shuffle[...] = jnp.zeros_like(shuffle)
+    for c in range(6):
+        for j in range(4):
+            shuffle[c : c + 1, 128 * j : 128 * j + 128] = rows[13 + j : 14 + j, 128 * c : 128 * c + 128]
+    flat = dot_plain(shuffle[...].astype(LOW), spread_matrix())
+    for c in range(6):
+        feed_row[:, 512 * c : 512 * c + 512] = flat[c : c + 1]
+
+
+def norm_forward(inputs, i, small, gain, shift, norms, spreads):
+    centred = inputs - jnp.mean(inputs, axis=-1, keepdims=True)
+    inverse = lax.rsqrt(jnp.mean(centred * centred, axis=-1, keepdims=True) + norm_eps)
+    unit = centred * inverse
+    norms[i] = unit
+    spreads[i] = jnp.broadcast_to(inverse, spreads.shape[1:])
+    return unit * small[gain : gain + 1] + small[shift : shift + 1]
+
+
+def head_mask(which):
+    lane = lax.broadcasted_iota(jnp.int32, (TOKENS, 128), 1)
+    return (lane < 64) if which == 0 else (lane >= 64)
+
+
+def one_head(pair, which):
+    return jnp.where(head_mask(which), pair, jnp.zeros_like(pair))
+
+
+def soft_weights(queries, keys, which, valid):
+    scores = dot_second(one_head(queries, which), keys) * 0.125 + valid
+    weight = jnp.exp(scores - jnp.max(scores, axis=-1, keepdims=True))
+    return weight / jnp.sum(weight, axis=-1, keepdims=True)
+
+
+def key_mask(count):
+    lane = lax.broadcasted_iota(jnp.int32, (TOKENS, TOKENS), 1)
+    return jnp.where(lane < count, 0.0, masked_score).astype(WIDE)
+
+
+def attention_forward(projected, context, valid):
+    def pair(i, carry):
+        def part(at):
+            return projected[:, pl.ds(pl.multiple_of(at * 768 + 128 * i, 128), 128)]
+
+        queries, keys, values = part(0), part(1), part(2)
+        total = jnp.zeros((TOKENS, 128), WIDE)
+        for which in (0, 1):
+            soft = soft_weights(queries, keys, which, valid).astype(LOW)
+            total += dot_plain(soft, one_head(values, which))
+        context[:, pl.ds(pl.multiple_of(128 * i, 128), 128)] = total.astype(LOW)
+        return carry
+
+    lax.fori_loop(0, 6, pair, 0)
+
+
+def shifted(rows, down):
+    turned = pltpu.roll(rows, 1 if down else TOKENS - 1, 0)
+    row = lax.broadcasted_iota(jnp.int32, rows.shape, 0)
+    return jnp.where(row == (0 if down else TOKENS - 1), 0.0, turned)
+
+
+def window(joined, k):
+    if k == 1:
+        return joined[...]
+    return shifted(joined[...].astype(WIDE), k == 0).astype(LOW)
 
 
 def forward_kernel(per_place, *refs):
     count = len(KINDS)
     own = dict(zip(KINDS, refs[:count]))
-    codes, lengths = refs[count : count + 2]
-    outs = refs[count + 2 :]
-    whole = dict(zip(KINDS, outs[:count]))
-    record_out, pooled = outs[count : count + 2]
-    record, state, shifts, sent, got, own_sem, record_sem = outs[count + 2 :]
+    codes, lengths, hidden, valid_keys = refs[count : count + 4]
+    outs = refs[count + 4 :]
+    kept = dict(zip(KINDS, outs[:count]))
+    (record_out, output, projected, context, active, slope, joined, pooled_low, norms, spreads, small) = outs[count : count + 11]
+    scratch = outs[count + 11 :]
+    whole = dict(zip(KINDS, scratch[:count]))
+    (record, spelled, state, pooled, shifts, feed_row, shuffle, first, second, merged, sent, got, own_sem, kept_sem, record_sem) = scratch[count:]
     spot = Spot(per_place)
     own_copies = [
         pltpu.make_async_copy(own[kind], whole[kind].at[spot.z, spot.x, spot.y], own_sem.at[i])
@@ -239,82 +320,169 @@
     spot.greet()
     for copy in own_copies:
         copy.wait()
-    gather = Gather(spot, own, whole, (sent, got))
-    steps = gather.program()
-    lead = steps.index(("fifth", 1)) + 1
-    gather.run(steps[:lead])
-
-    table = whole["TABLE"][...].reshape(EMB, 1024)
-    cell = whole["CELL"]
-    ones = (lax.broadcasted_iota(jnp.int32, (TOKENS, 128), 1) < 2).astype(LOW)
+    gather = Gather(spot, whole, (sent, got))
+    turns = gather.turns()
+
+    def keep(kind):
+        return pltpu.make_async_copy(whole[kind], kept[kind], kept_sem.at[KINDS.index(kind)])
+
+    def weights(kind):
+        value = whole[kind][...]
+        return value.reshape(-1, value.shape[-1])
+
+    for turn in turns[:5]:
+        gather.run(turn)
+    for kind in ("CELL", "TABLE"):
+        keep(kind).start()
+    cell, table = whole["CELL"], weights("TABLE")
 
     def embed(c, carry):
-        rows = dot_second(one_hot(codes, c, 1024), table).astype(LOW)
-        record[c, :, pl.ds(0, EMB)] = rows
-        record[CHARS - 1 - c, :, pl.ds(RECORD, EMB)] = rows
-        record[c, :, pl.ds(EMB + HID, 128)] = ones
-        record[c, :, pl.ds(RECORD + EMB + HID, 128)] = ones
+        which = (lax.broadcasted_iota(jnp.int32, (1024, TOKENS), 0) == codes[pl.ds(c, 1)]).astype(LOW)
+        spelled[c] = jnp.transpose(dot_plain(table, which)).astype(LOW)
         return carry
 
     lax.fori_loop(0, CHARS, embed, 0)
     pick = (
         lax.broadcasted_iota(jnp.int32, (8, 128), 0) == lax.broadcasted_iota(jnp.int32, (8, 128), 1)
     ).astype(LOW)
+    ones = (lax.broadcasted_iota(jnp.int32, (TOKENS, 128), 1) < 2).astype(LOW)
     for way in (0, 1):
         late = cell[pl.ds(2 * way, 2)].reshape(3 * HID, X_WIDTH)[2 * HID :, EMB + HID :]
         shifts[way] = dot_second(pick, late)
+        for slot in range(RING):
+            record[slot, :, pl.ds(way * RECORD + EMB + HID, 128)] = ones
     state[...] = jnp.zeros_like(state)
     pooled[...] = jnp.zeros_like(pooled)
-    rest = steps[lead:]
-    share = -(-len(rest) // CHARS)
+    steps = [step for turn in turns[5:GRU_TURNS] for step in turn]
+    share = -(-len(steps) // CHARS)
+
+    def record_copy(t):
+        return pltpu.make_async_copy(record.at[t % RING], record_out.at[t], record_sem.at[t % RING])
 
     def advance(t, carry):
-        gru_forward_step(t, cell, record, state, pooled, shifts, lengths)
-        pltpu.make_async_copy(record.at[t], record_out.at[t], record_sem.at[t]).start()
+        @pl.when(t >= RING)
+        def _():
+            record_copy(t - RING).wait()
+
+        gru_forward_step(t, cell, spelled, record, state, pooled, shifts, lengths)
+        record_copy(t).start()
         for k in range(CHARS):
-
-            @pl.when(t == k)
-            def _():
-                gather.run(rest[k * share : (k + 1) * share])
+            if steps[k * share : (k + 1) * share]:
+
+                @pl.when(t == k)
+                def _():
+                    gather.run(steps[k * share : (k + 1) * share])
 
         return carry
 
     lax.fori_loop(0, CHARS, advance, 0)
-    pooled[...] = pooled[...] / lengths[...].astype(WIDE)
+    pooled_low[...] = (pooled[...] / lengths[...].astype(WIDE)).astype(LOW)
+
+    later = iter(turns[GRU_TURNS:])
+
+    def go_on():
+        gather.run(next(later))
+
+    for kind in ("ATT", "OUT"):
+        keep(kind).start()
+    read_small(whole["OUT"], small, feed_row, shuffle)
+    attention_in = weights("ATT")
+    for i, bias in enumerate((0, None, 1)):
+        block = dot_second(hidden[...], attention_in[768 * i : 768 * i + 768])
+        if bias is not None:
+            block = block + small[bias : bias + 1]
+        projected[:, 768 * i : 768 * i + 768] = block.astype(LOW)
+    attention_forward(projected, context, key_mask(valid_keys[0]))
+    attended = dot_second(context[...], weights("OUT")[:, :768]) + small[2:3]
+    first[...] = norm_forward(hidden[...].astype(WIDE) + attended, 0, small, 10, 3, norms, spreads)
+    go_on()
+    keep("IN").start()
+    first_low = first[...].astype(LOW)
+    for c in range(4):
+        rows = whole["IN"][c].reshape(768, 768)
+        inner = dot_second(first_low, rows) + feed_row[:, 768 * c : 768 * c + 768]
+        share_below = 0.5 * (1.0 + lax.erf(inner * 0.7071067811865476))
+        active[:, 768 * c : 768 * c + 768] = (inner * share_below).astype(LOW)
+        slope[:, 768 * c : 768 * c + 768] = (
+            share_below + inner * (0.3989422804014327 * jnp.exp(-0.5 * inner * inner))
+        ).astype(LOW)
+    go_on()
+    go_on()
+    keep("FEED").start()
+    two = first[...] + dot_second(active[...], weights("FEED")) + small[4:5]
+    second[...] = norm_forward(two, 1, small, 11, 5, norms, spreads)
+    go_on()
+    keep("STREAM").start()
+    stream = weights("STREAM")
+    joined[:, :768] = (dot_second(second[...].astype(LOW), stream[:, :768]) + small[6:7]).astype(LOW)
+    joined[:, 768:] = (dot_second(pooled_low[...], stream[:, 768:]) + small[7:8]).astype(LOW)
+    for k in range(3):
+        go_on()
+        taps = whole["MERGE"][:, :, :, :, pl.ds(1536 * k, 1536)].reshape(768, 1536)
+        part = dot_second(window(joined, k), taps)
+        merged[...] = part if k == 0 else merged[...] + part
+    keep("MERGE").start()
+    third = second[...] + merged[...] + small[8:9]
+    output[...] = norm_forward(third, 2, small, 12, 9, norms, spreads).astype(LOW)
 
     def landed(t, carry):
-        pltpu.make_async_copy(record.at[t], record_out.at[t], record_sem.at[t]).wait()
+        record_copy(t).wait()
         return carry
 
-    lax.fori_loop(0, CHARS, landed, 0)
+    lax.fori_loop(CHARS - RING, CHARS, landed, 0)
     gather.run([("drain", p) for p in range(len(PIECES))])
-
-
-def gather_and_read(own, codes, lengths, per_place):
+    for kind in KINDS:
+        keep(kind).wait()
+
+
+GRU_TURNS = 8
+
+
+def gather_and_read(own, codes, lengths, hidden, valid_keys, per_place):
     count = len(KINDS)
     in_vmem = pl.BlockSpec(memory_space=pltpu.VMEM)
     anywhere = pl.BlockSpec(memory_space=pl.ANY)
+    whole_shapes = [(4, 2, 2) + BLOCKS[kind] for kind in KINDS]
+    saved = {
+        "output": ((TOKENS, 768), LOW),
+        "projected": ((TOKENS, 2304), LOW),
+        "context": ((TOKENS, 768), LOW),
+        "active": ((TOKENS, 3072), LOW),
+        "slope": ((TOKENS, 3072), LOW),
+        "joined": ((TOKENS, 1536), LOW),
+        "pooled": ((TOKENS, 768), LOW),
+        "norms": ((3, TOKENS, 768), WIDE),
+        "spreads": ((3, TOKENS, 128), WIDE),
+        "small": ((32, 768), WIDE),
+    }
     results = pl.pallas_call(
         partial(forward_kernel, per_place),
-        out_shape=[jax.ShapeDtypeStruct((4, 2, 2) + BLOCKS[kind], LOW) for kind in KINDS]
+        out_shape=[jax.ShapeDtypeStruct(shape, LOW) for shape in whole_shapes]
+        + [jax.ShapeDtypeStruct((CHARS, TOKENS, 2 * RECORD), LOW)]
+        + [jax.ShapeDtypeStruct(shape, kind) for shape, kind in saved.values()],
+        in_specs=[anywhere] * count + [in_vmem] * 3 + [pl.BlockSpec(memory_space=pltpu.SMEM)],
+        out_specs=[anywhere] * (count + 1) + [in_vmem] * len(saved),
+        scratch_shapes=[pltpu.VMEM(shape, LOW) for shape in whole_shapes]
         + [
-            jax.ShapeDtypeStruct((CHARS, TOKENS, 2 * RECORD), LOW),
-            jax.ShapeDtypeStruct((TOKENS, 2 * HID), WIDE),
-        ],
-        in_specs=[in_vmem] * (count + 2),
-        out_specs=[in_vmem if kind in ("CELL", "TABLE") else anywhere for kind in KINDS] + [anywhere, in_vmem],
-        scratch_shapes=[
-            pltpu.VMEM((CHARS, TOKENS, 2 * RECORD), LOW),
+            pltpu.VMEM((RING, TOKENS, 2 * RECORD), LOW),
+            pltpu.VMEM((CHARS, TOKENS, EMB), LOW),
+            pltpu.VMEM((TOKENS, 2 * HID), WIDE),
             pltpu.VMEM((TOKENS, 2 * HID), WIDE),
             pltpu.VMEM((2, 8, HID), WIDE),
+            pltpu.VMEM((1, 3072), WIDE),
+            pltpu.VMEM((8, 512), WIDE),
+            pltpu.VMEM((TOKENS, 768), WIDE),
+            pltpu.VMEM((TOKENS, 768), WIDE),
+            pltpu.VMEM((TOKENS, 768), WIDE),
             pltpu.SemaphoreType.DMA((len(PIECES), 10)),
             pltpu.SemaphoreType.DMA((len(PIECES), 10)),
             pltpu.SemaphoreType.DMA((count,)),
-            pltpu.SemaphoreType.DMA((CHARS,)),
+            pltpu.SemaphoreType.DMA((count,)),
+            pltpu.SemaphoreType.DMA((RING,)),
         ],
-        compiler_params=pltpu.CompilerParams(collective_id=0, has_side_effects=True, vmem_limit_bytes=56 << 20),
-    )(*[own[kind] for kind in KINDS], codes, lengths)
-    return dict(zip(KINDS, results[:count])), results[count], results[count + 1]
+        compiler_params=pltpu.CompilerParams(collective_id=0, has_side_effects=True, vmem_limit_bytes=60 << 20),
+    )(*[own[kind] for kind in KINDS], codes, lengths, hidden, valid_keys)
+    return dict(zip(KINDS, results[:count])), results[count], dict(zip(saved, results[count + 1 :]))
 
 
 def pack(shards, per_place):
@@ -405,7 +573,7 @@
     drive, recur = dot_first(every(GATE_N, HID), x), dot_first(every(GATE_Q, HID), x)
     lane = lax.broadcasted_iota(jnp.int32, (HID, X_WIDTH), 1)
     parts.append(jnp.where((lane < EMB) | (lane == EMB + HID), drive, recur).astype(LOW))
-    result[...] = jnp.concatenate(parts, axis=0).reshape(result.shape)
+    result[:, :, :, 0:144] = jnp.concatenate(parts, axis=0).reshape(2, 2, 2, 144, X_WIDTH)
 
 
 def table_gradient(c, cell, record, codes, result):
@@ -438,7 +606,7 @@
         ("TABLE", 0, 16, 256, 768, 256, 32, 512, False),
     ],
 )
-SLOTS = 7
+SLOTS = 6
 SUBS = 5
 DENSE_PARTS = 10
 AT_FIRST, AT_HOP, AT_NEXT, AT_LAST, AT_RESULT = SUBS, SUBS, SUBS + 4, SUBS + 5, SUBS + 6
@@ -645,12 +813,12 @@
             turn = []
             for stage, p in (
                 ("stage_one", s),
+                ("release", s - 5),
                 ("fetch", s + 1),
                 ("stage_two", s - 1),
                 ("stage_three", s - 2),
                 ("stage_four", s - 3),
                 ("stage_five", s - 4),
-                ("release", s - 5),
             ):
                 if 0 <= p < count:
                     turn.append((stage, p))
@@ -666,32 +834,252 @@
                     getattr(self, stage)(core, p)
 
 
+def norm_backward(grad, i, gain, norms, spreads, small, gradients, gain_row, shift_row):
+    unit, inverse = norms[i], spreads[i][:, :1]
+    scaled = grad * small[gain : gain + 1]
+    gradients[gain_row : gain_row + 1] = jnp.sum(grad * unit, axis=0, keepdims=True)
+    gradients[shift_row : shift_row + 1] = jnp.sum(grad, axis=0, keepdims=True)
+    centre = jnp.mean(scaled, axis=-1, keepdims=True)
+    slope = jnp.mean(scaled * unit, axis=-1, keepdims=True)
+    return inverse * (scaled - centre - unit * slope)
+
+
+def attention_backward(projected, back, context_grad, valid, gradients):
+    def pair(i, carry):
+        def lanes(at):
+            return pl.ds(pl.multiple_of(at * 768 + 128 * i, 128), 128)
+
+        queries, keys, values = (projected[:, lanes(at)] for at in range(3))
+        above = context_grad[:, lanes(0)]
+        totals = [jnp.zeros((TOKENS, 128), WIDE) for _ in range(3)]
+        for which in (0, 1):
+            soft = soft_weights(queries, keys, which, valid)
+            part = one_head(above, which)
+            soft_grad = dot_second(part, values)
+            score = soft * (soft_grad - jnp.sum(soft * soft_grad, axis=-1, keepdims=True))
+            score = score.astype(LOW)
+            totals[0] += dot_plain(score, one_head(keys, which))
+            totals[1] += dot_first(score, one_head(queries, which))
+            totals[2] += dot_first(soft.astype(LOW), part)
+        totals[0] *= 0.125
+        totals[1] *= 0.125
+        for at in range(3):
+            back[:, lanes(at)] = totals[at].astype(LOW)
+        gradients[0:1, lanes(0)] = jnp.sum(totals[0], axis=0, keepdims=True)
+        gradients[1:2, lanes(0)] = jnp.sum(totals[2], axis=0, keepdims=True)
+        return carry
+
+    lax.fori_loop(0, 6, pair, 0)
+
+
+class Outbox:
+    def __init__(self, thin, thick, sems):
+        self.thin, self.thick, self.sems = thin, thick, sems
+        self.count = 0
+        self.flying = {}
+
+    def settle(self, key):
+        self.flying.pop(key).wait()
+
+    def settle_all(self):
+        for key in list(self.flying):
+            self.settle(key)
+
+    def send(self, key, source, target):
+        copy = pltpu.make_async_copy(source, target, self.sems.at[key])
+        copy.start()
+        self.flying[key] = copy
+
+    def room(self):
+        key = self.count % THIN
+        self.count += 1
+        if key in self.flying:
+            self.settle(key)
+        return key
+
+    def square(self, left, right, target):
+        key = self.room()
+        for half in (0, 1):
+            rows = dot_first(left[:, 384 * half : 384 * half + 384], right).astype(LOW)
+            self.thin[key, pl.ds(2 * half, 2)] = rows.reshape(2, 2, 2, 48, 768)
+        self.send(key, self.thin.at[key], target)
+
+    def block(self, left, right, target, shape):
+        if THIN in self.flying:
+            self.settle(THIN)
+        rows = shape[0] * shape[1] * shape[2] * shape[3]
+        parts = [
+            dot_first(left[:, at : at + 384], right).astype(LOW) for at in range(0, rows, 384)
+        ]
+        self.thick[0 : shape[0], :, :, 0 : shape[3]] = jnp.concatenate(parts, axis=0).reshape(shape)
+        self.send(THIN, self.thick.at[0 : shape[0], :, :, 0 : shape[3]], target)
+
+
+THIN = 2
+DENSE_KINDS = tuple(kind for kind in KINDS if kind not in ("CELL", "TABLE"))
+SAVED = ("projected", "context", "active", "slope", "joined", "pooled", "norms", "spreads", "small")
+
+
 def backward_kernel(per_place, *refs):
-    dense_kinds = [kind for kind in KINDS if kind not in ("CELL", "TABLE")]
-    grads = dict(zip(dense_kinds, refs[:6]))
-    record_in, cell, codes, lengths, pool_grad = refs[6:11]
-    result = dict(zip(KINDS, refs[11:19]))
-    landing, grads["CELL"], grads["TABLE"] = refs[19:22]
-    record, state_grad, total, cell_part, table_part = refs[22:27]
-    buffers, (record_sem, out_sem), sems = refs[27:32], refs[32:34], refs[34:39]
+    weights = dict(zip(DENSE_KINDS, refs[:6]))
+    record_in, cell, codes, lengths, hidden, cotangent, valid_keys = refs[6:13]
+    saved = dict(zip(SAVED, refs[13:22]))
+    outs = refs[22:]
+    result = dict(zip(KINDS, outs[:8]))
+    hidden_grad, landing = outs[8:10]
+    grads = dict(zip(KINDS, outs[10:18]))
+    scratch = outs[18:]
+    record, state_grad, pool_grad, total, gradients, grad, inner, back, thin, thick = scratch[:10]
+    table_part, columns, shuffle = scratch[10:13]
+    buffers = scratch[13:18]
+    record_sem, weight_sem, outbox_sem, column_sem = scratch[18:22]
+    sems = scratch[22:27]
     spot = Spot(per_place)
+    norms, spreads, small = saved["norms"], saved["spreads"], saved["small"]
+
+    def weight_copies(kind):
+        source = weights[kind]
+        if kind == "MERGE":
+            pairs = [(source, record.at[pl.ds(14, 6)])]
+        elif kind == "FEED":
+            pairs = [(source, record.at[pl.ds(8, 6), :, pl.ds(0, 3072)])]
+        elif kind == "STREAM":
+            pairs = [(source, record.at[pl.ds(8, 6), :, pl.ds(3072, 1536)])]
+        elif kind == "OUT":
+            pairs = [(source.at[j, :, pl.ds(0, 768)], record.at[0, :, pl.ds(768 * j, 768)]) for j in range(6)]
+        else:
+            first, count = (4, 4) if kind == "IN" else (1, 3)
+            pairs = [(source.at[:, j], record.at[pl.ds(first, count), :, pl.ds(768 * j, 768)]) for j in range(6)]
+        at = DENSE_KINDS.index(kind)
+        return [pltpu.make_async_copy(a, b, weight_sem.at[at, j]) for j, (a, b) in enumerate(pairs)]
+
+    def need(kind):
+        for copy in weight_copies(kind):
+            copy.wait()
+
+    def rows_of(slot):
+        return jnp.concatenate([record[slot, :, pl.ds(768 * j, 768)] for j in range(6)], axis=0)
 
     def record_copy(t):
         return pltpu.make_async_copy(record_in.at[t], record.at[t], record_sem.at[t])
 
-    def fill(i, carry):
-        record_copy(CHARS - 1 - i).start()
-        return carry
-
-    lax.fori_loop(0, CHARS, fill, 0)
+    def fill(first, count):
+        for t in range(first, first + count):
+            record_copy(t).start()
+
+    for kind in ("MERGE", "STREAM", "FEED", "IN", "OUT", "ATT"):
+        for copy in weight_copies(kind):
+            copy.start()
     spot.greet()
     reduce = Reduce(spot, grads, landing, buffers, result, sems)
-    reduce.run([("give", p) for p in range(DENSE_PARTS)])
-    turns = reduce.program()
+    outbox = Outbox(thin, thick, outbox_sem)
+    turns = iter(reduce.program())
+
+    def give(*parts):
+        outbox.settle_all()
+        reduce.run([("give", p) for p in parts])
+
+    def go_on():
+        reduce.run(next(turns))
+
+    gradients[...] = jnp.zeros_like(gradients)
+    merged = norm_backward(cotangent[...].astype(WIDE), 2, 12, norms, spreads, small, gradients, 12, 9)
+    gradients[8:9] = jnp.sum(merged, axis=0, keepdims=True)
+    grad[...] = merged
+    merged_low = merged.astype(LOW)
+    joined = saved["joined"]
+    for k in range(3):
+        taps = window(joined, k)
+        for half in (0, 1):
+            lanes = pl.ds(1536 * k + 768 * half, 768)
+            outbox.square(merged_low, taps[:, 768 * half : 768 * half + 768], grads["MERGE"].at[..., lanes])
+        give(k)
+    need("MERGE")
+    parts = [
+        dot_plain(merged_low, record[pl.ds(14, 6), :, pl.ds(1536 * k, 1536)].reshape(768, 1536)) for k in range(3)
+    ]
+    joined_grad = parts[1] + shifted(parts[0], False) + shifted(parts[2], True)
+    fill(14, 6)
+    gradients[6:7] = jnp.sum(joined_grad[:, :768], axis=0, keepdims=True)
+    gradients[7:8] = jnp.sum(joined_grad[:, 768:], axis=0, keepdims=True)
+    token_low, char_low = joined_grad[:, :768].astype(LOW), joined_grad[:, 768:].astype(LOW)
+    second_low = (norms[1] * small[11:12] + small[5:6]).astype(LOW)
+    outbox.square(token_low, second_low, grads["STREAM"].at[..., pl.ds(0, 768)])
+    outbox.square(char_low, saved["pooled"][...], grads["STREAM"].at[..., pl.ds(768, 768)])
+    give(3)
+    go_on()
+    need("STREAM")
+    stream = record[pl.ds(8, 6), :, pl.ds(3072, 1536)].reshape(768, 1536)
+    pool_grad[...] = dot_plain(char_low, stream[:, 768:]) / lengths[...].astype(WIDE)
+    second_grad = grad[...] + dot_plain(token_low, stream[:, :768])
+    two = norm_backward(second_grad, 1, 11, norms, spreads, small, gradients, 11, 5)
+    gradients[4:5] = jnp.sum(two, axis=0, keepdims=True)
+    grad[...] = two
+    two_low = two.astype(LOW)
+    for c in range(4):
+        outbox.square(two_low, saved["active"][:, 768 * c : 768 * c + 768], grads["FEED"].at[..., pl.ds(768 * c, 768)])
+        if c % 2 == 1:
+            give(4 + c // 2)
+    go_on()
+    need("FEED")
+    first_low = (norms[0] * small[10:11] + small[3:4]).astype(LOW)
+    shuffle[...] = jnp.zeros_like(shuffle)
+    for c in range(4):
+        lanes = pl.ds(768 * c, 768)
+        part = dot_plain(two_low, record[pl.ds(8, 6), :, lanes].reshape(768, 768))
+        part = part * saved["slope"][:, lanes].astype(WIDE)
+        inner[:, lanes] = part.astype(LOW)
+        sums = jnp.sum(part, axis=0, keepdims=True)
+        for half in (0, 1):
+            at = 768 * c + 384 * half
+            done = 0
+            while done < 384:
+                row, lane = (at + done) // 512, (at + done) % 512
+                size = min(512 - lane, 384 - done)
+                start = 384 * half + done
+                shuffle[row : row + 1, lane : lane + size] = sums[:, start : start + size]
+                done += size
+        outbox.block(inner[:, lanes], first_low, grads["IN"].at[pl.ds(c, 1)], (1, 2, 2, 192, 768))
+    fill(8, 6)
+    give(6, 7)
+    go_on()
+    need("IN")
+    first_grad = grad[...]
+    for c in range(4):
+        first_grad += dot_plain(inner[:, 768 * c : 768 * c + 768], rows_of(4 + c))
+    one = norm_backward(first_grad, 0, 10, norms, spreads, small, gradients, 10, 3)
+    fill(4, 4)
+    gradients[2:3] = jnp.sum(one, axis=0, keepdims=True)
+    grad[...] = one
+    one_low = one.astype(LOW)
+    need("OUT")
+    context_grad = dot_plain(one_low, rows_of(0)).astype(LOW)
+    inner[:, pl.ds(0, 768)] = context_grad
+    attention_backward(saved["projected"], back, inner, key_mask(valid_keys[0]), gradients)
+    outbox.square(one_low, saved["context"][...], grads["OUT"].at[..., pl.ds(0, 768)])
+    flat = dot_second(shuffle[...].astype(LOW), spread_matrix())
+    for c in range(6):
+        for j in range(4):
+            gradients[13 + j : 14 + j, 128 * c : 128 * c + 128] = flat[c : c + 1, 128 * j : 128 * j + 128]
+    columns[:, :, :, :, pl.ds(0, 128)] = jnp.transpose(gradients[...]).astype(LOW).reshape(4, 2, 2, 48, 128)
+    columns[:, :, :, :, pl.ds(128, 128)] = jnp.zeros((4, 2, 2, 48, 128), LOW)
+    column_copy = pltpu.make_async_copy(columns, grads["OUT"].at[..., pl.ds(768, 256)], column_sem.at[0])
+    column_copy.start()
+    go_on()
+    for i in range(2):
+        outbox.block(back[:, pl.ds(1152 * i, 1152)], hidden[...], grads["ATT"].at[pl.ds(2 * i, 2)], (2, 2, 2, 144, 768))
+    column_copy.wait()
+    give(8, 9)
+    need("ATT")
+    hidden_back = grad[...]
+    for i in range(3):
+        hidden_back += dot_plain(back[:, pl.ds(768 * i, 768)], rows_of(1 + i))
+    hidden_grad[...] = hidden_back.astype(LOW)
+    fill(0, 4)
+
     state_grad[...] = jnp.zeros_like(state_grad)
     total[...] = jnp.zeros_like(total)
-    early = TURNS_IN_LOOP
-    steps = [step for turn in turns[:early] for step in turn]
+    steps = [step for _ in range(TURNS_IN_LOOP) for step in next(turns)]
     share = -(-len(steps) // CHARS)
 
     def retreat(i, carry):
@@ -699,20 +1087,20 @@
         record_copy(t).wait()
         gru_backward_step(t, cell, record, state_grad, pool_grad, lengths)
         for k in range(CHARS):
-
-            @pl.when(i == k)
-            def _():
-                reduce.run(steps[k * share : (k + 1) * share])
+            if steps[k * share : (k + 1) * share]:
+
+                @pl.when(i == k)
+                def _():
+                    reduce.run(steps[k * share : (k + 1) * share])
 
         return carry
 
     lax.fori_loop(0, CHARS, retreat, 0)
     for way in (0, 1):
-        cell_gradient(way, record, cell_part)
-        copy = pltpu.make_async_copy(cell_part, grads["CELL"].at[pl.ds(2 * way, 2)], out_sem.at[0])
-        copy.start()
-        reduce.run(turns[early + way])
-        copy.wait()
+        outbox.settle_all()
+        cell_gradient(way, record, thick)
+        outbox.send(THIN, thick.at[:, :, :, 0:144], grads["CELL"].at[pl.ds(2 * way, 2)])
+        go_on()
 
     def look_up(c, carry):
         table_gradient(c, cell, record, codes, total)
@@ -720,43 +1108,61 @@
 
     lax.fori_loop(0, CHARS, look_up, 0)
     table_part[...] = jnp.transpose(total[...]).astype(LOW).reshape((4, 2, 2) + BLOCKS["TABLE"])
-    copy = pltpu.make_async_copy(table_part, grads["TABLE"], out_sem.at[0])
-    copy.start()
-    copy.wait()
-    reduce.run([("give", p) for p in range(DENSE_PARTS, len(PARTS))])
-    for turn in turns[early + 2 :]:
+    outbox.send(0, table_part, grads["TABLE"])
+    give(10, 11)
+    for turn in turns:
         reduce.run(turn)
     reduce.run([("finish", p) for p in range(len(PARTS))])
 
 
-TURNS_IN_LOOP = 7
-
-
-def reduce_and_return(grads, record, cell, codes, lengths, pool_grad, per_place):
-    dense_kinds = [kind for kind in KINDS if kind not in ("CELL", "TABLE")]
+TURNS_IN_LOOP = 3
+
+
+def reduce_and_return(whole, saved, record, codes, lengths, hidden, cotangent, valid_keys, per_place):
     in_vmem = pl.BlockSpec(memory_space=pltpu.VMEM)
     anywhere = pl.BlockSpec(memory_space=pl.ANY)
     count = len(PARTS)
     shapes = [jax.ShapeDtypeStruct((2,) + BLOCKS[kind], LOW) for kind in KINDS]
-    shapes += [jax.ShapeDtypeStruct((count, 4, 2, 2, ROWS, LANES), LOW)]
-    shapes += [jax.ShapeDtypeStruct((4, 2, 2) + BLOCKS[kind], LOW) for kind in ("CELL", "TABLE")]
+    shapes += [
+        jax.ShapeDtypeStruct((TOKENS, 768), LOW),
+        jax.ShapeDtypeStruct((count, 4, 2, 2, ROWS, LANES), LOW),
+    ]
+    shapes += [jax.ShapeDtypeStruct((4, 2, 2) + BLOCKS[kind], LOW) for kind in KINDS]
+    views = {
+        "ATT": (3, 6, 128, 768),
+        "OUT": (6, 128, 1024),
+        "IN": (4, 6, 128, 768),
+        "FEED": (6, 128, 3072),
+        "STREAM": (6, 128, 1536),
+        "MERGE": (6, 128, 4608),
+    }
     results = pl.pallas_call(
         partial(backward_kernel, per_place),
         out_shape=shapes,
-        in_specs=[anywhere] * 7 + [in_vmem] * 4,
-        out_specs=[anywhere] * len(shapes),
+        in_specs=[anywhere] * 7 + [in_vmem] * 5 + [pl.BlockSpec(memory_space=pltpu.SMEM)] + [in_vmem] * len(SAVED),
+        out_specs=[anywhere] * 8 + [in_vmem] + [anywhere] * 9,
         scratch_shapes=[
             pltpu.VMEM((CHARS, TOKENS, 2 * RECORD), LOW),
             pltpu.VMEM((TOKENS, 2 * HID), WIDE),
+            pltpu.VMEM((TOKENS, 2 * HID), WIDE),
             pltpu.VMEM((1024, EMB), WIDE),
-            pltpu.VMEM((2, 2, 2) + BLOCKS["CELL"], LOW),
+            pltpu.VMEM((128, 768), WIDE),
+            pltpu.VMEM((TOKENS, 768), WIDE),
+            pltpu.VMEM((TOKENS, 3072), LOW),
+            pltpu.VMEM((TOKENS, 2304), LOW),
+            pltpu.VMEM((THIN, 4, 2, 2, 48, 768), LOW),
+            pltpu.VMEM((2, 2, 2, 192, 768), LOW),
             pltpu.VMEM((4, 2, 2) + BLOCKS["TABLE"], LOW),
+            pltpu.VMEM((4, 2, 2, 48, 256), LOW),
+            pltpu.VMEM((8, 512), WIDE),
             pltpu.VMEM((SLOTS, 4, 2, 2, ROWS, LANES), LOW),
             pltpu.VMEM((2, 4, 2, 2, ROWS, LANES), LOW),
             pltpu.VMEM((SLOTS, 4, 2, ROWS, LANES), LOW),
             pltpu.VMEM((SLOTS, 8, ROWS, LANES), LOW),
             pltpu.VMEM((SLOTS, 2, ROWS, LANES), LOW),
             pltpu.SemaphoreType.DMA((CHARS,)),
+            pltpu.SemaphoreType.DMA((6, 6)),
+            pltpu.SemaphoreType.DMA((THIN + 1,)),
             pltpu.SemaphoreType.DMA((1,)),
             pltpu.SemaphoreType.DMA((count, MOVES)),
             pltpu.SemaphoreType.DMA((count, MOVES)),
@@ -764,121 +1170,19 @@
             pltpu.SemaphoreType.DMA((count, SUBS)),
             pltpu.SemaphoreType.REGULAR((5,)),
         ],
-        compiler_params=pltpu.CompilerParams(collective_id=1, has_side_effects=True, vmem_limit_bytes=60 << 20),
-    )(*[grads[kind] for kind in dense_kinds], record, cell, codes, lengths, pool_grad)
-    return dict(zip(KINDS, results[:8]))
-
-
-def layer_norm(inputs, gain_row, shift_row):
-    centred = inputs - jnp.mean(inputs, axis=-1, keepdims=True)
-    spread = jnp.mean(centred * centred, axis=-1, keepdims=True)
-    return centred * lax.rsqrt(spread + norm_eps) * gain_row + shift_row
-
-
-def gelu_exact(inputs):
-    return jax.nn.gelu(inputs, approximate=False)
-
-
-def dense(whole, hidden, sequence_length, cotangent, pooled):
-    w = {kind: part.reshape(-1, part.shape[-1]) for kind, part in whole.items()}
-    small = w["OUT"][:, 768:785]
-    small_rows = jnp.transpose(small[:, :13]).astype(WIDE)
-    biases, gains = small_rows[:10], small_rows[10:]
-    feed_bias = small[:, 13:].reshape(-1).astype(WIDE)
-    length, width = hidden.shape
-    head = width // HEADS
-    scale = head ** (-0.5)
-    joint_bias = jnp.concatenate([biases[0], jnp.zeros_like(biases[0]), biases[1]])
-    projected = (dot_second(hidden, w["ATT"]) + joint_bias).astype(LOW)
-    projected = projected.reshape(length, 3, HEADS, head)
-    queries, keys, values = projected[:, 0], projected[:, 1], projected[:, 2]
-    mask = jnp.where(jnp.arange(length) < sequence_length[0], 0.0, masked_score).astype(WIDE)
-    scores = jnp.einsum("qhd,khd->hqk", queries, keys, preferred_element_type=WIDE) * scale + mask
-    weight = jnp.exp(scores - jnp.max(scores, axis=-1, keepdims=True))
-    soft = weight / jnp.sum(weight, axis=-1, keepdims=True)
-    soft_low = soft.astype(LOW)
-    context = jnp.einsum("hqk,khd->qhd", soft_low, values, preferred_element_type=WIDE)
-    context = context.astype(LOW).reshape(length, width)
-    one_sum = hidden.astype(WIDE) + dot_second(context, w["OUT"][:, :768]) + biases[2]
-    first = layer_norm(one_sum, gains[0], biases[3])
-    first_low = first.astype(LOW)
-    inner = dot_second(first_low, w["IN"]) + feed_bias
-    active = gelu_exact(inner).astype(LOW)
-    two_sum = first + dot_second(active, w["FEED"]) + biases[4]
-    second = layer_norm(two_sum, gains[1], biases[5])
-    second_low = second.astype(LOW)
-    pooled_low = pooled.astype(LOW)
-    token_side = dot_second(second_low, w["STREAM"][:, :768]) + biases[6]
-    char_side = dot_second(pooled_low, w["STREAM"][:, 768:]) + biases[7]
-    joined = jnp.concatenate([token_side, char_side], axis=-1).astype(LOW)
-    padded = jnp.pad(joined, ((1, 1), (0, 0)))
-    windows = jnp.concatenate([padded[:-2], padded[1:-1], padded[2:]], axis=-1)
-    third_sum = second + dot_second(windows, w["MERGE"]) + biases[8]
-    output = layer_norm(third_sum, gains[2], biases[9]).astype(LOW)
-
-    _, pull_three = jax.vjp(layer_norm, third_sum, gains[2], biases[9])
-    merged_grad, gain_three, shift_three = pull_three(cotangent.astype(WIDE))
-    merged_low = merged_grad.astype(LOW)
-    grads = {"MERGE": dot_first(merged_low, windows)}
-    window_grad = dot_plain(merged_low, w["MERGE"]).reshape(length, 3, 2 * width)
-    joined_grad = (
-        window_grad[:, 1]
-        + jnp.pad(window_grad[1:, 0], ((0, 1), (0, 0)))
-        + jnp.pad(window_grad[:-1, 2], ((1, 0), (0, 0)))
+        compiler_params=pltpu.CompilerParams(collective_id=1, has_side_effects=True, vmem_limit_bytes=63 << 20),
+    )(
+        *[whole[kind].reshape(views[kind]) for kind in DENSE_KINDS],
+        record,
+        whole["CELL"],
+        codes,
+        lengths,
+        hidden,
+        cotangent,
+        valid_keys,
+        *[saved[name] for name in SAVED],
     )
-    token_grad, char_grad = joined_grad[:, :width], joined_grad[:, width:]
-    token_low, char_low = token_grad.astype(LOW), char_grad.astype(LOW)
-    grads["STREAM"] = jnp.concatenate([dot_first(token_low, second_low), dot_first(char_low, pooled_low)], axis=1)
-    pooled_grad = dot_plain(char_low, w["STREAM"][:, 768:])
-    second_grad = merged_grad + dot_plain(token_low, w["STREAM"][:, :768])
-    _, pull_two = jax.vjp(layer_norm, two_sum, gains[1], biases[5])
-    two_grad, gain_two, shift_two = pull_two(second_grad)
-    two_low = two_grad.astype(LOW)
-    grads["FEED"] = dot_first(two_low, active)
-    _, pull_gelu = jax.vjp(gelu_exact, inner)
-    (inner_grad,) = pull_gelu(dot_plain(two_low, w["FEED"]))
-    inner_low = inner_grad.astype(LOW)
-    grads["IN"] = dot_first(inner_low, first_low)
-    first_grad = two_grad + dot_plain(inner_low, w["IN"])
-    _, pull_one = jax.vjp(layer_norm, one_sum, gains[0], biases[3])
-    one_grad, gain_one, shift_one = pull_one(first_grad)
-    one_low = one_grad.astype(LOW)
-    grad_out = dot_first(one_low, context)
-    context_grad = dot_plain(one_low, w["OUT"][:, :768]).astype(LOW).reshape(length, HEADS, head)
-    soft_grad = jnp.einsum("qhd,khd->hqk", context_grad, values, preferred_element_type=WIDE)
-    value_grad = jnp.einsum("hqk,qhd->khd", soft_low, context_grad, preferred_element_type=WIDE)
-    score_grad = soft * (soft_grad - jnp.sum(soft * soft_grad, axis=-1, keepdims=True))
-    score_low = score_grad.astype(LOW)
-    query_grad = jnp.einsum("hqk,khd->qhd", score_low, keys, preferred_element_type=WIDE) * scale
-    key_grad = jnp.einsum("hqk,qhd->khd", score_low, queries, preferred_element_type=WIDE) * scale
-    projected_low = jnp.stack([query_grad, key_grad, value_grad], axis=1).reshape(length, 3 * width).astype(LOW)
-    grads["ATT"] = dot_first(projected_low, hidden)
-    hidden_grad = (one_grad + dot_plain(projected_low, w["ATT"])).astype(LOW)
-    small_grads = jnp.stack(
-        [
-            jnp.sum(query_grad, axis=0).reshape(width),
-            jnp.sum(value_grad, axis=0).reshape(width),
-            jnp.sum(one_grad, axis=0),
-            shift_one,
-            jnp.sum(two_grad, axis=0),
-            shift_two,
-            jnp.sum(token_grad, axis=0),
-            jnp.sum(char_grad, axis=0),
-            jnp.sum(merged_grad, axis=0),
-            shift_three,
-            gain_one,
-            gain_two,
-            gain_three,
-        ]
-    )
-    feed_bias_grad = jnp.sum(inner_grad, axis=0).reshape(width, 4)
-    grads["OUT"] = jnp.pad(
-        jnp.concatenate([grad_out, jnp.transpose(small_grads), feed_bias_grad], axis=1), ((0, 0), (0, 256 - 17))
-    )
-    grads = {
-        kind: part.astype(LOW).reshape((4, 2, 2) + BLOCKS[kind]) for kind, part in grads.items()
-    }
-    return output, hidden_grad, pooled_grad, grads
+    return dict(zip(KINDS, results[:8])), results[8]
 
 
 def unpack(final):
@@ -906,13 +1210,13 @@
     wide = lax.axis_size("wide")
     per_place = wide // 2
     own = pack(parameters, per_place)
-    codes = jnp.transpose(char_codes)[:, :, None]
+    codes = jnp.transpose(char_codes)
     lengths = word_length[:, None]
-    whole, record, pooled = gather_and_read(own, codes, lengths, per_place)
-    output, hidden_grad, pooled_grad, grads = dense(whole, hidden, sequence_length, cotangent, pooled)
-    pool_grad = pooled_grad / lengths.astype(WIDE)
-    rows = jnp.transpose(char_codes)
-    final = reduce_and_return(grads, record, whole["CELL"], rows, lengths, pool_grad, per_place)
+    whole, record, saved = gather_and_read(own, codes, lengths, hidden, sequence_length, per_place)
+    final, hidden_grad = reduce_and_return(
+        whole, saved, record, codes, lengths, hidden, cotangent, sequence_length, per_place
+    )
+    output = saved["output"]
     return (output, hidden_grad, *unpack(final))
 
 

time: 456 us -> 380 us (0.83)
  matrix products: 59.9 us -> 0 us
  local copies, waits for them, and re-layouts: 39.5 us -> 17.8 us
  Pallas kernels: 321 us -> 338 us
  other arithmetic: 25.7 us -> 14.3 us
    dot_general x26 -> x0, matrix products: 58.6 us -> none  [the longest x7 20.1 us: dot_first(): lax.dot_general(left_side, right_side, (((0,), (0,)), ((), ())), preferre...]
    dot_general x1 -> x0, local copies, waits for them, and re-layouts: 10.3 us -> none  [dot_plain(): return jnp.dot(left_side, right_side, preferred_element_type=WIDE)]
    pallas_call x1, Pallas kernels: 163 us -> 173 us  [reduce_and_return(): pl.pallas_call(partial(backward_kernel, per_place), out_shape=shapes, in_...]
    pallas_call x1, Pallas kernels: 158 us -> 165 us  [gather_and_read(): pl.pallas_call(partial(forward_kernel, per_place), out_shape=[jax.ShapeDt...]
    reduce_sum x12 -> x0, other arithmetic: 6.1 us -> none  [the longest x3 2.01 us: layer_norm(): centred = inputs - jnp.mean(inputs, axis=-1, keepdims=True)]
    unnamed x159 -> x41, local copies, waits for them, and re-layouts: 13.8 us -> 9.99 us
where the time goes in v3:
time: 380 us; the launch traced here: 373 us
  Pallas kernels  338 us (89%)
  local copies, waits for them, and re-layouts  17.8 us (5%)
  other arithmetic  14.3 us (4%)
    pallas_call x1, Pallas kernels, reduce_and_return(): pl.pallas_call(partial(backward_kernel, per_place), out_shape=shapes, in_...  173 us
    pallas_call x1, Pallas kernels, gather_and_read(): pl.pallas_call(partial(forward_kernel, per_place), out_shape=[jax.ShapeDt...  165 us
    unnamed x41, local copies, waits for them, and re-layouts  9.99 us
  transfers between devices with their start and end apart: 4, of which 0 were waited for; matrix products, arithmetic and copies ran while one was open for 4% of the time, Pallas kernels for 0%

profile of v3, /device:TPU:0, one launch (start us, length us, event | category | flops | bytes accessed | tf_op | source)
XLA Modules:
  0.0 373.4 jit_solution(3748383107605328209)
XLA Ops:
  0.7 0.8 pad.13
  1.5 0.5 collective-permute-start.1
  2.0 0.8 copy.42
  2.8 0.8 fusion.5
  3.6 0.9 pad_maximum_fusion.6
  4.5 0.5 collective-permute-start
  5.0 0.7 reshape.78
  5.8 0.8 copy.44
  6.6 0.8 copy.43
  7.3 0.8 fusion.13
  8.2 0.9 bitcast_dynamic-update-slice_fusion
  9.1 0.8 bitcast_dynamic-update-slice_fusion.5
  9.9 0.8 bitcast_dynamic-update-slice_fusion.4
  10.7 0.9 bitcast_dynamic-update-slice_fusion.3
  11.5 0.9 bitcast_dynamic-update-slice_fusion.2
  12.4 0.9 bitcast_dynamic-update-slice_fusion.1
  14.0 0.7 copy.45.refs_9_
  14.8 0.6 pad_maximum_fusion.9.refs_1_
  15.5 0.7 pad_maximum_fusion.4.refs_4_
  16.2 0.1 broadcast_select_fusion.2
  16.3 0.8 pad_maximum_fusion.5
  17.1 0.6 pad_maximum_fusion.8.refs_3_
  17.8 0.7 pad_maximum_fusion.7.refs_6_
  18.5 0.7 pad_maximum_fusion.3.refs_5_
  19.2 0.8 pad_maximum_fusion.2.refs_7_
  20.0 165.2 %shard_map.289 = (bf16[4,2,2,144,768]{4,3,2,1,0:T(8,128)(2,1)}, bf16[4,2,2,16,1024]{4,3,2,1,0:T(8,128)(2,1)}, bf16[4,2,2,144,768]{4,3,2,1,0:T(8,128)(2,1)}, bf16...) custom-call(bf16[144,768]{1,0:T(8,128)(2,1)} %get-tuple-element.77.r, ...), custom_call_target="tpu_custom_call" | custom-call | tf_op jit(solution)/shard_map/pallas_call | solution.py:458
  185.2 173.0 %shard_map.290 = (bf16[2,144,768]{2,1,0:T(8,128)(2,1)}, bf16[2,16,1024]{2,1,0:T(8,128)(2,1)}, bf16[2,144,768]{2,1,0:T(8,128)(2,1)}, bf16[2,48,1024]{2,1,0:T(8,12...) custom-call(bf16[3,6,128,768]{3,2,1,0:T(8,128)(2,1)} %bitcast.102, ...), custom_call_target="tpu_custom_call" | custom-call | tf_op jit(solution)/shard_map/pallas_call | solution.py:1139
  358.3 1.0 bitcast_convert_fusion.4
  359.3 0.1 slice.94
  359.4 0.1 slice.84
  359.5 0.7 slice_bitcast_fusion.7
  360.2 1.1 convert_bitcast_fusion.1
  361.3 0.7 slice_bitcast_fusion.6
  362.1 0.8 slice_bitcast_fusion.3
  362.9 0.7 convert_bitcast_fusion.2
  363.5 0.7 copy.52
  364.2 0.7 copy.53
  364.9 0.7 reshape.85
  365.7 0.1 bitcast_convert_fusion.1
  365.8 1.4 copy.47
  367.2 1.2 convert_bitcast_fusion
  368.4 0.2 bitcast_convert_fusion
  368.6 0.1 slice_bitcast_fusion.2
  368.7 0.7 copy.51
  369.4 0.9 pad_maximum_fusion.1
  370.2 1.3 pad_maximum_fusion
  371.6 0.7 copy.63
  372.3 0.7 copy.64
  (42 shorter events, 0.4 us)
Async XLA Ops:
  0.6 14.1 %copy-start.12 = (bf16[1000,8]{0,1:T(8,128)(2,1)S(1)}, bf16[1000,8]{0,1:T(8,128)(2,1)}, u32[]{:S(2)}) copy-start(bf16[1000,8]{0,1:T(8,128)(2,1)} %param.28) | copy-start | bytes 48004
  0.7 14.8 %copy-start.10 = (bf16[768,96]{0,1:T(8,128)(2,1)S(1)}, bf16[768,96]{0,1:T(8,128)(2,1)}, u32[]{:S(2)}) copy-start(bf16[768,96]{0,1:T(8,128)(2,1)} %param.25) | copy-start | bytes 442372
  0.7 15.5 %copy-start.4 = (bf16[768,72]{0,1:T(8,128)(2,1)S(1)}, bf16[768,72]{0,1:T(8,128)(2,1)}, u32[]{:S(2)}) copy-start(bf16[768,72]{0,1:T(8,128)(2,1)} %param.23) | copy-start | bytes 331780
  0.7 13.4 %copy-start.13 = (s32[128]{0:T(128)S(1)}, s32[128]{0:T(128)}, u32[]{:S(2)}) copy-start(s32[128]{0:T(128)} %param.20) | copy-start | bytes 1540
  1.5 13.3 %collective-permute-start.1 = (bf16[8,1024]{1,0:T(8,128)(2,1)S(1)}, bf16[8,1024]{1,0:T(8,128)(2,1)S(1)}, u32[]{:S(2)}, u32[]{:S(2)}) collective-permute-start(bf16[8,1024]{1,0:T(8,128)(2,1)S(1)} %pad.13), channel_id=1, source_target_pairs={{0,1},{1,0},{2,3},{3,2},{4,5},{5,4},{6,7},{7,6},{8,9},{9,8},{10,11... | collective-permute-start | bytes 49160 | tf_op jit(solution)/shard_map/ppermute | solution.py:518
  1.9 13.5 %collective-permute-start.3 = (bf16[96,768]{1,0:T(8,128)(2,1)}, bf16[96,768]{1,0:T(8,128)(2,1)S(1)}, u32[]{:S(2)}, u32[]{:S(2)}) collective-permute-start(bf16[96,768]{1,0:T(8,128)(2,1)} %bitcast.108), channel_id=1, source_target_pairs={{0,1},{1,0},{2,3},{3,2},{4,5},{5,4},{6,7},{7,6},{8,9},{9,8},{10,11... | collective-permute-start | bytes 442376 | tf_op jit(solution)/shard_map/ppermute | solution.py:518
  4.5 11.7 %collective-permute-start = (bf16[72,1536]{1,0:T(8,128)(2,1)S(1)}, bf16[72,1536]{1,0:T(8,128)(2,1)S(1)}, u32[]{:S(2)}, u32[]{:S(2)}) collective-permute-start(bf16[72,1536]{1,0:T(8,128)(2,1)S(1)} %pad_maximum_fusion.6), channel_id=1, source_target_pairs={{0,1},{1,0},{2,3},{3,2},{4,5},{5,4},{6,7},{7,6},{8,9},{9,8},{10,11... | collective-permute-start | bytes 663560 | tf_op jit(solution)/shard_map/ppermute | solution.py:518
  13.3 3.8 %collective-permute-start.2 = (bf16[24,10240]{1,0:T(8,128)(2,1)S(1)}, bf16[24,10240]{1,0:T(8,128)(2,1)S(1)}, u32[]{:S(2)}, u32[]{:S(2)}) collective-permute-start(bf16[24,10240]{1,0:T(8,128)(2,1)S(1)} %bitcast_dynamic-update-slice_fusion.1), channel_id=1, source_target_pairs={{0,1},{1,0},{2,3},{3,2},{4,5},{5,4},{6,7},{7,6},{8,9},{9,8},{10,11... | collective-permute-start | bytes 1474568 | tf_op jit(solution)/shard_map/ppermute | solution.py:518
  358.2 2.0 copy-start.5
  358.3 2.0 copy-start.6
  359.3 2.0 copy-start
  360.2 2.7 copy-start.11
  360.2 5.3 %copy-start.7 = (bf16[2,48,1536]{2,1,0:T(8,128)(2,1)S(1)}, bf16[2,48,1536]{2,1,0:T(8,128)(2,1)}, u32[]{:S(2)}) copy-start(bf16[2,48,1536]{2,1,0:T(8,128)(2,1)} %get-tuple-element.67) | copy-start | bytes 884740
  361.3 2.9 slice-start
  362.1 3.6 copy-start.3
  365.7 1.5 copy-start.2
  365.8 2.6 copy-start.1
  370.2 1.3 copy-start.8
  370.2 2.0 copy-start.9
